TPU v7x, 32 devices: a whole 2x2x4 slice. The times are simulated.
32 devices in a mesh: groups: 2 (over y), ep: 8 (over z, x), dp: 2 (over core).
Axes of the slice: x: 2, y: 2, z: 4, core: 2. Of those that a mesh axis runs over, the one named last changes fastest.
Arguments:
- tokens: bfloat16 [2048, 2048], P(('groups', 'ep'), 'dp'), parts along dimension 0, may hold values from -6 to 6
- out_grad: bfloat16 [2048, 2048], P(('groups', 'ep'), 'dp'), parts along dimension 0, may hold values from -6 to 6
- route_gates: bfloat16 [2048, 8], P(('groups', 'ep', 'dp')), parts along dimension 0, may hold values from 0.099609375 to 1
- expert_ids: int32 [2048, 8], P(('groups', 'ep', 'dp')), parts along dimension 0, may hold values from 0 to 127, all different within a row; in each aligned block of 64 rows (0 to 63, 64 to 127, ...) at most 6 rows name the same one
- w_gate: bfloat16 [128, 2048, 384], P('ep', 'dp'), may hold values from -0.125 to 0.125
- w_up: bfloat16 [128, 2048, 384], P('ep', 'dp'), may hold values from -0.125 to 0.125
- w_down: bfloat16 [128, 384, 2048], P('ep', None, 'dp'), may hold values from -0.3125 to 0.3125
Outputs:
- grad_input: bfloat16 [2048, 2048], P(('groups', 'ep'), 'dp'), parts along dimension 0
- grad_gate_w: bfloat16 [256, 2048, 384], P(('groups', 'ep'), 'dp'), parts along dimension 0
- grad_up_w: bfloat16 [256, 2048, 384], P(('groups', 'ep'), 'dp'), parts along dimension 0
There are 2 independent parts, one for each index of `groups`. A program takes and returns all parts, laid end to end along the dimension named above; an argument that names none is the same for every part. Nothing has to cross between parts.
Inputs may be any that keep to these rules, and one draw needn't show every extreme that they name: `expert_ids`: each token names 8 different experts. In each aligned block of 64 tokens (the routing rows of one device) no expert is named by more than 6 tokens, and in every draw some block has an expert named by exactly 6.
All inputs are finite; a program needn't handle non-finite values.
Results may differ from a plain program's by a relative error of at most 0.0058.
Values may be sent and summed in bfloat16 or wider, within the bound.
No kernel may reach another device: no remote copies, remote signals or barrier semaphores. Data moves between devices by JAX's collectives and lax.ppermute only.
A program may use at most 320 MiB of HBM per device.

v0:
```python
import jax
import jax.numpy as jnp
from jax import lax
from jax.sharding import PartitionSpec as P

CAP = 6


def route_slots(expert_ids, experts, stride, offset):
    flattened = expert_ids.reshape(-1)
    onehot = (flattened[:, None] == jnp.arange(experts, dtype=jnp.int32)[None, :]).astype(jnp.int32)
    ranking = jnp.sum(onehot * (jnp.cumsum(onehot, axis=0) - 1), axis=1)
    return flattened * stride + offset + ranking


def fill_slots(values, slot_ids, slot_count):
    zeroed = jnp.zeros((slot_count,) + values.shape[1:], values.dtype)
    return zeroed.at[slot_ids].set(values)


def swiglu_back(pre_gate, pre_up, raw_down, gate_rows):
    grad_hidden = gate_rows.astype(jnp.float32)[..., None] * raw_down
    sigmoid = jax.nn.sigmoid(pre_gate)
    grad_gate_pre = (grad_hidden * pre_up * sigmoid * (1.0 + pre_gate * (1.0 - sigmoid))).astype(
        jnp.bfloat16
    )
    grad_up_pre = (grad_hidden * pre_gate * sigmoid).astype(jnp.bfloat16)
    return (grad_gate_pre, grad_up_pre)


def share_pre_grads(grad_gate_pre, grad_up_pre):
    return (
        lax.all_gather(grad_gate_pre, "dp", axis=2, tiled=True),
        lax.all_gather(grad_up_pre, "dp", axis=2, tiled=True),
    )


def weight_terms(shaped_rows, both_gate, both_up):
    grad_gate_w = jnp.einsum(
        "nlbcd,nlbcf->ldf", shaped_rows, both_gate, preferred_element_type=jnp.float32
    )
    grad_up_w = jnp.einsum(
        "nlbcd,nlbcf->ldf", shaped_rows, both_up, preferred_element_type=jnp.float32
    )
    return (grad_gate_w.astype(jnp.bfloat16), grad_up_w.astype(jnp.bfloat16))


def expert_work(token_rows, grad_rows, gate_rows, w_gate, w_up, w_down):
    full_gate, full_up, full_down = (
        lax.all_gather(w_gate, "dp", axis=1, tiled=True),
        lax.all_gather(w_up, "dp", axis=1, tiled=True),
        lax.all_gather(w_down, "dp", axis=2, tiled=True),
    )
    pre_gate = jnp.einsum(
        "nlcd,ldf->nlcf", token_rows, full_gate, preferred_element_type=jnp.float32
    )
    pre_up = jnp.einsum("nlcd,ldf->nlcf", token_rows, full_up, preferred_element_type=jnp.float32)
    raw_down = jnp.einsum(
        "nlcd,lfd->nlcf", grad_rows, full_down, preferred_element_type=jnp.float32
    )
    grad_gate_pre, grad_up_pre = swiglu_back(pre_gate, pre_up, raw_down, gate_rows)
    row_grad = (
        jnp.einsum("nlcf,ldf->nlcd", grad_gate_pre, full_gate, preferred_element_type=jnp.float32)
        + jnp.einsum("nlcf,ldf->nlcd", grad_up_pre, full_up, preferred_element_type=jnp.float32)
    ).astype(jnp.bfloat16)
    return (row_grad, grad_gate_pre, grad_up_pre)


def body(tokens, out_grad, route_gates, expert_ids, w_gate, w_up, w_down):
    ep_count = lax.axis_size("ep")
    local_count = w_gate.shape[0]
    experts = local_count * ep_count
    block_rows, top_count = expert_ids.shape
    capacity = CAP
    half_width = tokens.shape[1]
    feature_width = 2 * half_width
    pair_ids = lax.all_gather(expert_ids, "dp", axis=0, tiled=True)
    first_slots = route_slots(pair_ids[:block_rows], experts, 2 * capacity, 0)
    second_slots = route_slots(pair_ids[block_rows:], experts, 2 * capacity, capacity)
    slot_ids = jnp.concatenate([first_slots, second_slots])
    own_slots = lax.dynamic_index_in_dim(
        slot_ids.reshape(2, block_rows * top_count), lax.axis_index("dp"), 0, keepdims=False
    )
    token_of = jnp.arange(2 * block_rows * top_count, dtype=jnp.int32) // top_count
    slot_count = experts * 2 * capacity
    send_rows = fill_slots(tokens[token_of], slot_ids, slot_count).reshape(
        ep_count, local_count * 2 * capacity, half_width
    )
    send_grads = fill_slots(out_grad[token_of], slot_ids, slot_count).reshape(
        ep_count, local_count * 2 * capacity, half_width
    )
    send_gates = fill_slots(route_gates.reshape(-1), own_slots, slot_count).reshape(
        ep_count, local_count * 2 * capacity
    )
    recv_rows, recv_grads, recv_gates = (
        lax.all_to_all(send_rows, "ep", split_axis=0, concat_axis=0, tiled=True),
        lax.all_to_all(send_grads, "ep", split_axis=0, concat_axis=0, tiled=True),
        lax.all_to_all(send_gates, "ep", split_axis=0, concat_axis=0, tiled=True),
    )
    shaped_rows = recv_rows.reshape(ep_count, local_count, 2, capacity, half_width)
    shaped_grads = recv_grads.reshape(ep_count, local_count, 2, capacity, half_width)
    shaped_gates = recv_gates.reshape(ep_count, local_count, 2, capacity)
    joined_rows, joined_grads = (
        lax.all_to_all(shaped_rows, "dp", split_axis=2, concat_axis=4, tiled=True),
        lax.all_to_all(shaped_grads, "dp", split_axis=2, concat_axis=4, tiled=True),
    )
    token_rows = joined_rows.reshape(ep_count, local_count, capacity, feature_width)
    grad_rows = joined_grads.reshape(ep_count, local_count, capacity, feature_width)
    gate_rows = lax.dynamic_index_in_dim(shaped_gates, lax.axis_index("dp"), 2, keepdims=False)
    row_grad, grad_gate_pre, grad_up_pre = expert_work(
        token_rows, grad_rows, gate_rows, w_gate, w_up, w_down
    )
    both_gate, both_up = share_pre_grads(
        grad_gate_pre.reshape(ep_count, local_count, 1, capacity, -1),
        grad_up_pre.reshape(ep_count, local_count, 1, capacity, -1),
    )
    spread = lax.all_to_all(
        row_grad.reshape(ep_count, local_count, 1, capacity, feature_width),
        "dp",
        split_axis=4,
        concat_axis=2,
        tiled=True,
    )
    grad_gate_w, grad_up_w = weight_terms(shaped_rows, both_gate, both_up)
    returned = lax.all_to_all(
        spread.reshape(ep_count, local_count * 2 * capacity, half_width),
        "ep",
        split_axis=0,
        concat_axis=0,
        tiled=True,
    )
    returned = returned.reshape(slot_count, half_width)
    per_route = (
        returned[slot_ids].astype(jnp.float32).reshape(2 * block_rows, top_count, half_width)
    )
    grad_input = jnp.sum(per_route, axis=1).astype(jnp.bfloat16)
    return (grad_input, grad_gate_w, grad_up_w)


def solution(mesh):
    in_specs = (
        P(("groups", "ep"), "dp"),
        P(("groups", "ep"), "dp"),
        P(("groups", "ep", "dp"), None),
        P(("groups", "ep", "dp"), None),
        P("ep", "dp", None),
        P("ep", "dp", None),
        P("ep", None, "dp"),
    )
    out_specs = (
        P(("groups", "ep"), "dp"),
        P(("groups", "ep"), "dp", None),
        P(("groups", "ep"), "dp", None),
    )
    return jax.shard_map(body, mesh=mesh, in_specs=in_specs, out_specs=out_specs, check_vma=False)
```

profile of v0, /device:TPU:12, one launch (start us, length us, event | category | flops | bytes accessed | tf_op | source)
XLA Modules:
  0.0 524.2 jit_solution(4730677631511413808)
XLA Ops:
  13.2 15.2 %scatter_custom_fusion.2 = bf16[1536,1024]{1,0:T(8,128)(2,1)} fusion(s32[1024]{0:T(1024)S(1)} %bitcast.139, bf16[128,1024]{1,0:T(8,128)(2,1)S(1)} %copy-done, s32[1024]{0:T(1024)S(1)} %broadcast_clamp_fusion.1, bf16[]{:T(256)} %constant.46.clone.1), kind=kCustom, calls=%fused_computation.21 | custom fusion | bytes 3145730 | tf_op jit(solution)/shard_map/scatter | solution.py:18
  28.4 6.7 %all-to-all-start.3 = ((bf16[8,192,1024]{2,1,0:T(8,128)(2,1)}), bf16[8,192,1024]{2,1,0:T(8,128)(2,1)S(1)}, u32[]{:S(2)}, u32[]{:S(2)}) async-start(bf16[8,192,1024]{2,1,0:T(8,128)(2,1)} %bitcast.131), calls=%async_computation.3 | async-start | bytes 6291456 | tf_op jit(solution)/shard_map/all_to_all | solution.py:96
  39.9 63.8 %all-to-all-done.3 = bf16[8,192,1024]{2,1,0:T(8,128)(2,1)S(1)} async-done(((bf16[8,192,1024]{2,1,0:T(8,128)(2,1)}), bf16[8,192,1024]{2,1,0:T(8,128)(2,1)S(1)}, u32[]{:S(2)}, u32[]{:S(2)}) %all-to-all-start.3) | async-done | bytes 3145760 | tf_op jit(solution)/shard_map/all_to_all | solution.py:96
  103.7 6.1 %all-to-all-start = ((bf16[8,1,192]{2,1,0:T(2,128)(2,1)}), bf16[8,1,192]{2,1,0:T(2,128)(2,1)S(1)}, u32[]{:S(2)}, u32[]{:S(2)}) async-start(bf16[8,1,192]{2,1,0:T(2,128)(2,1)} %all_to_all.62), calls=%async_computation | async-start | bytes 16384 | tf_op jit(solution)/shard_map/all_to_all | solution.py:98
  109.8 19.9 %scatter_custom_fusion.1 = bf16[1536,1024]{1,0:T(8,128)(2,1)} fusion(s32[1024]{0:T(1024)S(1)} %bitcast.140, bf16[128,1024]{1,0:T(8,128)(2,1)} %param.8, s32[1024]{0:T(1024)S(1)} %broadcast_clamp_fusion.1, bf16[]{:T(256)} %constant.46.clone.1), kind=kCustom, calls=%fused_computation.23 | custom fusion | bytes 3146240 | tf_op jit(solution)/shard_map/scatter | solution.py:18
  133.5 9.5 %all_to_all.70 = bf16[8,16,2,6,1024]{4,0,3,1,2:T(8,128)(2,1)} all-to-all(bf16[8,16,2,6,1024]{4,0,3,1,2:T(8,128)(2,1)S(1)} %copy.126), channel_id=1, replica_groups=mesh['groups'=2,'ep'=8,'dp'=2] {'dp'}, dimensions={2} | all-to-all | bytes 6291456 | tf_op jit(solution)/shard_map/all_to_all | solution.py:104
  143.0 6.0 %all-to-all-start.1 = ((bf16[8,192,1024]{2,1,0:T(8,128)(2,1)}), bf16[8,192,1024]{2,1,0:T(8,128)(2,1)}, u32[]{:S(2)}, u32[]{:S(2)}) async-start(bf16[8,192,1024]{2,1,0:T(8,128)(2,1)} %bitcast.14), calls=%async_computation.1 | async-start | bytes 6291456 | tf_op jit(solution)/shard_map/all_to_all | solution.py:97
  152.4 65.2 %all-to-all-done.1 = bf16[8,192,1024]{2,1,0:T(8,128)(2,1)} async-done(((bf16[8,192,1024]{2,1,0:T(8,128)(2,1)}), bf16[8,192,1024]{2,1,0:T(8,128)(2,1)}, u32[]{:S(2)}, u32[]{:S(2)}) %all-to-all-start.1) | async-done | bytes 3145760 | tf_op jit(solution)/shard_map/all_to_all | solution.py:97
  221.6 14.8 %all_to_all.71 = bf16[8,16,2,6,1024]{4,0,3,1,2:T(8,128)(2,1)S(1)} all-to-all(bf16[8,16,2,6,1024]{4,0,3,1,2:T(8,128)(2,1)S(1)} %copy.123), channel_id=1, replica_groups=mesh['groups'=2,'ep'=8,'dp'=2] {'dp'}, dimensions={2} | all-to-all | bytes 6291456 | tf_op jit(solution)/shard_map/all_to_all | solution.py:105
  238.6 11.1 %fusion.27 = f32[8,16,6,384]{3,0,2,1:T(8,128)} fusion(bf16[8,16,6,2048]{3,0,2,1:T(8,128)(2,1)S(1)} %bitcast.124, bf16[16,2048,384]{2,1,0:T(8,128)(2,1)} %all-gather.13.cloned.1.call-done), kind=kOutput, calls=%fused_computation.29 | convolution fusion | flops 1207959552 | bytes 29491200 | tf_op jit(solution)/shard_map/nlcd,ldf->nlcf/dot_general | solution.py:54
  249.7 14.9 %multiply_convert_fusion = (bf16[8,16,6,384]{3,0,2,1:T(8,128)(2,1)}, f32[8,16,6,384]{3,0,2,1:T(8,128)}) fusion(f32[8,16,6,384]{3,0,2,1:T(8,128)} %fusion.27, bf16[8,16,6,2048]{3,0,2,1:T(8,128)(2,1)} %bitcast.126, bf16[16,384,2048]{2,1,0:T(8,128)(2,1)} %all-gather.9.cloned.1.call-done, f32[8,16,6]{0,2,1:T(8,128)S(1)} %copy.121), kind=kOutput, calls=%fused_computation.37 | convolution fusion | flops 1210023936 | bytes 31263744 | tf_op jit(solution)/shard_map/nlcd,lfd->nlcf/dot_general | solution.py:58
  264.6 12.1 %fusion.42 = bf16[8,16,6,384]{3,0,2,1:T(8,128)(2,1)} fusion(f32[8,16,6,384]{3,0,2,1:T(8,128)} %get-tuple-element.6, bf16[8,16,6,2048]{3,0,2,1:T(8,128)(2,1)S(1)} %bitcast.125, bf16[16,2048,384]{2,1,0:T(8,128)(2,1)} %all-gather.11.cloned.1.call-done, f32[8,16,6,384]{3,0,2,1:T(8,128)} %fusion.27), kind=kOutput, calls=%fused_computation.34 | convolution fusion | flops 1210908672 | bytes 31260672 | tf_op jit(solution)/shard_map/nlcd,ldf->nlcf/dot_general | solution.py:57
  276.7 14.4 %fusion = f32[16,8,6,2048]{3,1,2,0:T(8,128)} fusion(bf16[8,16,6,384]{3,0,2,1:T(8,128)(2,1)} %fusion.42, bf16[16,2048,384]{2,1,0:T(8,128)(2,1)} %all-gather.13.cloned.1.call-done), kind=kOutput, calls=%fused_computation.8 | convolution fusion | flops 1207959552 | bytes 32047104 | tf_op jit(solution)/shard_map/nlcf,ldf->nlcd/dot_general | solution.py:63
  291.1 14.0 %fusion.12 = bf16[8,16,1,6,2048]{4,0,3,1,2:T(8,128)(2,1)S(1)} fusion(f32[16,8,6,2048]{3,1,2,0:T(8,128)} %fusion, bf16[8,16,6,384]{3,0,2,1:T(8,128)(2,1)} %get-tuple-element.5, bf16[16,2048,384]{2,1,0:T(8,128)(2,1)} %all-gather.11.cloned.1.call-done), kind=kOutput, calls=%fused_computation.19 | convolution fusion | flops 1211105280 | bytes 35192832 | tf_op jit(solution)/shard_map/nlcf,ldf->nlcd/dot_general | solution.py:64
  305.2 25.1 %copy.128 = bf16[8,16,1,6,2048]{1,0,3,2,4:T(8,128)(2,1)} copy(bf16[8,16,1,6,2048]{4,0,3,1,2:T(8,128)(2,1)S(1)} %fusion.12) | data formatting | bytes 6291456 | tf_op jit(solution)/shard_map/reshape | solution.py:118
  330.2 35.7 %reshape.354 = bf16[2,2,393216]{2,1,0:T(2,128)(2,1)S(1)} reshape(bf16[2048,1,6,8,16]{4,3,2,1,0:T(8,128)(2,1)} %bitcast.122) | data formatting | bytes 6291456
  365.9 7.3 %all_to_all.72 = bf16[2,2,393216]{2,1,0:T(2,128)(2,1)} all-to-all(bf16[2,2,393216]{2,1,0:T(2,128)(2,1)S(1)} %reshape.354), channel_id=1, replica_groups=mesh['groups'=2,'ep'=8,'dp'=2] {'dp'}, dimensions={0} | all-to-all | bytes 6291456 | tf_op jit(solution)/shard_map/all_to_all | solution.py:117
  373.2 28.7 %reshape.355 = bf16[2048,1,6,8,16]{4,3,2,1,0:T(8,128)(2,1)} reshape(bf16[2,2,393216]{2,1,0:T(2,128)(2,1)} %all_to_all.72) | data formatting | bytes 6291456
  401.9 26.0 %copy.141 = bf16[8,16,1,6,2,1024]{5,4,1,3,0,2:T(2,128)(2,1)S(1)} copy(bf16[8,16,1,6,2,1024]{1,0,3,5,4,2:T(8,128)(2,1)} %bitcast.123) | data formatting | bytes 6291456 | tf_op jit(solution)/shard_map/all_to_all | solution.py:117
  433.0 6.5 %all-to-all-start.6 = ((bf16[8,192,1024]{2,1,0:T(8,128)(2,1)}), bf16[8,192,1024]{2,1,0:T(8,128)(2,1)S(1)}, u32[]{:S(2)}, u32[]{:S(2)}) async-start(bf16[8,192,1024]{2,1,0:T(8,128)(2,1)} %copy.131), calls=%async_computation.6 | async-start | bytes 6291456 | tf_op jit(solution)/shard_map/all_to_all | solution.py:125
  440.1 10.5 %bitcast_convert_fusion.1 = bf16[16,1024,384]{2,1,0:T(8,128)(2,1)} fusion(bf16[8,16,2,6,384]{4,0,3,2,1:T(8,128)(2,1)} %bitcast.145, bf16[8,16,2,6,1024]{4,0,3,2,1:T(8,128)(2,1)} %bitcast.129), kind=kOutput, calls=%fused_computation.7 | convolution fusion | flops 1214251008 | bytes 16908288 | tf_op jit(solution)/shard_map/nlbcd,nlbcf->ldf/dot_general | solution.py:39
  452.0 10.5 %bitcast_convert_fusion = bf16[16,1024,384]{2,1,0:T(8,128)(2,1)} fusion(bf16[8,16,2,6,384]{4,0,3,2,1:T(8,128)(2,1)} %bitcast.146, bf16[8,16,2,6,1024]{4,0,3,2,1:T(8,128)(2,1)} %bitcast.130), kind=kOutput, calls=%fused_computation.6 | convolution fusion | flops 1214251008 | bytes 16908288 | tf_op jit(solution)/shard_map/nlbcd,nlbcf->ldf/dot_general | solution.py:42
  462.5 45.9 %all-to-all-done.6 = bf16[8,192,1024]{2,1,0:T(8,128)(2,1)S(1)} async-done(((bf16[8,192,1024]{2,1,0:T(8,128)(2,1)}), bf16[8,192,1024]{2,1,0:T(8,128)(2,1)S(1)}, u32[]{:S(2)}, u32[]{:S(2)}) %all-to-all-start.6) | async-done | bytes 3145760 | tf_op jit(solution)/shard_map/all_to_all | solution.py:125
  508.4 5.3 %gather_fusion = bf16[1024,1024]{1,0:T(8,128)(2,1)} fusion(bf16[1536,1024]{1,0:T(8,128)(2,1)S(1)} %bitcast.121, s32[1024]{0:T(1024)S(1)} %copy-done.3), kind=kCustom, calls=%fused_computation.2 | custom fusion | bytes 4198400 | tf_op jit(solution)/shard_map/gather | solution.py:134
  (77 shorter events, 34.8 us)
Async XLA Ops:
  7.2 6.1 %copy-start = (bf16[128,1024]{1,0:T(8,128)(2,1)S(1)}, bf16[128,1024]{1,0:T(8,128)(2,1)}, u32[]{:S(2)}) copy-start(bf16[128,1024]{1,0:T(8,128)(2,1)} %param.7) | copy-start | bytes 786436
  7.2 231.4 %all-gather.13.cloned.1.call-start = ((), (), s32[]{:S(2)}) async-start(), calls=%async_computation.9 | async-start | bytes 37748736 | tf_op jit(solution)/shard_map/all_gather | solution.py:50
  7.9 241.8 %all-gather.9.cloned.1.call-start = ((), (), s32[]{:S(2)}) async-start(), calls=%async_computation.7 | async-start | bytes 37748736 | tf_op jit(solution)/shard_map/all_gather | solution.py:52
  8.7 0.7 copy-start.4
  8.7 255.9 %all-gather.11.cloned.1.call-start = ((), (), s32[]{:S(2)}) async-start(), calls=%async_computation.8 | async-start | bytes 37748736 | tf_op jit(solution)/shard_map/all_gather | solution.py:51
  28.4 6.7 %copy-start.5 = (bf16[64,8]{0,1:T(8,128)(2,1)S(1)}, bf16[64,8]{0,1:T(8,128)(2,1)}, u32[]{:S(2)}) copy-start(bf16[64,8]{0,1:T(8,128)(2,1)} %param.9) | copy-start | bytes 3076
  28.4 75.3 %all-to-all-start.3 = ((bf16[8,192,1024]{2,1,0:T(8,128)(2,1)}), bf16[8,192,1024]{2,1,0:T(8,128)(2,1)S(1)}, u32[]{:S(2)}, u32[]{:S(2)}) async-start(bf16[8,192,1024]{2,1,0:T(8,128)(2,1)} %bitcast.131), calls=%async_computation.3 | async-start | bytes 6291456 | tf_op jit(solution)/shard_map/all_to_all | solution.py:96
  103.7 29.8 %all-to-all-start = ((bf16[8,1,192]{2,1,0:T(2,128)(2,1)}), bf16[8,1,192]{2,1,0:T(2,128)(2,1)S(1)}, u32[]{:S(2)}, u32[]{:S(2)}) async-start(bf16[8,1,192]{2,1,0:T(2,128)(2,1)} %all_to_all.62), calls=%async_computation | async-start | bytes 16384 | tf_op jit(solution)/shard_map/all_to_all | solution.py:98
  131.4 1.7 copy-start.2
  143.0 74.5 %all-to-all-start.1 = ((bf16[8,192,1024]{2,1,0:T(8,128)(2,1)}), bf16[8,192,1024]{2,1,0:T(8,128)(2,1)}, u32[]{:S(2)}, u32[]{:S(2)}) async-start(bf16[8,192,1024]{2,1,0:T(8,128)(2,1)} %bitcast.14), calls=%async_computation.1 | async-start | bytes 6291456 | tf_op jit(solution)/shard_map/all_to_all | solution.py:97
  149.0 291.2 %all-gather.15.cloned.1.call-start = ((), (), s32[]{:S(2)}) async-start(), calls=%async_computation.10 | async-start | bytes 1769472 | tf_op jit(solution)/shard_map/all_gather | solution.py:33
  433.0 75.4 %all-to-all-start.6 = ((bf16[8,192,1024]{2,1,0:T(8,128)(2,1)}), bf16[8,192,1024]{2,1,0:T(8,128)(2,1)S(1)}, u32[]{:S(2)}, u32[]{:S(2)}) async-start(bf16[8,192,1024]{2,1,0:T(8,128)(2,1)} %copy.131), calls=%async_computation.6 | async-start | bytes 6291456 | tf_op jit(solution)/shard_map/all_to_all | solution.py:125
  439.5 12.5 %all-gather.17.cloned.1.call-start = ((), (), s32[]{:S(2)}) async-start(), calls=%async_computation.11 | async-start | bytes 1769472 | tf_op jit(solution)/shard_map/all_gather | solution.py:34
  452.0 56.4 %copy-start.3 = (s32[1024]{0:T(1024)S(1)}, s32[1024]{0:T(1024)}, u32[]{:S(2)}) copy-start(s32[1024]{0:T(1024)} %broadcast_clamp_fusion) | copy-start | bytes 12292
  508.4 9.0 %copy-start.1 = (bf16[128,1024]{1,0:T(8,128)(2,1)S(1)}, bf16[128,1024]{1,0:T(8,128)(2,1)}, u32[]{:S(2)}) copy-start(bf16[128,1024]{1,0:T(8,128)(2,1)} %param.7) | copy-start | bytes 786436
Sparse Core Ops, SparseCore 0:
  9.6 43.4 all-gather.12
  54.6 41.4 all-gather.8
  97.7 45.5 all-gather.10
  276.8 10.5 all-gather.14
  441.6 10.3 all-gather.16
where the time goes:
time: 532 us; the launch traced here: 524 us
  local copies, waits for them, and re-layouts  179 us (34%)
  waiting for transfers between devices  179 us (34%)
  matrix products  87.5 us (16%)
  blocking collectives  33.4 us (6%)
  starting transfers between devices  25.4 us (5%)
  between operations  14.3 us (3%)
  other arithmetic  5.53 us (1%)
    unnamed x15, local copies, waits for them, and re-layouts  66.1 us
    all_to_all x1, waiting for transfers between devices, body(): lax.all_to_all(send_grads, 'ep', split_axis=0, concat_axis=0, tiled=True)  65.2 us
    all_to_all x1, waiting for transfers between devices, body(): lax.all_to_all(send_rows, 'ep', split_axis=0, concat_axis=0, tiled=True)  63.8 us
    all_to_all x1, waiting for transfers between devices, body(): lax.all_to_all(spread.reshape(ep_count, local_count * 2 * capacity, half_...  45.9 us
    scatter x3, local copies, waits for them, and re-layouts, fill_slots(): return zeroed.at[slot_ids].set(values)  38.9 us
    all_to_all x2, local copies, waits for them, and re-layouts, body(): lax.all_to_all(row_grad.reshape(ep_count, local_count, 1, capacity, featu...  27.7 us
    reshape x1, local copies, waits for them, and re-layouts, body(): row_grad.reshape(ep_count, local_count, 1, capacity, feature_width)  25.1 us
    dot_general x1, matrix products, expert_work(): jnp.einsum('nlcd,lfd->nlcf', grad_rows, full_down, preferred_element_type...  14.9 us
  transfers between devices with their start and end apart: 9, of which 4 were waited for; matrix products, arithmetic and copies ran while one was open for 47% of the time, Pallas kernels for 0%

commit v1 on v0

--- a/solution.py
+++ b/solution.py
@@ -1,9 +1,14 @@
+import functools
+
 import jax
 import jax.numpy as jnp
 from jax import lax
+from jax.experimental import pallas as pl
+from jax.experimental.pallas import tpu as pltpu
 from jax.sharding import PartitionSpec as P
 
 CAP = 6
+VMEM_LIMIT = 48 * 1024 * 1024
 
 
 def route_slots(expert_ids, experts, stride, offset):
@@ -66,7 +71,7 @@
     return (row_grad, grad_gate_pre, grad_up_pre)
 
 
-def body(tokens, out_grad, route_gates, expert_ids, w_gate, w_up, w_down):
+def exchange_body(tokens, out_grad, route_gates, expert_ids, w_gate, w_up, w_down):
     ep_count = lax.axis_size("ep")
     local_count = w_gate.shape[0]
     experts = local_count * ep_count
@@ -137,6 +142,453 @@
     return (grad_input, grad_gate_w, grad_up_w)
 
 
+def arrival_orders(lines):
+    orders = []
+    for here in range(lines):
+        flip = here >= (lines + 1) // 2
+        near = sorted(
+            (j for j in range(lines) if j != here),
+            key=lambda j: (abs(j - here), (j < here) if flip else (j > here)),
+        )
+        orders.append([here] + near)
+    return orders
+
+
+def pick(here, choices):
+    result, distinct = choices[0], []
+    for position, value in enumerate(choices):
+        if not any(value is seen for seen, _ in distinct):
+            distinct.append((value, [position]))
+        else:
+            for seen, places in distinct:
+                if seen is value:
+                    places.append(position)
+    result = distinct[0][0]
+    for value, places in distinct[1:]:
+        chosen = functools.reduce(jnp.logical_or, [here == place for place in places])
+        result = jnp.where(chosen, value, result)
+    return result
+
+
+def along_line(value, lines, upward, first):
+    if upward:
+        moves = [(q, q + 1) for q in range(lines - 1) if q >= first]
+    else:
+        moves = [(q, q - 1) for q in range(1, lines) if lines - 1 - q >= first]
+    pairs = [(2 * a + side, 2 * b + side) for a, b in moves for side in range(2)]
+    return lax.ppermute(value, "ep", pairs)
+
+
+def across_pair(value, lines):
+    return lax.ppermute(value, "ep", [(i, i ^ 1) for i in range(2 * lines)])
+
+
+def across_cores(value):
+    return lax.ppermute(value, "dp", [(0, 1), (1, 0)])
+
+
+def gather_pieces(value, lines, here, orders):
+    ups, downs = [], []
+    up = down = value
+    for step in range(lines - 1):
+        up, down = along_line(up, lines, True, step), along_line(down, lines, False, step)
+        ups.append(up)
+        downs.append(down)
+    pieces = []
+    for m in range(lines):
+        choices = []
+        for q in range(lines):
+            source = orders[q][m]
+            if source == q:
+                choices.append(value)
+            elif source < q:
+                choices.append(ups[q - source - 1])
+            else:
+                choices.append(downs[source - q - 1])
+        own = pick(here, choices)
+        pieces += [own, across_pair(own, lines)]
+    return pieces
+
+
+def scatter_sums(partial, lines, here, orders):
+    halves = [None] * lines
+    for m in reversed(range(lines)):
+        other = across_pair(partial[2 * m + 1], lines)
+        halves[m] = partial[2 * m].astype(jnp.float32) + other.astype(jnp.float32)
+    up = down = None
+    for step in range(1, lines):
+        reach = lines - step
+        moved = []
+        for upward, came in ((True, up), (False, down)):
+            choices = []
+            for q in range(lines):
+                target = q + reach if upward else q - reach
+                usable = 0 <= target < lines
+                choices.append(halves[orders[q].index(target)] if usable else None)
+            spare = next(c for c in choices if c is not None)
+            total = pick(here, [spare if c is None else c for c in choices])
+            if came is not None:
+                total = total + came.astype(jnp.float32)
+            total = total.astype(jnp.bfloat16)
+            if upward:
+                moves = [(q, q + 1) for q in range(lines) if q + reach < lines]
+            else:
+                moves = [(q, q - 1) for q in range(lines) if q - reach >= 0]
+            pairs = [(2 * a + side, 2 * b + side) for a, b in moves for side in range(2)]
+            moved.append(lax.ppermute(total, "ep", pairs))
+        up, down = moved
+    total = halves[0]
+    if lines > 1:
+        total = total + up.astype(jnp.float32) + down.astype(jnp.float32)
+    return total.astype(jnp.bfloat16)
+
+
+def route_kernel(order_ref, base_ref, info_ref, slot_ref, gate_ref, *, top_count, block_rows):
+    local_count = slot_ref.shape[0]
+    chunk = info_ref.shape[2]
+    row = lax.broadcasted_iota(jnp.int32, (chunk, chunk), 0)
+    column = lax.broadcasted_iota(jnp.int32, (chunk, chunk), 1)
+    before = ((row < column) & (row // block_rows == column // block_rows)).astype(jnp.bfloat16)
+    lane = lax.broadcasted_iota(jnp.int32, (local_count, chunk), 1)
+    expert = (base_ref[0] + lax.broadcasted_iota(jnp.int32, (local_count, chunk), 0)).astype(
+        jnp.float32
+    )
+    for piece in range(info_ref.shape[0]):
+        info = info_ref[order_ref[piece]].astype(jnp.float32)
+        named = jnp.zeros((local_count, chunk), jnp.float32)
+        gate = jnp.zeros((local_count, chunk), jnp.float32)
+        for k in range(top_count):
+            match = info[k : k + 1, :] == expert
+            named = jnp.where(match, 1.0, named)
+            gate = jnp.where(match, info[top_count + k : top_count + k + 1, :], gate)
+        rank = jnp.dot(
+            named.astype(jnp.bfloat16), before, preferred_element_type=jnp.float32
+        ).astype(jnp.int32)
+        block = piece * (chunk // block_rows) + lane // block_rows
+        columns = pl.ds(piece * chunk, chunk)
+        slot_ref[:, columns] = jnp.where(named > 0.5, block * CAP + rank, -1)
+        gate_ref[:, columns] = gate
+
+
+def one_hot(slot_ref, expert, slots):
+    tokens = slot_ref.shape[1]
+    own = slot_ref[pl.ds(expert, 1), :]
+    return lax.broadcasted_iota(jnp.int32, (slots, tokens), 0) == own
+
+
+def collect_rows(piece_refs, rows_ref, sems):
+    chunk = piece_refs[0].shape[0]
+    copies = [
+        pltpu.make_async_copy(ref, rows_ref.at[pl.ds(m * chunk, chunk)], sems.at[m])
+        for m, ref in enumerate(piece_refs)
+    ]
+    for copy in copies:
+        copy.start()
+    for copy in copies:
+        copy.wait()
+
+
+def pre_kernel(count, slots, slot_ref, *refs):
+    pieces = refs[:count]
+    gate_w_ref, up_w_ref, x_ref, gate_ref, up_ref, rows_ref, sems = refs[count:]
+    step = pl.program_id(0)
+    batch = gate_w_ref.shape[0]
+
+    @pl.when(step == 0)
+    def _():
+        collect_rows(pieces, rows_ref, sems)
+
+    hot = jnp.concatenate(
+        [one_hot(slot_ref, step * batch + i, slots).astype(jnp.bfloat16) for i in range(batch)]
+    )
+    x = jnp.dot(hot, rows_ref[...], preferred_element_type=jnp.float32).astype(jnp.bfloat16)
+    for i in range(batch):
+        own = x[i * slots : (i + 1) * slots]
+        x_ref[i] = own
+        gate_ref[i] = jnp.dot(own, gate_w_ref[i], preferred_element_type=jnp.float32)
+        up_ref[i] = jnp.dot(own, up_w_ref[i], preferred_element_type=jnp.float32)
+
+
+def down_kernel(count, slots, slot_ref, gates_ref, *refs):
+    pieces = refs[:count]
+    down_w_ref, raw_ref, rows_ref, sems = refs[count:]
+    step = pl.program_id(0)
+    batch = down_w_ref.shape[0]
+
+    @pl.when(step == 0)
+    def _():
+        collect_rows(pieces, rows_ref, sems)
+
+    hots = [one_hot(slot_ref, step * batch + i, slots) for i in range(batch)]
+    hot = jnp.concatenate([h.astype(jnp.bfloat16) for h in hots])
+    x = jnp.dot(hot, rows_ref[...], preferred_element_type=jnp.float32).astype(jnp.bfloat16)
+    for i in range(batch):
+        own = x[i * slots : (i + 1) * slots]
+        raw = lax.dot_general(
+            own, down_w_ref[i], (((1,), (1,)), ((), ())), preferred_element_type=jnp.float32
+        )
+        gates = gates_ref[pl.ds(step * batch + i, 1), :]
+        gate = jnp.sum(jnp.where(hots[i], gates, 0.0), axis=1, keepdims=True)
+        raw_ref[i] = gate * raw
+
+
+def add_rows(slot_ref, step, slots, grads, gate_w_ref, up_w_ref, sum_ref, out_ref):
+    batch = gate_w_ref.shape[0]
+    contract = (((1,), (1,)), ((), ()))
+    hots, rows = [], []
+    for i, (grad_gate, grad_up) in enumerate(grads):
+        row = lax.dot_general(
+            grad_gate, gate_w_ref[i], contract, preferred_element_type=jnp.float32
+        ) + lax.dot_general(grad_up, up_w_ref[i], contract, preferred_element_type=jnp.float32)
+        rows.append(row.astype(jnp.bfloat16))
+        hots.append(one_hot(slot_ref, step * batch + i, slots).astype(jnp.bfloat16))
+    added = lax.dot_general(
+        jnp.concatenate(hots),
+        jnp.concatenate(rows),
+        (((0,), (0,)), ((), ())),
+        preferred_element_type=jnp.float32,
+    )
+
+    @pl.when(step == 0)
+    def _():
+        sum_ref[...] = added
+
+    @pl.when(step > 0)
+    def _():
+        sum_ref[...] += added
+
+    @pl.when(step == pl.num_programs(0) - 1)
+    def _():
+        out_ref[...] = sum_ref[...].astype(jnp.bfloat16)
+
+
+def first_rows_kernel(
+    slots,
+    slot_ref,
+    gate_own,
+    gate_other,
+    up_own,
+    up_other,
+    raw_own,
+    raw_other,
+    gate_w_ref,
+    up_w_ref,
+    grad_gate_ref,
+    grad_up_ref,
+    out_ref,
+    sum_ref,
+):
+    step = pl.program_id(0)
+    batch = gate_w_ref.shape[0]
+    grads = []
+    for i in range(batch):
+        pre_gate = gate_own[i] + gate_other[i]
+        pre_up = up_own[i] + up_other[i]
+        grad_hidden = raw_own[i] + raw_other[i]
+        sigmoid = jax.nn.sigmoid(pre_gate)
+        scaled = grad_hidden * sigmoid
+        grad_gate = (scaled * pre_up * (1.0 + pre_gate * (1.0 - sigmoid))).astype(jnp.bfloat16)
+        grad_up = (scaled * pre_gate).astype(jnp.bfloat16)
+        grad_gate_ref[i] = grad_gate
+        grad_up_ref[i] = grad_up
+        grads.append((grad_gate, grad_up))
+    add_rows(slot_ref, step, slots, grads, gate_w_ref, up_w_ref, sum_ref, out_ref)
+
+
+def later_rows_kernel(
+    slots, slot_ref, grad_gate_ref, grad_up_ref, gate_w_ref, up_w_ref, out_ref, sum_ref
+):
+    grads = [(grad_gate_ref[i], grad_up_ref[i]) for i in range(gate_w_ref.shape[0])]
+    add_rows(slot_ref, pl.program_id(0), slots, grads, gate_w_ref, up_w_ref, sum_ref, out_ref)
+
+
+def weight_kernel(x_ref, grad_gate_ref, grad_up_ref, gate_out_ref, up_out_ref):
+    contract = (((0,), (0,)), ((), ()))
+    for i in range(x_ref.shape[0]):
+        x = x_ref[i]
+        gate_out_ref[i] = lax.dot_general(
+            x, grad_gate_ref[i], contract, preferred_element_type=jnp.float32
+        ).astype(jnp.bfloat16)
+        up_out_ref[i] = lax.dot_general(
+            x, grad_up_ref[i], contract, preferred_element_type=jnp.float32
+        ).astype(jnp.bfloat16)
+
+
+def params():
+    return pltpu.CompilerParams(
+        vmem_limit_bytes=VMEM_LIMIT, dimension_semantics=("arbitrary",)
+    )
+
+
+def cost(flops, moved):
+    return pl.CostEstimate(flops=int(flops), bytes_accessed=int(moved), transcendentals=0)
+
+
+def whole(*shape):
+    return pl.BlockSpec(shape, lambda e: (0,) * len(shape))
+
+
+def batched(batch, *shape):
+    return pl.BlockSpec((batch,) + shape, lambda e: (e,) + (0,) * len(shape))
+
+
+def gather_body(tokens, out_grad, route_gates, expert_ids, w_gate, w_up, w_down):
+    ep_count = lax.axis_size("ep")
+    lines = ep_count // 2
+    local_count, half_width, hidden = w_gate.shape
+    block_rows, top_count = expert_ids.shape
+    chunk = 2 * block_rows
+    token_count = ep_count * chunk
+    slots = 2 * ep_count * CAP
+    chunks = 2
+    width = half_width // chunks
+    batch = 2 if local_count % 2 == 0 else 1
+    steps = local_count // batch
+    place = lax.axis_index("ep")
+    here, side = place // 2, place % 2
+    orders = arrival_orders(lines)
+    bf16, f32 = jnp.bfloat16, jnp.float32
+    memory = pl.BlockSpec(memory_space=pl.ANY)
+    smem = pl.BlockSpec(memory_space=pltpu.SMEM)
+    vmem = pl.BlockSpec(memory_space=pltpu.VMEM)
+
+    own_info = jnp.concatenate([expert_ids.astype(bf16), route_gates], axis=1).T
+    info = jnp.zeros((ep_count, 2 * top_count, chunk), bf16)
+    info = lax.dynamic_update_slice(
+        info, own_info[None], (place, 0, lax.axis_index("dp") * block_rows)
+    )
+    info = info + across_cores(info)
+    bit = 1
+    while bit < ep_count:
+        info = info + lax.ppermute(info, "ep", [(i, i ^ bit) for i in range(ep_count)])
+        bit *= 2
+
+    token_pieces = gather_pieces(tokens, lines, here, orders)
+    grad_pieces = gather_pieces(out_grad, lines, here, orders)
+
+    line_order = jnp.asarray(orders, jnp.int32)[here]
+    order = (2 * line_order[:, None] + jnp.stack([side, 1 - side])[None, :]).reshape(-1)
+    slot_of, gate_of = pl.pallas_call(
+        functools.partial(route_kernel, top_count=top_count, block_rows=block_rows),
+        out_shape=(
+            jax.ShapeDtypeStruct((local_count, token_count), jnp.int32),
+            jax.ShapeDtypeStruct((local_count, token_count), f32),
+        ),
+        in_specs=[smem, smem, vmem],
+        out_specs=(vmem, vmem),
+        compiler_params=pltpu.CompilerParams(vmem_limit_bytes=VMEM_LIMIT),
+        cost_estimate=cost(1e7, 1e6),
+        name="route",
+    )(order, (place * local_count).reshape(1), info)
+
+    rows_scratch = [
+        pltpu.VMEM((token_count, half_width), bf16),
+        pltpu.SemaphoreType.DMA((ep_count,)),
+    ]
+    weight_bytes = local_count * half_width * hidden * 2
+    matmul_flops = 2 * local_count * slots * half_width * hidden
+    hot_flops = 2 * local_count * slots * half_width * token_count
+    pre_shape = jax.ShapeDtypeStruct((local_count, slots, hidden), f32)
+    grad_shape = jax.ShapeDtypeStruct((local_count, slots, hidden), bf16)
+    x, gate_part, up_part = pl.pallas_call(
+        functools.partial(pre_kernel, ep_count, slots),
+        grid=(steps,),
+        out_shape=(
+            jax.ShapeDtypeStruct((local_count, slots, half_width), bf16),
+            pre_shape,
+            pre_shape,
+        ),
+        in_specs=[whole(local_count, token_count)]
+        + [memory] * ep_count
+        + [batched(batch, half_width, hidden)] * 2,
+        out_specs=(
+            batched(batch, slots, half_width),
+            batched(batch, slots, hidden),
+            batched(batch, slots, hidden),
+        ),
+        scratch_shapes=rows_scratch,
+        compiler_params=params(),
+        cost_estimate=cost(hot_flops + 2 * matmul_flops, 2.5 * weight_bytes),
+        name="pre",
+    )(slot_of, *token_pieces, w_gate, w_up)
+    gate_other, up_other = across_cores(gate_part), across_cores(up_part)
+
+    raw_part = pl.pallas_call(
+        functools.partial(down_kernel, ep_count, slots),
+        grid=(steps,),
+        out_shape=pre_shape,
+        in_specs=[whole(local_count, token_count)] * 2
+        + [memory] * ep_count
+        + [batched(batch, hidden, half_width)],
+        out_specs=batched(batch, slots, hidden),
+        scratch_shapes=rows_scratch,
+        compiler_params=params(),
+        cost_estimate=cost(hot_flops + matmul_flops, 1.3 * weight_bytes),
+        name="down",
+    )(slot_of, gate_of, *grad_pieces, w_down)
+    raw_other = across_cores(raw_part)
+
+    def part_of_weights(number):
+        return pl.BlockSpec((batch, width, hidden), lambda e: (e, number, 0))
+
+    rows_cost = cost(
+        (2 * matmul_flops + hot_flops) / chunks, 2 * weight_bytes / chunks + weight_bytes / 2
+    )
+    sums = jax.ShapeDtypeStruct((token_count, width), bf16)
+    sum_scratch = [pltpu.VMEM((token_count, width), f32)]
+    grad_gate, grad_up, partial = pl.pallas_call(
+        functools.partial(first_rows_kernel, slots),
+        grid=(steps,),
+        out_shape=(grad_shape, grad_shape, sums),
+        in_specs=[whole(local_count, token_count)]
+        + [batched(batch, slots, hidden)] * 6
+        + [part_of_weights(0)] * 2,
+        out_specs=(
+            batched(batch, slots, hidden),
+            batched(batch, slots, hidden),
+            whole(token_count, width),
+        ),
+        scratch_shapes=sum_scratch,
+        compiler_params=params(),
+        cost_estimate=rows_cost,
+        name="rows_first",
+    )(slot_of, gate_part, gate_other, up_part, up_other, raw_part, raw_other, w_gate, w_up)
+    partials = [partial]
+    for number in range(1, chunks):
+        partials.append(
+            pl.pallas_call(
+                functools.partial(later_rows_kernel, slots),
+                grid=(steps,),
+                out_shape=sums,
+                in_specs=[whole(local_count, token_count)]
+                + [batched(batch, slots, hidden)] * 2
+                + [part_of_weights(number)] * 2,
+                out_specs=whole(token_count, width),
+                scratch_shapes=sum_scratch,
+                compiler_params=params(),
+                cost_estimate=rows_cost,
+                name="rows_later",
+            )(slot_of, grad_gate, grad_up, w_gate, w_up)
+        )
+    weight_shape = jax.ShapeDtypeStruct(w_gate.shape, bf16)
+    grad_gate_w, grad_up_w = pl.pallas_call(
+        weight_kernel,
+        grid=(steps,),
+        out_shape=(weight_shape, weight_shape),
+        in_specs=[batched(batch, slots, half_width)] + [batched(batch, slots, hidden)] * 2,
+        out_specs=(batched(batch, half_width, hidden), batched(batch, half_width, hidden)),
+        compiler_params=params(),
+        cost_estimate=cost(2 * matmul_flops, 2.5 * weight_bytes),
+        name="weight_grads",
+    )(x, grad_gate, grad_up)
+
+    returned = [
+        scatter_sums(value.reshape(ep_count, chunk, width), lines, here, orders)
+        for value in partials
+    ]
+    return (jnp.concatenate(returned, axis=1), grad_gate_w, grad_up_w)
+
+
 def solution(mesh):
     in_specs = (
         P(("groups", "ep"), "dp"),
@@ -152,4 +604,6 @@
         P(("groups", "ep"), "dp", None),
         P(("groups", "ep"), "dp", None),
     )
+    ep_count = mesh.shape["ep"]
+    body = gather_body if ep_count in (2, 4, 8) else exchange_body
     return jax.shard_map(body, mesh=mesh, in_specs=in_specs, out_specs=out_specs, check_vma=False)

time: 532 us -> 197 us (0.37); the launches traced: 524 us -> 195 us
  local copies, waits for them, and re-layouts: 179 us -> 0.7 us
  waiting for transfers between devices: 179 us -> 43.9 us
  matrix products: 87.5 us -> 0 us
  Pallas kernels: 0 us -> 63.8 us
  starting transfers between devices: 25.4 us -> 80.6 us
  blocking collectives: 33.4 us -> 0 us
  between operations: 14.3 us -> 1.24 us
    all_to_all x4 -> x0, waiting for transfers between devices: 175 us -> none  [the longest x1 65.2 us: body(): lax.all_to_all(send_grads, 'ep', split_axis=0, concat_axis=0, tiled=True)]
    dot_general x7 -> x0, matrix products: 87.5 us -> none  [the longest x1 14.9 us: expert_work(): jnp.einsum('nlcd,lfd->nlcf', grad_rows, full_down, preferred_element_type...]
    ppermute x0 -> x47, starting transfers between devices: none -> 80.6 us  [the longest x12 30.8 us: scatter_sums(): moved.append(lax.ppermute(total, 'ep', pairs))]
    unnamed x15 -> x12, local copies, waits for them, and re-layouts: 66.1 us -> 0.31 us
    pallas_call x0 -> x6, Pallas kernels: none -> 63.8 us  [the longest x1 15 us: gather_body(): pl.pallas_call(functools.partial(pre_kernel, ep_count, slots), grid=(step...]
    ppermute x0 -> x47, waiting for transfers between devices: none -> 43.9 us  [the longest x16 16.3 us: across_pair(): return lax.ppermute(value, 'ep', [(i, i ^ 1) for i in range(2 * lines)])]
    scatter x3 -> x0, local copies, waits for them, and re-layouts: 38.9 us -> none  [fill_slots(): return zeroed.at[slot_ids].set(values)]
    all_to_all x7 -> x0, local copies, waits for them, and re-layouts: 38.2 us -> none  [the longest x2 27.7 us: body(): lax.all_to_all(row_grad.reshape(ep_count, local_count, 1, capacity, featu...]
  transfers between devices with their start and end apart: 9 -> 47, of which waited for: 4 -> 16; matrix products, arithmetic and copies ran while one was open for 47% -> 2% of each run, Pallas kernels for 0% -> 26%
where the time goes in v1:
time: 197 us; the launch traced here: 195 us
  starting transfers between devices  80.6 us (41%)
  Pallas kernels  63.8 us (32%)
  waiting for transfers between devices  43.9 us (22%)
  other arithmetic  4.64 us (2%)
    ppermute x12, starting transfers between devices, scatter_sums(): moved.append(lax.ppermute(total, 'ep', pairs))  30.8 us
    ppermute x12, starting transfers between devices, along_line(): return lax.ppermute(value, 'ep', pairs)  29.8 us
    ppermute x16, starting transfers between devices, across_pair(): return lax.ppermute(value, 'ep', [(i, i ^ 1) for i in range(2 * lines)])  17.6 us
    ppermute x16, waiting for transfers between devices, across_pair(): return lax.ppermute(value, 'ep', [(i, i ^ 1) for i in range(2 * lines)])  16.3 us
    pallas_call x1, Pallas kernels, gather_body(): pl.pallas_call(functools.partial(pre_kernel, ep_count, slots), grid=(step...  15 us
    pallas_call x1, Pallas kernels, gather_body(): pl.pallas_call(functools.partial(first_rows_kernel, slots), grid=(steps,)...  13.9 us
    pallas_call x1, Pallas kernels, gather_body(): pl.pallas_call(functools.partial(later_rows_kernel, slots), grid=(steps,)...  11.9 us
    pallas_call x1, Pallas kernels, gather_body(): pl.pallas_call(functools.partial(down_kernel, ep_count, slots), grid=(ste...  11.3 us
  transfers between devices with their start and end apart: 47, of which 16 were waited for; matrix products, arithmetic and copies ran while one was open for 2% of the time, Pallas kernels for 26%

profile of v1, /device:TPU:12, one launch (start us, length us, event | category | flops | bytes accessed | tf_op | source)
XLA Modules:
  0.0 195.0 jit_solution(968943341384808310)
XLA Ops:
  0.6 3.5 %collective-permute-start.17 = (bf16[128,1024]{1,0:T(8,128)(2,1)}, bf16[128,1024]{1,0:T(8,128)(2,1)S(1)}, u32[]{:S(2)}, u32[]{:S(2)}) collective-permute-start(bf16[128,1024]{1,0:T(8,128)(2,1)} %refs_0_.3), channel_id=1, source_target_pairs={{0,4},{2,6},{4,8},{6,10},{8,12},{10,14},{1,5},{3,7},{5,9},{7,11},{... | collective-permute-start | bytes 786440 | tf_op jit(solution)/shard_map/ppermute | solution.py:179
  4.1 2.4 %collective-permute-start.18 = (bf16[128,1024]{1,0:T(8,128)(2,1)}, bf16[128,1024]{1,0:T(8,128)(2,1)S(1)}, u32[]{:S(2)}, u32[]{:S(2)}) collective-permute-start(bf16[128,1024]{1,0:T(8,128)(2,1)} %refs_0_.3), channel_id=1, source_target_pairs={{4,0},{6,2},{8,4},{10,6},{12,8},{14,10},{5,1},{7,3},{9,5},{11,7},{... | collective-permute-start | bytes 786440 | tf_op jit(solution)/shard_map/ppermute | solution.py:179
  6.5 3.5 %collective-permute-start.5 = (bf16[128,1024]{1,0:T(8,128)(2,1)}, bf16[128,1024]{1,0:T(8,128)(2,1)S(1)}, u32[]{:S(2)}, u32[]{:S(2)}) collective-permute-start(bf16[128,1024]{1,0:T(8,128)(2,1)} %refs_0_.2), channel_id=1, source_target_pairs={{0,4},{2,6},{4,8},{6,10},{8,12},{10,14},{1,5},{3,7},{5,9},{7,11},{... | collective-permute-start | bytes 786440 | tf_op jit(solution)/shard_map/ppermute | solution.py:179
  10.0 2.4 %collective-permute-start.6 = (bf16[128,1024]{1,0:T(8,128)(2,1)}, bf16[128,1024]{1,0:T(8,128)(2,1)S(1)}, u32[]{:S(2)}, u32[]{:S(2)}) collective-permute-start(bf16[128,1024]{1,0:T(8,128)(2,1)} %refs_0_.2), channel_id=1, source_target_pairs={{4,0},{6,2},{8,4},{10,6},{12,8},{14,10},{5,1},{7,3},{9,5},{11,7},{... | collective-permute-start | bytes 786440 | tf_op jit(solution)/shard_map/ppermute | solution.py:179
  13.1 3.5 %collective-permute-start.20 = (bf16[128,1024]{1,0:T(8,128)(2,1)S(1)}, bf16[128,1024]{1,0:T(8,128)(2,1)S(1)}, u32[]{:S(2)}, u32[]{:S(2)}) collective-permute-start(bf16[128,1024]{1,0:T(8,128)(2,1)S(1)} %collective-permute-done.17), channel_id=1, source_target_pairs={{4,8},{6,10},{8,12},{10,14},{5,9},{7,11},{9,13},{11,15},{20,24},{2... | collective-permute-start | bytes 786440 | tf_op jit(solution)/shard_map/ppermute | solution.py:179
  23.1 2.3 %collective-permute-done.1 = bf16[8,16,128]{2,1,0:T(8,128)(2,1)S(1)} collective-permute-done((bf16[8,16,128]{2,1,0:T(8,128)(2,1)S(1)}, bf16[8,16,128]{2,1,0:T(8,128)(2,1)S(1)}, u32[]{:S(2)}, u32[]{:S(2)}) %collective-permute-start.1) | collective-permute-done | bytes 32800 | tf_op jit(solution)/shard_map/ppermute | solution.py:463
  25.5 3.9 %collective-permute-start.8 = (bf16[128,1024]{1,0:T(8,128)(2,1)S(1)}, bf16[128,1024]{1,0:T(8,128)(2,1)S(1)}, u32[]{:S(2)}, u32[]{:S(2)}) collective-permute-start(bf16[128,1024]{1,0:T(8,128)(2,1)S(1)} %collective-permute-done.5), channel_id=1, source_target_pairs={{4,8},{6,10},{8,12},{10,14},{5,9},{7,11},{9,13},{11,15},{20,24},{2... | collective-permute-start | bytes 786440 | tf_op jit(solution)/shard_map/ppermute | solution.py:179
  34.4 4.8 %collective-permute-done.3 = bf16[8,16,128]{2,1,0:T(8,128)(2,1)S(1)} collective-permute-done((bf16[8,16,128]{2,1,0:T(8,128)(2,1)S(1)}, bf16[8,16,128]{2,1,0:T(8,128)(2,1)S(1)}, u32[]{:S(2)}, u32[]{:S(2)}) %collective-permute-start.3) | collective-permute-done | bytes 32800 | tf_op jit(solution)/shard_map/ppermute | solution.py:463
  42.7 4.2 %collective-permute-start.12 = (bf16[128,1024]{1,0:T(8,128)(2,1)S(1)}, bf16[128,1024]{1,0:T(8,128)(2,1)S(1)}, u32[]{:S(2)}, u32[]{:S(2)}) collective-permute-start(bf16[128,1024]{1,0:T(8,128)(2,1)S(1)} %collective-permute-done.9), channel_id=1, source_target_pairs={{4,0},{6,2},{5,1},{7,3},{20,16},{22,18},{21,17},{23,19}} | collective-permute-start | bytes 786440 | tf_op jit(solution)/shard_map/ppermute | solution.py:179
  55.7 4.1 %collective-permute-done.25.refs_7_ = bf16[128,1024]{1,0:T(8,128)(2,1)S(1)} collective-permute-done((bf16[128,1024]{1,0:T(8,128)(2,1)S(1)}, bf16[128,1024]{1,0:T(8,128)(2,1)S(1)}, u32[]{:S(2)}, u32[]{:S(2)}) %collective-permute-start.25) | collective-permute-done | bytes 262176 | tf_op jit(solution)/shard_map/ppermute | solution.py:183
  61.3 4.1 %collective-permute-done.22.refs_5_ = bf16[128,1024]{1,0:T(8,128)(2,1)S(1)} collective-permute-done((bf16[128,1024]{1,0:T(8,128)(2,1)S(1)}, bf16[128,1024]{1,0:T(8,128)(2,1)S(1)}, u32[]{:S(2)}, u32[]{:S(2)}) %collective-permute-start.22) | collective-permute-done | bytes 262176 | tf_op jit(solution)/shard_map/ppermute | solution.py:183
  67.0 4.1 %collective-permute-done.19.refs_3_ = bf16[128,1024]{1,0:T(8,128)(2,1)S(1)} collective-permute-done((bf16[128,1024]{1,0:T(8,128)(2,1)S(1)}, bf16[128,1024]{1,0:T(8,128)(2,1)S(1)}, u32[]{:S(2)}, u32[]{:S(2)}) %collective-permute-start.19) | collective-permute-done | bytes 262176 | tf_op jit(solution)/shard_map/ppermute | solution.py:183
  71.1 11.3 %down.1.raw_own = f32[16,96,384]{2,1,0:T(8,128)S(1)} custom-call(s32[16,1024]{1,0:T(8,128)S(1)} %get-tuple-element.13.slot_ref, f32[16,1024]{1,0:T(8,128)S(1)} %get-tuple-element.16.gates_ref, bf16[128,1024]{1,0:T(8,128)(2,1)S(1)} %copy-done.1, bf16[128,1024]{1,0:T(8,128)(2,1)S(1)} %collective-permute-done.16.refs_1_, ...), custom_call_target="tpu_custom_call" | custom-call | flops 4429185024 | bytes 16357785 | tf_op jit(solution)/shard_map/down/pallas_call | solution.py:516
  84.6 15.0 %pre.1 = (bf16[16,96,1024]{2,1,0:T(8,128)(2,1)}, f32[16,96,384]{2,1,0:T(8,128)S(1)}, f32[16,96,384]{2,1,0:T(8,128)}) custom-call(s32[16,1024]{1,0:T(8,128)S(1)} %get-tuple-element.13.slot_ref, bf16[128,1024]{1,0:T(8,128)(2,1)S(1)} %copy-done.2, bf16[128,1024]{1,0:T(8,128)(2,1)S(1)} %collective-permute-done.4.refs_1_, ...), custom_call_target="tpu_custom_call" | custom-call | flops 5637144576 | bytes 31457280 | tf_op jit(solution)/shard_map/pre/pallas_call | solution.py:493
  100.1 6.6 %collective-permute-done.14.gate_other = f32[16,96,384]{2,1,0:T(8,128)S(1)} collective-permute-done((f32[16,96,384]{2,1,0:T(8,128)S(1)}, f32[16,96,384]{2,1,0:T(8,128)S(1)}, u32[]{:S(2)}, u32[]{:S(2)}) %collective-permute-start.14) | collective-permute-done | bytes 2359328 | tf_op jit(solution)/shard_map/ppermute | solution.py:187
  108.2 13.9 %rows_first.1 = (bf16[16,96,384]{2,1,0:T(8,128)(2,1)S(1)}, bf16[16,96,384]{2,1,0:T(8,128)(2,1)S(1)}, bf16[1024,512]{1,0:T(8,128)(2,1)S(1)}) custom-call(s32[16,1024]{1,0:T(8,128)S(1)} %get-tuple-element.13.slot_ref, f32[16,96,384]{2,1,0:T(8,128)S(1)} %get-tuple-element.14.gate_own, f32[16,96,384]{2,1,0:T(8,128)} %copy-done.5, ...), custom_call_target="tpu_custom_call" | custom-call | flops 2818572288 | bytes 18874368 | tf_op jit(solution)/shard_map/rows_first/pallas_call | solution.py:539
  126.2 11.9 %rows_later.1 = bf16[1024,512]{1,0:T(8,128)(2,1)S(1)} custom-call(s32[16,1024]{1,0:T(8,128)S(1)} %get-tuple-element.13.slot_ref, bf16[16,96,384]{2,1,0:T(8,128)(2,1)S(1)} %get-tuple-element.18.grad_gate_ref, bf16[16,96,384]{2,1,0:T(8,128)(2,1)S(1)} %get-tuple-element.19.grad_up_ref, bf16[16,1024,384]{2,1,0:T(8,128)(2,1)} %gate_w_ref.3, ...), custom_call_target="tpu_custom_call" | custom-call | flops 2818572288 | bytes 18874368 | tf_op jit(solution)/shard_map/rows_later/pallas_call | solution.py:559
  139.7 11.1 %weight_grads.1 = (bf16[16,1024,384]{2,1,0:T(8,128)(2,1)}, bf16[16,1024,384]{2,1,0:T(8,128)(2,1)}) custom-call(bf16[16,96,1024]{2,1,0:T(8,128)(2,1)S(1)} %copy-done.3, bf16[16,96,384]{2,1,0:T(8,128)(2,1)S(1)} %get-tuple-element.18.grad_gate_ref, bf16[16,96,384]{2,1,0:T(8,128)(2,1)S(1)} %get-tuple-element.19.grad_up_ref), custom_call_target="tpu_custom_call" | custom-call | flops 2415919104 | bytes 31457280 | tf_op jit(solution)/shard_map/weight_grads/pallas_call | solution.py:574
  154.1 4.2 %collective-permute-done.31 = bf16[128,512]{1,0:T(8,128)(2,1)S(1)} collective-permute-done((bf16[128,512]{1,0:T(8,128)(2,1)S(1)}, bf16[128,512]{1,0:T(8,128)(2,1)S(1)}, u32[]{:S(2)}, u32[]{:S(2)}) %collective-permute-start.31) | collective-permute-done | bytes 131104 | tf_op jit(solution)/shard_map/ppermute | solution.py:238
  160.4 7.7 %collective-permute-start.32 = (bf16[128,512]{1,0:T(8,128)(2,1)S(1)}, bf16[128,512]{1,0:T(8,128)(2,1)S(1)}, u32[]{:S(2)}, u32[]{:S(2)}) collective-permute-start(bf16[128,512]{1,0:T(8,128)(2,1)S(1)} %get-tuple-element.25), channel_id=1, source_target_pairs={{0,4},{2,6},{4,8},{6,10},{1,5},{3,7},{5,9},{7,11},{16,20},{18,22},... | collective-permute-start | bytes 393224 | tf_op jit(solution)/shard_map/ppermute | solution.py:238
  170.6 4.4 %collective-permute-start.42 = (bf16[128,512]{1,0:T(8,128)(2,1)S(1)}, bf16[128,512]{1,0:T(8,128)(2,1)S(1)}, u32[]{:S(2)}, u32[]{:S(2)}) collective-permute-start(bf16[128,512]{1,0:T(8,128)(2,1)S(1)} %get-tuple-element.29), channel_id=1, source_target_pairs={{0,4},{2,6},{4,8},{6,10},{1,5},{3,7},{5,9},{7,11},{16,20},{18,22},... | collective-permute-start | bytes 393224 | tf_op jit(solution)/shard_map/ppermute | solution.py:238
  176.8 4.6 %collective-permute-start.33 = (bf16[128,512]{1,0:T(8,128)(2,1)S(1)}, bf16[128,512]{1,0:T(8,128)(2,1)S(1)}, u32[]{:S(2)}, u32[]{:S(2)}) collective-permute-start(bf16[128,512]{1,0:T(8,128)(2,1)S(1)} %get-tuple-element.23), channel_id=1, source_target_pairs={{0,4},{2,6},{4,8},{6,10},{8,12},{10,14},{1,5},{3,7},{5,9},{7,11},{... | collective-permute-start | bytes 393224 | tf_op jit(solution)/shard_map/ppermute | solution.py:238
  183.4 3.9 %collective-permute-start.43 = (bf16[128,512]{1,0:T(8,128)(2,1)S(1)}, bf16[128,512]{1,0:T(8,128)(2,1)S(1)}, u32[]{:S(2)}, u32[]{:S(2)}) collective-permute-start(bf16[128,512]{1,0:T(8,128)(2,1)S(1)} %get-tuple-element.27), channel_id=1, source_target_pairs={{0,4},{2,6},{4,8},{6,10},{8,12},{10,14},{1,5},{3,7},{5,9},{7,11},{... | collective-permute-start | bytes 393224 | tf_op jit(solution)/shard_map/ppermute | solution.py:238
  190.3 3.9 %collective-permute-done.46 = bf16[128,512]{1,0:T(8,128)(2,1)S(1)} collective-permute-done((bf16[128,512]{1,0:T(8,128)(2,1)S(1)}, bf16[128,512]{1,0:T(8,128)(2,1)S(1)}, u32[]{:S(2)}, u32[]{:S(2)}) %collective-permute-start.46) | collective-permute-done | bytes 131104 | tf_op jit(solution)/shard_map/ppermute | solution.py:238
  (114 shorter events, 52.6 us)
Async XLA Ops:
  0.6 12.4 %collective-permute-start.17 = (bf16[128,1024]{1,0:T(8,128)(2,1)}, bf16[128,1024]{1,0:T(8,128)(2,1)S(1)}, u32[]{:S(2)}, u32[]{:S(2)}) collective-permute-start(bf16[128,1024]{1,0:T(8,128)(2,1)} %refs_0_.3), channel_id=1, source_target_pairs={{0,4},{2,6},{4,8},{6,10},{8,12},{10,14},{1,5},{3,7},{5,9},{7,11},{... | collective-permute-start | bytes 786440 | tf_op jit(solution)/shard_map/ppermute | solution.py:179
  6.5 19.0 %collective-permute-start.5 = (bf16[128,1024]{1,0:T(8,128)(2,1)}, bf16[128,1024]{1,0:T(8,128)(2,1)S(1)}, u32[]{:S(2)}, u32[]{:S(2)}) collective-permute-start(bf16[128,1024]{1,0:T(8,128)(2,1)} %refs_0_.2), channel_id=1, source_target_pairs={{0,4},{2,6},{4,8},{6,10},{8,12},{10,14},{1,5},{3,7},{5,9},{7,11},{... | collective-permute-start | bytes 786440 | tf_op jit(solution)/shard_map/ppermute | solution.py:179
  10.0 19.5 %collective-permute-start.6 = (bf16[128,1024]{1,0:T(8,128)(2,1)}, bf16[128,1024]{1,0:T(8,128)(2,1)S(1)}, u32[]{:S(2)}, u32[]{:S(2)}) collective-permute-start(bf16[128,1024]{1,0:T(8,128)(2,1)} %refs_0_.2), channel_id=1, source_target_pairs={{4,0},{6,2},{8,4},{10,6},{12,8},{14,10},{5,1},{7,3},{9,5},{11,7},{... | collective-permute-start | bytes 786440 | tf_op jit(solution)/shard_map/ppermute | solution.py:179
  13.1 18.4 %collective-permute-start.20 = (bf16[128,1024]{1,0:T(8,128)(2,1)S(1)}, bf16[128,1024]{1,0:T(8,128)(2,1)S(1)}, u32[]{:S(2)}, u32[]{:S(2)}) collective-permute-start(bf16[128,1024]{1,0:T(8,128)(2,1)S(1)} %collective-permute-done.17), channel_id=1, source_target_pairs={{4,8},{6,10},{8,12},{10,14},{5,9},{7,11},{9,13},{11,15},{20,24},{2... | collective-permute-start | bytes 786440 | tf_op jit(solution)/shard_map/ppermute | solution.py:179
  16.6 15.6 %collective-permute-start.21 = (bf16[128,1024]{1,0:T(8,128)(2,1)S(1)}, bf16[128,1024]{1,0:T(8,128)(2,1)S(1)}, u32[]{:S(2)}, u32[]{:S(2)}) collective-permute-start(bf16[128,1024]{1,0:T(8,128)(2,1)S(1)} %collective-permute-done.18), channel_id=1, source_target_pairs={{4,0},{6,2},{8,4},{10,6},{5,1},{7,3},{9,5},{11,7},{20,16},{22,18},... | collective-permute-start | bytes 786440 | tf_op jit(solution)/shard_map/ppermute | solution.py:179
  25.5 15.9 %collective-permute-start.8 = (bf16[128,1024]{1,0:T(8,128)(2,1)S(1)}, bf16[128,1024]{1,0:T(8,128)(2,1)S(1)}, u32[]{:S(2)}, u32[]{:S(2)}) collective-permute-start(bf16[128,1024]{1,0:T(8,128)(2,1)S(1)} %collective-permute-done.5), channel_id=1, source_target_pairs={{4,8},{6,10},{8,12},{10,14},{5,9},{7,11},{9,13},{11,15},{20,24},{2... | collective-permute-start | bytes 786440 | tf_op jit(solution)/shard_map/ppermute | solution.py:179
  29.5 12.5 %collective-permute-start.9 = (bf16[128,1024]{1,0:T(8,128)(2,1)S(1)}, bf16[128,1024]{1,0:T(8,128)(2,1)S(1)}, u32[]{:S(2)}, u32[]{:S(2)}) collective-permute-start(bf16[128,1024]{1,0:T(8,128)(2,1)S(1)} %collective-permute-done.6), channel_id=1, source_target_pairs={{4,0},{6,2},{8,4},{10,6},{5,1},{7,3},{9,5},{11,7},{20,16},{22,18},... | collective-permute-start | bytes 786440 | tf_op jit(solution)/shard_map/ppermute | solution.py:179
  32.1 14.7 %collective-permute-start.24 = (bf16[128,1024]{1,0:T(8,128)(2,1)S(1)}, bf16[128,1024]{1,0:T(8,128)(2,1)S(1)}, u32[]{:S(2)}, u32[]{:S(2)}) collective-permute-start(bf16[128,1024]{1,0:T(8,128)(2,1)S(1)} %collective-permute-done.21), channel_id=1, source_target_pairs={{4,0},{6,2},{5,1},{7,3},{20,16},{22,18},{21,17},{23,19}} | collective-permute-start | bytes 786440 | tf_op jit(solution)/shard_map/ppermute | solution.py:179
  39.2 43.3 %collective-permute-start.4 = (bf16[128,1024]{1,0:T(8,128)(2,1)}, bf16[128,1024]{1,0:T(8,128)(2,1)S(1)}, u32[]{:S(2)}, u32[]{:S(2)}) collective-permute-start(bf16[128,1024]{1,0:T(8,128)(2,1)} %refs_0_.2), channel_id=1, source_target_pairs={{0,2},{2,0},{4,6},{6,4},{8,10},{10,8},{12,14},{14,12},{1,3},{3,1},... | collective-permute-start | bytes 786440 | tf_op jit(solution)/shard_map/ppermute | solution.py:183
  41.4 12.8 %collective-permute-start.16 = (bf16[128,1024]{1,0:T(8,128)(2,1)}, bf16[128,1024]{1,0:T(8,128)(2,1)S(1)}, u32[]{:S(2)}, u32[]{:S(2)}) collective-permute-start(bf16[128,1024]{1,0:T(8,128)(2,1)} %refs_0_.3), channel_id=1, source_target_pairs={{0,2},{2,0},{4,6},{6,4},{8,10},{10,8},{12,14},{14,12},{1,3},{3,1},... | collective-permute-start | bytes 786440 | tf_op jit(solution)/shard_map/ppermute | solution.py:183
  47.0 12.9 %collective-permute-start.25 = (bf16[128,1024]{1,0:T(8,128)(2,1)S(1)}, bf16[128,1024]{1,0:T(8,128)(2,1)S(1)}, u32[]{:S(2)}, u32[]{:S(2)}) collective-permute-start(bf16[128,1024]{1,0:T(8,128)(2,1)S(1)} %get-tuple-element.39.refs_6_), channel_id=1, source_target_pairs={{0,2},{2,0},{4,6},{6,4},{8,10},{10,8},{12,14},{14,12},{1,3},{3,1},... | collective-permute-start | bytes 786440 | tf_op jit(solution)/shard_map/ppermute | solution.py:183
  48.6 16.9 %collective-permute-start.22 = (bf16[128,1024]{1,0:T(8,128)(2,1)S(1)}, bf16[128,1024]{1,0:T(8,128)(2,1)S(1)}, u32[]{:S(2)}, u32[]{:S(2)}) collective-permute-start(bf16[128,1024]{1,0:T(8,128)(2,1)S(1)} %get-tuple-element.40.refs_4_), channel_id=1, source_target_pairs={{0,2},{2,0},{4,6},{6,4},{8,10},{10,8},{12,14},{14,12},{1,3},{3,1},... | collective-permute-start | bytes 786440 | tf_op jit(solution)/shard_map/ppermute | solution.py:183
  50.7 20.3 %collective-permute-start.19 = (bf16[128,1024]{1,0:T(8,128)(2,1)S(1)}, bf16[128,1024]{1,0:T(8,128)(2,1)S(1)}, u32[]{:S(2)}, u32[]{:S(2)}) collective-permute-start(bf16[128,1024]{1,0:T(8,128)(2,1)S(1)} %get-tuple-element.41.refs_2_), channel_id=1, source_target_pairs={{0,2},{2,0},{4,6},{6,4},{8,10},{10,8},{12,14},{14,12},{1,3},{3,1},... | collective-permute-start | bytes 786440 | tf_op jit(solution)/shard_map/ppermute | solution.py:183
  54.2 28.3 %collective-permute-start.13 = (bf16[128,1024]{1,0:T(8,128)(2,1)S(1)}, bf16[128,1024]{1,0:T(8,128)(2,1)S(1)}, u32[]{:S(2)}, u32[]{:S(2)}) collective-permute-start(bf16[128,1024]{1,0:T(8,128)(2,1)S(1)} %get-tuple-element.42.refs_6_), channel_id=1, source_target_pairs={{0,2},{2,0},{4,6},{6,4},{8,10},{10,8},{12,14},{14,12},{1,3},{3,1},... | collective-permute-start | bytes 786440 | tf_op jit(solution)/shard_map/ppermute | solution.py:183
  59.8 22.7 %collective-permute-start.10 = (bf16[128,1024]{1,0:T(8,128)(2,1)S(1)}, bf16[128,1024]{1,0:T(8,128)(2,1)S(1)}, u32[]{:S(2)}, u32[]{:S(2)}) collective-permute-start(bf16[128,1024]{1,0:T(8,128)(2,1)S(1)} %get-tuple-element.43.refs_4_), channel_id=1, source_target_pairs={{0,2},{2,0},{4,6},{6,4},{8,10},{10,8},{12,14},{14,12},{1,3},{3,1},... | collective-permute-start | bytes 786440 | tf_op jit(solution)/shard_map/ppermute | solution.py:183
  65.5 19.1 %collective-permute-start.7 = (bf16[128,1024]{1,0:T(8,128)(2,1)S(1)}, bf16[128,1024]{1,0:T(8,128)(2,1)S(1)}, u32[]{:S(2)}, u32[]{:S(2)}) collective-permute-start(bf16[128,1024]{1,0:T(8,128)(2,1)S(1)} %get-tuple-element.44.refs_2_), channel_id=1, source_target_pairs={{0,2},{2,0},{4,6},{6,4},{8,10},{10,8},{12,14},{14,12},{1,3},{3,1},... | collective-permute-start | bytes 786440 | tf_op jit(solution)/shard_map/ppermute | solution.py:183
  82.4 17.7 %collective-permute-start.26 = (f32[16,96,384]{2,1,0:T(8,128)S(1)}, f32[16,96,384]{2,1,0:T(8,128)S(1)}, u32[]{:S(2)}, u32[]{:S(2)}) collective-permute-start(f32[16,96,384]{2,1,0:T(8,128)S(1)} %down.1.raw_own), channel_id=1, source_target_pairs={{0,1},{1,0},{2,3},{3,2},{4,5},{5,4},{6,7},{7,6},{8,9},{9,8},{10,11... | collective-permute-start | bytes 7077896 | tf_op jit(solution)/shard_map/ppermute | solution.py:187
  122.1 65.3 %collective-permute-start.27 = (bf16[128,512]{1,0:T(8,128)(2,1)S(1)}, bf16[128,512]{1,0:T(8,128)(2,1)S(1)}, u32[]{:S(2)}, u32[]{:S(2)}) collective-permute-start(bf16[128,512]{1,0:T(8,128)(2,1)S(1)} %get-tuple-element.31), channel_id=1, source_target_pairs={{0,2},{2,0},{4,6},{6,4},{8,10},{10,8},{12,14},{14,12},{1,3},{3,1},... | collective-permute-start | bytes 393224 | tf_op jit(solution)/shard_map/ppermute | solution.py:183
  123.6 27.1 %collective-permute-start.30 = (bf16[128,512]{1,0:T(8,128)(2,1)S(1)}, bf16[128,512]{1,0:T(8,128)(2,1)S(1)}, u32[]{:S(2)}, u32[]{:S(2)}) collective-permute-start(bf16[128,512]{1,0:T(8,128)(2,1)S(1)} %get-tuple-element.32), channel_id=1, source_target_pairs={{0,2},{2,0},{4,6},{6,4},{8,10},{10,8},{12,14},{14,12},{1,3},{3,1},... | collective-permute-start | bytes 393224 | tf_op jit(solution)/shard_map/ppermute | solution.py:183
  124.2 45.3 %collective-permute-start.29 = (bf16[128,512]{1,0:T(8,128)(2,1)S(1)}, bf16[128,512]{1,0:T(8,128)(2,1)S(1)}, u32[]{:S(2)}, u32[]{:S(2)}) collective-permute-start(bf16[128,512]{1,0:T(8,128)(2,1)S(1)} %get-tuple-element.33), channel_id=1, source_target_pairs={{0,2},{2,0},{4,6},{6,4},{8,10},{10,8},{12,14},{14,12},{1,3},{3,1},... | collective-permute-start | bytes 393224 | tf_op jit(solution)/shard_map/ppermute | solution.py:183
  125.7 27.2 %collective-permute-start.28 = (bf16[128,512]{1,0:T(8,128)(2,1)S(1)}, bf16[128,512]{1,0:T(8,128)(2,1)S(1)}, u32[]{:S(2)}, u32[]{:S(2)}) collective-permute-start(bf16[128,512]{1,0:T(8,128)(2,1)S(1)} %get-tuple-element.34), channel_id=1, source_target_pairs={{0,2},{2,0},{4,6},{6,4},{8,10},{10,8},{12,14},{14,12},{1,3},{3,1},... | collective-permute-start | bytes 393224 | tf_op jit(solution)/shard_map/ppermute | solution.py:183
  138.1 13.3 %collective-permute-start.40 = (bf16[128,512]{1,0:T(8,128)(2,1)S(1)}, bf16[128,512]{1,0:T(8,128)(2,1)S(1)}, u32[]{:S(2)}, u32[]{:S(2)}) collective-permute-start(bf16[128,512]{1,0:T(8,128)(2,1)S(1)} %get-tuple-element.36), channel_id=1, source_target_pairs={{0,2},{2,0},{4,6},{6,4},{8,10},{10,8},{12,14},{14,12},{1,3},{3,1},... | collective-permute-start | bytes 393224 | tf_op jit(solution)/shard_map/ppermute | solution.py:183
  159.8 29.6 %collective-permute-start.37 = (bf16[128,512]{1,0:T(8,128)(2,1)S(1)}, bf16[128,512]{1,0:T(8,128)(2,1)S(1)}, u32[]{:S(2)}, u32[]{:S(2)}) collective-permute-start(bf16[128,512]{1,0:T(8,128)(2,1)S(1)} %get-tuple-element.35), channel_id=1, source_target_pairs={{0,2},{2,0},{4,6},{6,4},{8,10},{10,8},{12,14},{14,12},{1,3},{3,1},... | collective-permute-start | bytes 393224 | tf_op jit(solution)/shard_map/ppermute | solution.py:183
  176.8 12.5 %collective-permute-start.33 = (bf16[128,512]{1,0:T(8,128)(2,1)S(1)}, bf16[128,512]{1,0:T(8,128)(2,1)S(1)}, u32[]{:S(2)}, u32[]{:S(2)}) collective-permute-start(bf16[128,512]{1,0:T(8,128)(2,1)S(1)} %get-tuple-element.23), channel_id=1, source_target_pairs={{0,4},{2,6},{4,8},{6,10},{8,12},{10,14},{1,5},{3,7},{5,9},{7,11},{... | collective-permute-start | bytes 393224 | tf_op jit(solution)/shard_map/ppermute | solution.py:238
  (29 other events, 253.7 us)

commit v2 on v0

--- a/solution.py
+++ b/solution.py
@@ -1,6 +1,10 @@
+import functools
+
 import jax
 import jax.numpy as jnp
 from jax import lax
+from jax.experimental import pallas as pl
+from jax.experimental.pallas import tpu as pltpu
 from jax.sharding import PartitionSpec as P
 
 CAP = 6
@@ -66,7 +70,7 @@
     return (row_grad, grad_gate_pre, grad_up_pre)
 
 
-def body(tokens, out_grad, route_gates, expert_ids, w_gate, w_up, w_down):
+def exchange_body(tokens, out_grad, route_gates, expert_ids, w_gate, w_up, w_down):
     ep_count = lax.axis_size("ep")
     local_count = w_gate.shape[0]
     experts = local_count * ep_count
@@ -137,6 +141,641 @@
     return (grad_input, grad_gate_w, grad_up_w)
 
 
+ORDERS = ((0, 1, 2, 3), (1, 0, 2, 3), (2, 3, 1, 0), (3, 2, 1, 0))
+LINES = len(ORDERS)
+PARTS = 2
+OUTER = ((0, 1), (1, 0), (2, 3), (3, 2))
+INNER = ((1, 2), (2, 1))
+TO_END = ((1, 0), (2, 3))
+FROM_END = ((0, 1), (3, 2))
+
+
+def along_line(value, moves):
+    pairs = [(2 * a + side, 2 * b + side) for a, b in moves for side in range(2)]
+    return lax.ppermute(value, "ep", pairs)
+
+
+def across_pair(value):
+    return lax.ppermute(value, "ep", [(i, i ^ 1) for i in range(2 * LINES)])
+
+
+def across_cores(value):
+    return lax.ppermute(value, "dp", [(0, 1), (1, 0)])
+
+
+def tie(values, *others):
+    values = list(values)
+    return list(lax.optimization_barrier(tuple(values) + tuple(others))[: len(values)])
+
+
+def gather_rows(rows, info, at_end, meanwhile):
+    def widen(info, bits):
+        came = [
+            lax.ppermute(info, "ep", [(i, i ^ bit) for i in range(2 * LINES)]) for bit in bits
+        ]
+        return functools.reduce(jnp.add, came, info)
+
+    outer, inner, other = along_line(rows, OUTER), along_line(rows, INNER), across_pair(rows)
+    info = widen(info + across_cores(info), [1])
+    outer, inner, other, info = tie((outer, inner, other, info))
+    pieces = [rows, other]
+
+    info = widen(info, [2, 4, 6])
+    outer, inner, info = tie((outer, inner, info))
+    second, third = along_line(inner, TO_END), along_line(outer, INNER)
+    other = across_pair(outer)
+    done = meanwhile(0, info, pieces)
+    second, third, other = tie((second, third, other), *done)
+    pieces += [outer, other]
+
+    middle = jnp.where(at_end, second, inner)
+    last, other = along_line(third, TO_END), across_pair(middle)
+    done = meanwhile(1, info, pieces)
+    last, other = tie((last, other), *done)
+    pieces += [middle, other]
+
+    meanwhile(2, info, [last, other])
+    for part in range(2):
+        far = jnp.where(at_end, last[part], third[part])
+        pieces += [far, across_pair(far)]
+        last, third = tie((last, third))
+    return pieces
+
+
+def scatter_sums(partial, meanwhile):
+    f32, bf16 = jnp.float32, jnp.bfloat16
+
+    def own_side(m, other):
+        return partial[2 * m].astype(f32) + other.astype(f32)
+
+    other = across_pair(partial[7])
+    (other,) = meanwhile(0, [other])
+    far = own_side(3, other)
+    outward, other = along_line(far.astype(bf16), FROM_END), across_pair(partial[5])
+    outward, other = meanwhile(1, [outward, other])
+    middle = own_side(2, other)
+    crossed = along_line((far + outward.astype(f32)).astype(bf16), INNER)
+    outward, other = along_line(middle.astype(bf16), FROM_END), across_pair(partial[3])
+    crossed, outward, other = meanwhile(2, [crossed, outward, other])
+    near = own_side(1, other) + crossed.astype(f32)
+    inner = along_line((middle + outward.astype(f32)).astype(bf16), INNER)
+    outer, other = along_line(near.astype(bf16), OUTER), across_pair(partial[1])
+    inner, outer, other = meanwhile(3, [inner, outer, other])
+    total = own_side(0, other) + outer.astype(f32) + inner.astype(f32)
+    return total.astype(bf16)
+
+
+def route_kernel(order_ref, base_ref, info_ref, slot_ref, gate_ref, *, top_count, block_rows):
+    local_count = slot_ref.shape[0]
+    chunk = info_ref.shape[2]
+    row = lax.broadcasted_iota(jnp.int32, (chunk, chunk), 0)
+    column = lax.broadcasted_iota(jnp.int32, (chunk, chunk), 1)
+    before = ((row < column) & (row // block_rows == column // block_rows)).astype(jnp.bfloat16)
+    lane = lax.broadcasted_iota(jnp.int32, (local_count, chunk), 1)
+    expert = (base_ref[0] + lax.broadcasted_iota(jnp.int32, (local_count, chunk), 0)).astype(
+        jnp.float32
+    )
+    for piece in range(info_ref.shape[0]):
+        info = info_ref[order_ref[piece]].astype(jnp.float32)
+        named = jnp.zeros((local_count, chunk), jnp.float32)
+        gate = jnp.zeros((local_count, chunk), jnp.float32)
+        for k in range(top_count):
+            match = info[k : k + 1, :] == expert
+            named = jnp.where(match, 1.0, named)
+            gate = jnp.where(match, info[top_count + k : top_count + k + 1, :], gate)
+        rank = jnp.dot(
+            named.astype(jnp.bfloat16), before, preferred_element_type=jnp.float32
+        ).astype(jnp.int32)
+        block = piece * (chunk // block_rows) + lane // block_rows
+        columns = pl.ds(piece * chunk, chunk)
+        slot_ref[:, columns] = jnp.where(named > 0.5, block * CAP + rank, -1)
+        gate_ref[:, columns] = gate
+
+
+def start_all(copies):
+    for copy in copies:
+        copy.start()
+    return copies
+
+
+def piece_copies(sources, rows_ref, sems):
+    chunk = rows_ref.shape[0] // len(sources)
+    return start_all(
+        [
+            pltpu.make_async_copy(source, rows_ref.at[pl.ds(m * chunk, chunk)], sems.at[m])
+            for m, source in enumerate(sources)
+        ]
+    )
+
+
+def group_copies(source, target, sems):
+    count, number = target.shape[0], sems.shape[0]
+    group = count // number
+    return start_all(
+        [
+            pltpu.make_async_copy(
+                source.at[pl.ds(i * group, group)], target.at[pl.ds(i * group, group)], sems.at[i]
+            )
+            for i in range(number)
+        ]
+    )
+
+
+def hot_part(slot_ref, experts, part, slots):
+    tokens = slot_ref.shape[1] // PARTS
+    count = slots // PARTS
+    columns = slice(part * tokens, (part + 1) * tokens)
+    row = lax.broadcasted_iota(jnp.int32, (count, tokens), 0) + part * count
+    return [row == slot_ref[e : e + 1, columns] for e in experts]
+
+
+def dispatch(part, slot_ref, rows_ref, x_ref):
+    local_count = slot_ref.shape[0]
+    count = 2 * LINES * 2 * CAP // PARTS
+    first_slot = part * count if x_ref.shape[1] > count else 0
+    group = min(8, local_count)
+    for first in range(0, local_count, group):
+        experts = range(first, first + group)
+        hot = jnp.concatenate(
+            [h.astype(jnp.bfloat16) for h in hot_part(slot_ref, experts, part, count * PARTS)]
+        )
+        found = jnp.dot(hot, rows_ref[...], preferred_element_type=jnp.float32)
+        found = found.astype(jnp.bfloat16)
+        for i, e in enumerate(experts):
+            x_ref[e, first_slot : first_slot + count] = found[i * count : (i + 1) * count]
+
+
+def turn_kernel(w_ref, out_ref, w_here, out_here, w_sems, out_sems):
+    weights = group_copies(w_ref, w_here, w_sems)
+    group = w_here.shape[0] // len(weights)
+    copies = []
+    for i, weight in enumerate(weights):
+        weight.wait()
+        for e in range(i * group, (i + 1) * group):
+            out_here[e] = w_here[e].T
+        span = pl.ds(i * group, group)
+        copies += start_all(
+            [pltpu.make_async_copy(out_here.at[span], out_ref.at[span], out_sems.at[i])]
+        )
+    for copy in copies:
+        copy.wait()
+
+
+def first_kernel(slot_ref, gates_ref, *refs):
+    pieces, (x_ref, grad_x_ref, slot_gates_ref) = refs[:4], refs[4:7]
+    tokens_here, grads_here, token_sems, grad_sems = refs[7:]
+    tokens = piece_copies([piece.at[0] for piece in pieces], tokens_here, token_sems)
+    grads = piece_copies([piece.at[1] for piece in pieces], grads_here, grad_sems)
+    for arrivals, rows_ref, target in (
+        (tokens, tokens_here, x_ref),
+        (grads, grads_here, grad_x_ref),
+    ):
+        for copy in arrivals:
+            copy.wait()
+        dispatch(0, slot_ref, rows_ref, target)
+    local_count, slots, lanes = slot_gates_ref.shape
+    tokens, count = slot_ref.shape[1] // PARTS, slots // PARTS
+    for e in range(local_count):
+        for part in range(PARTS):
+            gates = gates_ref[e : e + 1, part * tokens : (part + 1) * tokens]
+            gate = jnp.where(hot_part(slot_ref, [e], part, slots)[0], gates, 0.0)
+            slot_gates_ref[e, part * count : (part + 1) * count] = jnp.broadcast_to(
+                jnp.sum(gate, axis=1, keepdims=True), (count, lanes)
+            )
+
+
+def finish_slots(index, slot_ref, pieces, first_ref, rows_ref, x_here, piece_sems, first_sem):
+    sources = [piece.at[index] if len(piece.shape) == 3 else piece for piece in pieces]
+    arrivals = piece_copies(sources, rows_ref, piece_sems)
+    count = first_ref.shape[1]
+    first = pltpu.make_async_copy(first_ref, x_here.at[:, pl.ds(0, count)], first_sem)
+    first.start()
+
+    def finish():
+        for copy in arrivals:
+            copy.wait()
+        dispatch(1, slot_ref, rows_ref, x_here)
+        first.wait()
+
+    return finish
+
+
+def multiply(x_ref, w_ref, here, out_ref, out_sems, weights=None, side=0):
+    groups = out_sems.shape[0]
+    group = x_ref.shape[0] // groups
+    copies = []
+    for i in range(groups):
+        if weights is not None:
+            weights[i].wait()
+        for e in range(i * group, (i + 1) * group):
+            here[e] = lax.dot_general(
+                x_ref[e],
+                w_ref[e],
+                (((1,), (side,)), ((), ())),
+                preferred_element_type=jnp.float32,
+            )
+        span = pl.ds(i * group, group)
+        copies += start_all(
+            [pltpu.make_async_copy(here.at[span], out_ref.at[span], out_sems.at[i])]
+        )
+    return copies
+
+
+def load_kernel(w_ref, out_ref, sems):
+    for copy in group_copies(w_ref, out_ref, sems):
+        copy.wait()
+
+
+def pre_kernel(slot_ref, *refs):
+    pieces, refs = refs[:4], refs[4:]
+    first_ref, gate_w, up_w, x_ref, gate_ref, up_ref = refs[:6]
+    rows_here, x_here, up_w_here, gate_here, up_here = refs[6:11]
+    piece_sems, first_sem, up_w_sems, x_sem, gate_sems, up_sems = refs[11:]
+    finish = finish_slots(
+        0, slot_ref, pieces, first_ref, rows_here, x_here, piece_sems, first_sem
+    )
+    up_ws = group_copies(up_w, up_w_here, up_w_sems)
+    finish()
+    copies = start_all([pltpu.make_async_copy(x_here, x_ref, x_sem)])
+    copies += multiply(x_here, gate_w, gate_here, gate_ref, gate_sems)
+    copies += multiply(x_here, up_w_here, up_here, up_ref, up_sems, up_ws)
+    for copy in copies:
+        copy.wait()
+
+
+def down_kernel(slot_ref, *refs):
+    pieces, refs = refs[:4], refs[4:]
+    first_ref, down_w, raw_ref = refs[:3]
+    rows_here, x_here, w_here, here, piece_sems, first_sem, w_sems, out_sems = refs[3:]
+    finish = finish_slots(
+        1, slot_ref, pieces, first_ref, rows_here, x_here, piece_sems, first_sem
+    )
+    weights = group_copies(down_w, w_here, w_sems)
+    finish()
+    for copy in multiply(x_here, w_here, here, raw_ref, out_sems, weights, 1):
+        copy.wait()
+
+
+def keep_row(row, e, rows_ref):
+    count = row.shape[0] // PARTS
+    for part in range(PARTS):
+        rows_ref[part, e * count : (e + 1) * count] = row[part * count : (part + 1) * count]
+
+
+def combine(slot_ref, experts, rows_ref, sum_ref, outs, slots):
+    local_count = slot_ref.shape[0]
+    tokens, count = slot_ref.shape[1] // PARTS, slots // PARTS
+    copies = []
+    for part in reversed(range(PARTS)):
+        hot = jnp.concatenate(
+            [h.astype(jnp.bfloat16) for h in hot_part(slot_ref, experts, part, slots)]
+        )
+        total = lax.dot_general(
+            hot,
+            rows_ref[part, experts[0] * count : (experts[-1] + 1) * count],
+            (((0,), (0,)), ((), ())),
+            preferred_element_type=jnp.float32,
+        )
+        place = slice(part * tokens, (part + 1) * tokens)
+        if experts[0] > 0:
+            total += sum_ref[place]
+        if experts[-1] < local_count - 1:
+            sum_ref[place] = total
+        else:
+            each = len(outs) // PARTS
+            for i, (here, out, sem) in enumerate(outs[part * each : (part + 1) * each]):
+                rows = tokens // each
+                here[...] = total[i * rows : (i + 1) * rows].astype(jnp.bfloat16)
+                copies += start_all([pltpu.make_async_copy(here, out, sem)])
+    return copies
+
+
+def load_half_kernel(gate_w, up_w, gate_out, up_out, gate_sems, up_sems):
+    half = pl.ds(0, gate_out.shape[0])
+    copies = group_copies(gate_w.at[half], gate_out, gate_sems)
+    copies += group_copies(up_w.at[half], up_out, up_sems)
+    for copy in copies:
+        copy.wait()
+
+
+def rows_kernel(slot_ref, *refs):
+    slot_gates_ref, sources, refs = refs[0], refs[1:7], refs[7:]
+    gate_first, up_first, gate_w, up_w, grads_ref = refs[:5]
+    out_refs, refs = refs[5 : 5 + 2 * LINES], refs[5 + 2 * LINES :]
+    inputs_here, gate_here, up_here, grads_here, rows_ref, sum_ref, outs_here = refs[:7]
+    input_sems, gate_sems, up_sems, grad_sems, out_sems = refs[7:]
+    local_count, slots, hidden = inputs_here.shape[1:]
+    outs = [(outs_here.at[m], out, out_sems.at[m]) for m, out in enumerate(out_refs)]
+    copies = []
+    groups = input_sems.shape[1]
+    group = local_count // groups
+    half = gate_first.shape[0]
+    rest = pl.ds(half, local_count - half)
+    arrivals = []
+    for i in range(groups):
+        here = pl.ds(i * group, group)
+        arrivals.append(
+            start_all(
+                [
+                    pltpu.make_async_copy(
+                        source.at[here], inputs_here.at[j, here], input_sems.at[j, i]
+                    )
+                    for j, source in enumerate(sources)
+                ]
+            )
+        )
+    gate_ws = group_copies(gate_w.at[rest], gate_here, gate_sems)
+    up_ws = group_copies(up_w.at[rest], up_here, up_sems)
+    for i in range(groups):
+        for copy in arrivals[i]:
+            copy.wait()
+        for e in range(i * group, (i + 1) * group):
+            pre_gate = inputs_here[0, e] + inputs_here[1, e]
+            pre_up = inputs_here[2, e] + inputs_here[3, e]
+            raw = inputs_here[4, e] + inputs_here[5, e]
+            sigmoid = jax.nn.sigmoid(pre_gate)
+            scaled = slot_gates_ref[e, :, :1] * raw * sigmoid
+            grad_gate = (scaled * pre_up * (1.0 + pre_gate * (1.0 - sigmoid))).astype(jnp.bfloat16)
+            grad_up = (scaled * pre_gate).astype(jnp.bfloat16)
+            grads_here[e, :, :hidden] = grad_gate
+            grads_here[e, :, hidden:] = grad_up
+            if e < half:
+                gate_e, up_e = gate_first[e], up_first[e]
+            else:
+                span = half // len(gate_ws)
+                if (e - half) % span == 0:
+                    gate_ws[(e - half) // span].wait()
+                    up_ws[(e - half) // span].wait()
+                gate_e, up_e = gate_here[e - half], up_here[e - half]
+            row = jnp.dot(grad_gate, gate_e, preferred_element_type=jnp.float32)
+            row += lax.dot_general(
+                grad_up, up_e, (((1,), (1,)), ((), ())), preferred_element_type=jnp.float32
+            )
+            keep_row(row.astype(jnp.bfloat16), e, rows_ref)
+        if (i + 1) % (groups // 2) == 0:
+            last = (i + 1) * group
+            experts = range(last - local_count // 2, last)
+            here = pl.ds(experts[0], len(experts))
+            copies += start_all(
+                [
+                    pltpu.make_async_copy(
+                        grads_here.at[here], grads_ref.at[here], grad_sems.at[i // (groups // 2)]
+                    )
+                ]
+            )
+            copies += combine(slot_ref, experts, rows_ref, sum_ref, outs, slots)
+    for copy in copies:
+        copy.wait()
+
+
+def weight_kernel(x_ref, grads_ref, *refs):
+    gate_out_ref, up_out_ref = refs[-2:]
+    hidden = gate_out_ref.shape[-1]
+    for i in range(x_ref.shape[0]):
+        found = lax.dot_general(
+            x_ref[i], grads_ref[i], (((0,), (0,)), ((), ())), preferred_element_type=jnp.float32
+        ).astype(jnp.bfloat16)
+        gate_out_ref[i] = found[:, :hidden]
+        up_out_ref[i] = found[:, hidden:]
+
+
+def in_hbm(value):
+    return pltpu.with_memory_space_constraint(value, pltpu.HBM)
+
+
+def in_vmem(value):
+    return pltpu.with_memory_space_constraint(value, pltpu.VMEM)
+
+
+def params(mib):
+    return pltpu.CompilerParams(vmem_limit_bytes=mib * 1024 * 1024)
+
+
+def cost(flops, moved):
+    return pl.CostEstimate(flops=int(flops), bytes_accessed=int(moved), transcendentals=0)
+
+
+def gather_body(tokens, out_grad, route_gates, expert_ids, w_gate, w_up, w_down):
+    ep_count = 2 * LINES
+    local_count, half_width, hidden = w_gate.shape
+    block_rows, top_count = expert_ids.shape
+    chunk = 2 * block_rows
+    token_count = ep_count * chunk
+    slots = 2 * ep_count * CAP
+    part_slots, part_tokens = slots // PARTS, token_count // PARTS
+    place = lax.axis_index("ep")
+    here, side = place // 2, place % 2
+    at_end = (here == 0) | (here == LINES - 1)
+    bf16, f32 = jnp.bfloat16, jnp.float32
+    memory = pl.BlockSpec(memory_space=pl.ANY)
+    smem = pl.BlockSpec(memory_space=pltpu.SMEM)
+    vmem = pl.BlockSpec(memory_space=pltpu.VMEM)
+    copies = pltpu.SemaphoreType.DMA
+
+    own_info = jnp.concatenate([expert_ids.astype(bf16), route_gates], axis=1).T
+    info = jnp.zeros((ep_count, 2 * top_count, chunk), bf16)
+    info = lax.dynamic_update_slice(
+        info, own_info[None], (place, 0, lax.axis_index("dp") * block_rows)
+    )
+    line_order = jnp.asarray(ORDERS, jnp.int32)[here]
+    order = (2 * line_order[:, None] + jnp.stack([side, 1 - side])[None, :]).reshape(-1)
+
+    weight_bytes = local_count * half_width * hidden * 2
+    matmul_flops = 2 * local_count * slots * half_width * hidden
+    hot_flops = local_count * slots * half_width * token_count
+    groups = 4
+    piece_sems, w_sems = copies((ep_count // PARTS,)), copies((groups,))
+    rows_here = pltpu.VMEM((part_tokens, half_width), bf16)
+    x_shape = jax.ShapeDtypeStruct((local_count, slots, half_width), bf16)
+    x_here = pltpu.VMEM(x_shape.shape, bf16)
+    w_here, down_here = pltpu.VMEM(w_gate.shape, bf16), pltpu.VMEM(w_down.shape, bf16)
+    pre_shape = jax.ShapeDtypeStruct((local_count, slots, hidden), f32)
+    in_hbm_shape = pltpu.HBM(pre_shape.shape, f32)
+    pre_here = pltpu.VMEM(pre_shape.shape, f32)
+    batch = 2 if local_count % 2 == 0 else 1
+
+    def batched(*shape):
+        return pl.BlockSpec((batch,) + shape, lambda e: (e, 0, 0))
+
+    def turned(weights):
+        _, rows, columns = weights.shape
+        shape = (local_count, columns, rows)
+        return pl.pallas_call(
+            turn_kernel,
+            out_shape=pltpu.HBM(shape, bf16),
+            in_specs=[memory],
+            out_specs=memory,
+            scratch_shapes=[w_here, pltpu.VMEM(shape, bf16), w_sems, w_sems],
+            compiler_params=params(26),
+            cost_estimate=cost(0, 2 * weight_bytes),
+            name="turn",
+        )(in_hbm(weights))
+
+    made = {}
+
+    def beside_gather(turn, info, pieces):
+        if turn == 0:
+            (gate_w,) = tie([w_gate], info)
+            made["gate"] = turned(gate_w)
+            return [made["gate"]]
+        if turn == 2:
+            (gate_w,) = tie([w_gate], *pieces)
+            made["loaded"] = pl.pallas_call(
+                load_kernel,
+                out_shape=pltpu.VMEM(w_gate.shape, bf16),
+                in_specs=[memory],
+                out_specs=memory,
+                scratch_shapes=[w_sems],
+                compiler_params=params(24),
+                cost_estimate=cost(0, weight_bytes),
+                name="load",
+            )(in_hbm(gate_w))
+            return []
+        made["slots"], made["gates"] = pl.pallas_call(
+            functools.partial(route_kernel, top_count=top_count, block_rows=block_rows),
+            out_shape=(
+                jax.ShapeDtypeStruct((local_count, token_count), jnp.int32),
+                jax.ShapeDtypeStruct((local_count, token_count), f32),
+            ),
+            in_specs=[smem, smem, vmem],
+            out_specs=(vmem, vmem),
+            compiler_params=params(16),
+            cost_estimate=cost(1e7, 1e6),
+            name="route",
+        )(order, (place * local_count).reshape(1), info)
+        part_shape = jax.ShapeDtypeStruct((local_count, part_slots, half_width), bf16)
+        made["x"], made["grad_x"], made["slot_gates"] = pl.pallas_call(
+            first_kernel,
+            out_shape=(
+                part_shape,
+                part_shape,
+                jax.ShapeDtypeStruct((local_count, slots, 128), f32),
+            ),
+            in_specs=[vmem] * 2 + [memory] * 4,
+            out_specs=(vmem,) * 3,
+            scratch_shapes=[rows_here, rows_here, piece_sems, piece_sems],
+            compiler_params=params(32),
+            cost_estimate=cost(hot_flops, weight_bytes / 2),
+            name="first_slots",
+        )(made["slots"], made["gates"], *pieces)
+        return [made["x"], made["grad_x"]]
+
+    pieces = gather_rows(jnp.stack([tokens, out_grad]), info, at_end, beside_gather)
+    slot_of = made["slots"]
+
+    x, gate_part, up_part = pl.pallas_call(
+        pre_kernel,
+        out_shape=(x_shape, in_hbm_shape, in_hbm_shape),
+        in_specs=[vmem] + [memory] * 5 + [vmem, memory],
+        out_specs=(memory,) * 3,
+        scratch_shapes=[rows_here, x_here, w_here, pre_here, pre_here]
+        + [piece_sems, copies, w_sems, copies, w_sems, w_sems],
+        compiler_params=params(24),
+        cost_estimate=cost(hot_flops / 2 + 2 * matmul_flops, 2.8 * weight_bytes),
+        name="pre",
+    )(
+        slot_of,
+        *pieces[4:8],
+        made["x"],
+        in_vmem(made["loaded"]),
+        in_hbm(w_up),
+    )
+    grad_pieces = tie(pieces[8:], x)
+    raw_part = pl.pallas_call(
+        down_kernel,
+        out_shape=in_hbm_shape,
+        in_specs=[vmem] + [memory] * 6,
+        out_specs=memory,
+        scratch_shapes=[rows_here, x_here, down_here, pre_here]
+        + [piece_sems, copies, w_sems, w_sems],
+        compiler_params=params(19),
+        cost_estimate=cost(hot_flops / 2 + matmul_flops, 1.4 * weight_bytes),
+        name="down",
+    )(slot_of, *pieces[4:6], *grad_pieces, made["grad_x"], in_hbm(w_down))
+    gate_other, up_other = across_cores(gate_part), across_cores(up_part)
+    raw_other = across_cores(raw_part)
+    half = local_count // 2
+    gate_half, up_half = (half, hidden, half_width), (half, half_width, hidden)
+    gate_w, up_w = tie((made["gate"], w_up), raw_part, gate_other, up_other)
+    gate_first, up_first = pl.pallas_call(
+        load_half_kernel,
+        out_shape=(pltpu.VMEM(gate_half, bf16), pltpu.VMEM(up_half, bf16)),
+        in_specs=[memory] * 2,
+        out_specs=(memory,) * 2,
+        scratch_shapes=[w_sems, w_sems],
+        compiler_params=params(40),
+        cost_estimate=cost(0, weight_bytes),
+        name="load_half",
+    )(in_hbm(gate_w), in_hbm(up_w))
+    grads, *partial = pl.pallas_call(
+        rows_kernel,
+        out_shape=(jax.ShapeDtypeStruct((local_count, slots, 2 * hidden), bf16),)
+        + (jax.ShapeDtypeStruct((chunk, half_width), bf16),) * ep_count,
+        in_specs=[vmem] * 2 + [memory] * 6 + [vmem] * 2 + [memory] * 2,
+        out_specs=(memory,) * (1 + ep_count),
+        scratch_shapes=[
+            pltpu.VMEM((6,) + pre_shape.shape, f32),
+            pltpu.VMEM(gate_half, bf16),
+            pltpu.VMEM(up_half, bf16),
+            pltpu.VMEM((local_count, slots, 2 * hidden), bf16),
+            pltpu.VMEM((PARTS, local_count * part_slots, half_width), bf16),
+            pltpu.VMEM((token_count, half_width), f32),
+            pltpu.VMEM((ep_count, chunk, half_width), bf16),
+            copies((6, 2 * groups)),
+            w_sems,
+            w_sems,
+            copies((2,)),
+            copies((ep_count,)),
+        ],
+        compiler_params=params(40),
+        cost_estimate=cost(2 * matmul_flops + hot_flops, 2 * weight_bytes),
+        name="rows",
+    )(
+        slot_of,
+        made["slot_gates"],
+        *[
+            in_hbm(value)
+            for value in (gate_part, gate_other, up_part, up_other, raw_part, raw_other)
+        ],
+        in_vmem(gate_first),
+        in_vmem(up_first),
+        in_hbm(made["gate"]),
+        in_hbm(w_up),
+    )
+
+    turns = LINES
+    group = local_count // turns
+    weight_shape = jax.ShapeDtypeStruct(w_gate.shape, bf16)
+    weight_grads = []
+
+    def block_of(first, *shape):
+        return pl.BlockSpec((1,) + shape, lambda e: (first + e, 0, 0))
+
+    def meanwhile(turn, values):
+        first = turn * group
+        operands = [x, grads]
+        operands = tie(operands, *(held or partial))
+        weight_grads[:] = pl.pallas_call(
+            weight_kernel,
+            grid=(group,),
+            out_shape=(weight_shape, weight_shape),
+            in_specs=[block_of(first, slots, half_width), block_of(first, slots, 2 * hidden)]
+            + [memory] * len(weight_grads),
+            out_specs=(block_of(first, half_width, hidden), block_of(first, half_width, hidden)),
+            input_output_aliases={2 + i: i for i in range(len(weight_grads))},
+            compiler_params=params(32),
+            cost_estimate=cost(2 * matmul_flops / turns, 2.5 * weight_bytes / turns),
+            name="weight_grads",
+        )(*operands, *weight_grads)
+        *values, weight_grads[0], weight_grads[1] = tie([*values, *weight_grads])
+        held[:] = values
+        return values
+
+    held = []
+    grad_input = scatter_sums(partial, meanwhile)
+    return (grad_input, *weight_grads)
+
+
 def solution(mesh):
     in_specs = (
         P(("groups", "ep"), "dp"),
@@ -152,4 +791,6 @@
         P(("groups", "ep"), "dp", None),
         P(("groups", "ep"), "dp", None),
     )
+    ep_count = mesh.shape["ep"]
+    body = gather_body if ep_count == 2 * LINES else exchange_body
     return jax.shard_map(body, mesh=mesh, in_specs=in_specs, out_specs=out_specs, check_vma=False)

time: 532 us -> 140 us (0.26); the launches traced: 524 us -> 139 us
  local copies, waits for them, and re-layouts: 179 us -> 4.14 us
  waiting for transfers between devices: 179 us -> 22.5 us
  matrix products: 87.5 us -> 0 us
  Pallas kernels: 0 us -> 68.8 us
  blocking collectives: 33.4 us -> 0 us
  between operations: 14.3 us -> 1 us
  starting transfers between devices: 25.4 us -> 35.1 us
    all_to_all x4 -> x0, waiting for transfers between devices: 175 us -> none  [the longest x1 65.2 us: body(): lax.all_to_all(send_grads, 'ep', split_axis=0, concat_axis=0, tiled=True)]
    dot_general x7 -> x0, matrix products: 87.5 us -> none  [the longest x1 14.9 us: expert_work(): jnp.einsum('nlcd,lfd->nlcf', grad_rows, full_down, preferred_element_type...]
    pallas_call x0 -> x12, Pallas kernels: none -> 68.8 us  [the longest x4 16.4 us: meanwhile(): pl.pallas_call(weight_kernel, grid=(group,), out_shape=(weight_shape, wei...]
    unnamed x15 -> x12, local copies, waits for them, and re-layouts: 66.1 us -> 3.82 us
    scatter x3 -> x0, local copies, waits for them, and re-layouts: 38.9 us -> none  [fill_slots(): return zeroed.at[slot_ids].set(values)]
    all_to_all x7 -> x0, local copies, waits for them, and re-layouts: 38.2 us -> none  [the longest x2 27.7 us: body(): lax.all_to_all(row_grad.reshape(ep_count, local_count, 1, capacity, featu...]
    ppermute x0 -> x27, starting transfers between devices: none -> 35.1 us  [the longest x10 19.5 us: along_line(): return lax.ppermute(value, 'ep', pairs)]
    all_to_all x3 -> x0, blocking collectives: 31.6 us -> none  [the longest x1 14.8 us: body(): lax.all_to_all(shaped_grads, 'dp', split_axis=2, concat_axis=4, tiled=True)]
  transfers between devices with their start and end apart: 9 -> 27, of which waited for: 4 -> 13; matrix products, arithmetic and copies ran while one was open for 47% -> 3% of each run, Pallas kernels for 0% -> 39%
where the time goes in v2:
time: 140 us; the launch traced here: 139 us
  Pallas kernels  68.8 us (49%)
  starting transfers between devices  35.1 us (25%)
  waiting for transfers between devices  22.5 us (16%)
  other arithmetic  7.62 us (5%)
  local copies, waits for them, and re-layouts  4.14 us (3%)
    ppermute x10, starting transfers between devices, along_line(): return lax.ppermute(value, 'ep', pairs)  19.5 us
    pallas_call x4, Pallas kernels, meanwhile(): pl.pallas_call(weight_kernel, grid=(group,), out_shape=(weight_shape, wei...  16.4 us
    pallas_call x1, Pallas kernels, gather_body(): pl.pallas_call(rows_kernel, out_shape=(jax.ShapeDtypeStruct((local_count,...  14 us
    ppermute x9, starting transfers between devices, across_pair(): return lax.ppermute(value, 'ep', [(i, i ^ 1) for i in range(2 * LINES)])  10.7 us
    pallas_call x1, Pallas kernels, turned(): pl.pallas_call(turn_kernel, out_shape=pltpu.HBM(shape, bf16), in_specs=[m...  9.36 us
    ppermute x10, waiting for transfers between devices, along_line(): return lax.ppermute(value, 'ep', pairs)  8.53 us
    ppermute x4, waiting for transfers between devices, widen(): lax.ppermute(info, 'ep', [(i, i ^ bit) for i in range(2 * LINES)])  8.12 us
    pallas_call x1, Pallas kernels, gather_body(): pl.pallas_call(pre_kernel, out_shape=(x_shape, in_hbm_shape, in_hbm_shape...  7.54 us
  transfers between devices with their start and end apart: 27, of which 13 were waited for; matrix products, arithmetic and copies ran while one was open for 3% of the time, Pallas kernels for 39%

profile of v2, /device:TPU:12, one launch (start us, length us, event | category | flops | bytes accessed | tf_op | source)
XLA Modules:
  0.0 139.1 jit_solution(14442962023778171632)
XLA Ops:
  3.3 3.5 %collective-permute-start.1 = (bf16[2,128,1024]{2,1,0:T(8,128)(2,1)S(1)}, bf16[2,128,1024]{2,1,0:T(8,128)(2,1)S(1)}, u32[]{:S(2)}, u32[]{:S(2)}) collective-permute-start(bf16[2,128,1024]{2,1,0:T(8,128)(2,1)S(1)} %pad_maximum_fusion.refs_0_), channel_id=1, source_target_pairs={{4,8},{6,10},{8,4},{10,6},{5,9},{7,11},{9,5},{11,7},{20,24},{22,26... | collective-permute-start | bytes 1572872 | tf_op jit(solution)/shard_map/ppermute | solution.py:155
  11.1 5.0 %collective-permute-done.4 = bf16[8,16,128]{2,1,0:T(8,128)(2,1)S(1)} collective-permute-done((bf16[8,16,128]{2,1,0:T(8,128)(2,1)S(1)}, bf16[8,16,128]{2,1,0:T(8,128)(2,1)S(1)}, u32[]{:S(2)}, u32[]{:S(2)}) %collective-permute-start.4) | collective-permute-done | bytes 32800 | tf_op jit(solution)/shard_map/ppermute | solution.py:174
  16.2 2.4 %collective-permute-done.1 = bf16[2,128,1024]{2,1,0:T(8,128)(2,1)S(1)} collective-permute-done((bf16[2,128,1024]{2,1,0:T(8,128)(2,1)S(1)}, bf16[2,128,1024]{2,1,0:T(8,128)(2,1)S(1)}, u32[]{:S(2)}, u32[]{:S(2)}) %collective-permute-start.1) | collective-permute-done | bytes 524320 | tf_op jit(solution)/shard_map/ppermute | solution.py:155
  20.4 2.2 %collective-permute-start.6 = (bf16[8,16,128]{2,1,0:T(8,128)(2,1)S(1)}, bf16[8,16,128]{2,1,0:T(8,128)(2,1)S(1)}, u32[]{:S(2)}, u32[]{:S(2)}) collective-permute-start(bf16[8,16,128]{2,1,0:T(8,128)(2,1)S(1)} %add.83), channel_id=1, source_target_pairs={{0,8},{2,10},{4,12},{6,14},{8,0},{10,2},{12,4},{14,6},{1,9},{3,11}... | collective-permute-start | bytes 98312 | tf_op jit(solution)/shard_map/ppermute | solution.py:174
  26.5 2.8 %collective-permute-start.8 = (bf16[2,128,1024]{2,1,0:T(8,128)(2,1)S(1)}, bf16[2,128,1024]{2,1,0:T(8,128)(2,1)S(1)}, u32[]{:S(2)}, u32[]{:S(2)}) collective-permute-start(bf16[2,128,1024]{2,1,0:T(8,128)(2,1)S(1)} %collective-permute-done.1), channel_id=1, source_target_pairs={{4,0},{6,2},{8,12},{10,14},{5,1},{7,3},{9,13},{11,15},{20,16},{22,... | collective-permute-start | bytes 1572872 | tf_op jit(solution)/shard_map/ppermute | solution.py:155
  29.9 2.7 %collective-permute-start.9 = (bf16[2,128,1024]{2,1,0:T(8,128)(2,1)S(1)}, bf16[2,128,1024]{2,1,0:T(8,128)(2,1)}, u32[]{:S(2)}, u32[]{:S(2)}) collective-permute-start(bf16[2,128,1024]{2,1,0:T(8,128)(2,1)S(1)} %collective-permute-done.refs_2_), channel_id=1, source_target_pairs={{4,8},{6,10},{8,4},{10,6},{5,9},{7,11},{9,5},{11,7},{20,24},{22,26... | collective-permute-start | bytes 1572872 | tf_op jit(solution)/shard_map/ppermute | solution.py:155
  32.6 9.4 %turn.1.gate_w.refs_9_ = bf16[16,384,1024]{2,1,0:T(8,128)(2,1)} custom-call(bf16[16,1024,384]{2,1,0:T(8,128)(2,1)} %w_ref.1), custom_call_target="tpu_custom_call" | custom-call | bytes 25165824 | tf_op jit(solution)/shard_map/turn/pallas_call | solution.py:603
  42.9 1.6 %collective-permute-start.12 = (bf16[2,128,1024]{2,1,0:T(8,128)(2,1)S(1)}, bf16[2,128,1024]{2,1,0:T(8,128)(2,1)S(1)}, u32[]{:S(2)}, u32[]{:S(2)}) collective-permute-start(bf16[2,128,1024]{2,1,0:T(8,128)(2,1)S(1)} %broadcast_select_fusion.refs_0_), channel_id=1, source_target_pairs={{0,2},{2,0},{4,6},{6,4},{8,10},{10,8},{12,14},{14,12},{1,3},{3,1},... | collective-permute-start | bytes 1572872 | tf_op jit(solution)/shard_map/ppermute | solution.py:159
  44.4 2.1 %collective-permute-start.11 = (bf16[2,128,1024]{2,1,0:T(8,128)(2,1)}, bf16[2,128,1024]{2,1,0:T(8,128)(2,1)}, u32[]{:S(2)}, u32[]{:S(2)}) collective-permute-start(bf16[2,128,1024]{2,1,0:T(8,128)(2,1)} %collective-permute-done.9), channel_id=1, source_target_pairs={{4,0},{6,2},{8,12},{10,14},{5,1},{7,3},{9,13},{11,15},{20,16},{22,... | collective-permute-start | bytes 1572872 | tf_op jit(solution)/shard_map/ppermute | solution.py:155
  48.2 2.3 %first_slots.1 = (bf16[16,48,1024]{2,1,0:T(8,128)(2,1)S(1)}, bf16[16,48,1024]{2,1,0:T(8,128)(2,1)S(1)}, f32[16,96,128]{2,1,0:T(8,128)S(1)}) custom-call(s32[16,1024]{1,0:T(8,128)S(1)} %get-tuple-element.79.slot_ref, f32[16,1024]{1,0:T(8,128)S(1)} %get-tuple-element.80.gates_ref, bf16[2,128,1024]{2,1,0:T(8,128)(2,1)S(1)} %pad_maximum_fusion.refs_0_, ...), custom_call_target="tpu_custom_call" | custom-call | flops 1610612736 | bytes 6291456 | tf_op jit(solution)/shard_map/first_slots/pallas_call | solution.py:647
  50.5 3.0 %collective-permute-done.12.refs_1_ = bf16[2,128,1024]{2,1,0:T(8,128)(2,1)S(1)} collective-permute-done((bf16[2,128,1024]{2,1,0:T(8,128)(2,1)S(1)}, bf16[2,128,1024]{2,1,0:T(8,128)(2,1)S(1)}, u32[]{:S(2)}, u32[]{:S(2)}) %collective-permute-start.12) | collective-permute-done | bytes 524320 | tf_op jit(solution)/shard_map/ppermute | solution.py:159
  58.4 4.7 %load.1.refs_5_ = bf16[16,1024,384]{2,1,0:T(8,128)(2,1)S(1)} custom-call(bf16[16,1024,384]{2,1,0:T(8,128)(2,1)} %w_ref.1), custom_call_target="tpu_custom_call" | custom-call | bytes 12582912 | tf_op jit(solution)/shard_map/load/pallas_call | solution.py:623
  63.1 7.5 %pre.1 = (bf16[16,96,1024]{2,1,0:T(8,128)(2,1)S(1)}, f32[16,96,384]{2,1,0:T(8,128)}, f32[16,96,384]{2,1,0:T(8,128)}) custom-call(s32[16,1024]{1,0:T(8,128)S(1)} %get-tuple-element.79.slot_ref, bf16[2,128,1024]{2,1,0:T(8,128)(2,1)S(1)} %broadcast_select_fusion.refs_0_, bf16[2,128,1024]{2,1,0:T(8,128)(2,1)S(1)} %collective-permute-done.12.refs_1_, ...), custom_call_target="tpu_custom_call" | custom-call | flops 3221225472 | bytes 35232152 | tf_op jit(solution)/shard_map/pre/pallas_call | solution.py:666
  71.3 7.4 %down.1.refs_5_ = f32[16,96,384]{2,1,0:T(8,128)} custom-call(s32[16,1024]{1,0:T(8,128)S(1)} %get-tuple-element.79.slot_ref, bf16[2,128,1024]{2,1,0:T(8,128)(2,1)S(1)} %broadcast_select_fusion.refs_0_, bf16[2,128,1024]{2,1,0:T(8,128)(2,1)S(1)} %collective-permute-done.12.refs_1_, bf16[128,1024]{1,0:T(8,128)(2,1)S(1)} %select_bitcast_fusion.refs_2_, ...), custom_call_target="tpu_custom_call" | custom-call | flops 2013265920 | bytes 17616076 | tf_op jit(solution)/shard_map/down/pallas_call | solution.py:684
  78.9 6.4 %load_half.1 = (bf16[8,384,1024]{2,1,0:T(8,128)(2,1)S(1)}, bf16[8,1024,384]{2,1,0:T(8,128)(2,1)S(1)}) custom-call(bf16[16,384,1024]{2,1,0:T(8,128)(2,1)} %turn.1.gate_w.refs_9_, bf16[16,1024,384]{2,1,0:T(8,128)(2,1)} %refs_10_.1), custom_call_target="tpu_custom_call" | custom-call | bytes 12582912 | tf_op jit(solution)/shard_map/load_half/pallas_call | solution.py:700
  86.7 14.0 %rows.1 = (bf16[16,96,768]{2,1,0:T(8,128)(2,1)}, bf16[128,1024]{1,0:T(8,128)(2,1)S(1)}, bf16[128,1024]{1,0:T(8,128)(2,1)S(1)}, bf16[128,1024]{1,0:T(8,128)(2,1)S...) custom-call(s32[16,1024]{1,0:T(8,128)S(1)} %get-tuple-element.79.slo, ...), custom_call_target="tpu_custom_call" | custom-call | flops 4026531840 | bytes 25165824 | tf_op jit(solution)/shard_map/rows/pallas_call | solution.py:710
  102.8 1.7 %copy-done = bf16[16,96,768]{2,1,0:T(8,128)(2,1)S(1)} copy-done((bf16[16,96,768]{2,1,0:T(8,128)(2,1)S(1)}, bf16[16,96,768]{2,1,0:T(8,128)(2,1)}, u32[]{:S(2)}) %copy-start) | copy-done | bytes 2359320
  104.5 4.1 %weight_grads.4 = (bf16[16,1024,384]{2,1,0:T(8,128)(2,1)}, bf16[16,1024,384]{2,1,0:T(8,128)(2,1)}) custom-call(bf16[16,96,1024]{2,1,0:T(8,128)(2,1)S(1)} %get-tuple-element.136.x_ref, bf16[16,96,768]{2,1,0:T(8,128)(2,1)S(1)} %copy-done), custom_call_target="tpu_custom_call" | custom-call | flops 603979776 | bytes 7864320 | tf_op jit(solution)/shard_map/weight_grads/pallas_call | solution.py:758
  112.7 4.1 %weight_grads.5 = (bf16[16,1024,384]{2,1,0:T(8,128)(2,1)}, bf16[16,1024,384]{2,1,0:T(8,128)(2,1)}) custom-call(bf16[16,96,1024]{2,1,0:T(8,128)(2,1)S(1)} %get-tuple-element.136.x_ref, bf16[16,96,768]{2,1,0:T(8,128)(2,1)S(1)} %copy-done, bf16[16,1024,384]{2,1,0:T(8,128)(2,1)} %get-tuple-element.121.refs_0_, ...), custom_call_target="tpu_custom_call", output_to_operand_aliasing={{0}: (2, {}), {1}: (3, {})} | custom-call | flops 603979776 | bytes 7864320 | tf_op jit(solution)/shard_map/weight_grads/pallas_call | solution.py:758
  116.8 2.7 %collective-permute-done.19 = bf16[128,1024]{1,0:T(8,128)(2,1)S(1)} collective-permute-done((bf16[128,1024]{1,0:T(8,128)(2,1)S(1)}, bf16[128,1024]{1,0:T(8,128)(2,1)S(1)}, u32[]{:S(2)}, u32[]{:S(2)}) %collective-permute-start.19) | collective-permute-done | bytes 262176 | tf_op jit(solution)/shard_map/ppermute | solution.py:155
  121.1 2.7 %collective-permute-start.21 = (bf16[128,1024]{1,0:T(8,128)(2,1)S(1)}, bf16[128,1024]{1,0:T(8,128)(2,1)S(1)}, u32[]{:S(2)}, u32[]{:S(2)}) collective-permute-start(bf16[128,1024]{1,0:T(8,128)(2,1)S(1)} %add_convert_fusion.3), channel_id=1, source_target_pairs={{4,8},{6,10},{8,4},{10,6},{5,9},{7,11},{9,5},{11,7},{20,24},{22,26... | collective-permute-start | bytes 786440 | tf_op jit(solution)/shard_map/ppermute | solution.py:155
  125.2 4.1 %weight_grads.6 = (bf16[16,1024,384]{2,1,0:T(8,128)(2,1)}, bf16[16,1024,384]{2,1,0:T(8,128)(2,1)}) custom-call(bf16[16,96,1024]{2,1,0:T(8,128)(2,1)S(1)} %get-tuple-element.136.x_ref, bf16[16,96,768]{2,1,0:T(8,128)(2,1)S(1)} %copy-done, bf16[16,1024,384]{2,1,0:T(8,128)(2,1)} %get-tuple-element.129.refs_0_, ...), custom_call_target="tpu_custom_call", output_to_operand_aliasing={{0}: (2, {}), {1}: (3, {})} | custom-call | flops 603979776 | bytes 7864320 | tf_op jit(solution)/shard_map/weight_grads/pallas_call | solution.py:758
  130.0 2.9 %collective-permute-start.24 = (bf16[128,1024]{1,0:T(8,128)(2,1)S(1)}, bf16[128,1024]{1,0:T(8,128)(2,1)S(1)}, u32[]{:S(2)}, u32[]{:S(2)}) collective-permute-start(bf16[128,1024]{1,0:T(8,128)(2,1)S(1)} %add_convert_fusion.2), channel_id=1, source_target_pairs={{4,8},{6,10},{8,4},{10,6},{5,9},{7,11},{9,5},{11,7},{20,24},{22,26... | collective-permute-start | bytes 786440 | tf_op jit(solution)/shard_map/ppermute | solution.py:155
  133.0 4.1 %weight_grads.7 = (bf16[16,1024,384]{2,1,0:T(8,128)(2,1)}, bf16[16,1024,384]{2,1,0:T(8,128)(2,1)}) custom-call(bf16[16,96,1024]{2,1,0:T(8,128)(2,1)S(1)} %get-tuple-element.136.x_ref, bf16[16,96,768]{2,1,0:T(8,128)(2,1)S(1)} %copy-done, bf16[16,1024,384]{2,1,0:T(8,128)(2,1)} %get-tuple-element.138.refs_0_, ...), custom_call_target="tpu_custom_call", output_to_operand_aliasing={{0}: (2, {}), {1}: (3, {})} | custom-call | flops 603979776 | bytes 7864320 | tf_op jit(solution)/shard_map/weight_grads/pallas_call | solution.py:758
  (76 shorter events, 34.7 us)
Async XLA Ops:
  1.7 14.4 %collective-permute-start.2 = (bf16[2,128,1024]{2,1,0:T(8,128)(2,1)S(1)}, bf16[2,128,1024]{2,1,0:T(8,128)(2,1)S(1)}, u32[]{:S(2)}, u32[]{:S(2)}) collective-permute-start(bf16[2,128,1024]{2,1,0:T(8,128)(2,1)S(1)} %pad_maximum_fusion.refs_0_), channel_id=1, source_target_pairs={{0,2},{2,0},{4,6},{6,4},{8,10},{10,8},{12,14},{14,12},{1,3},{3,1},... | collective-permute-start | bytes 1572872 | tf_op jit(solution)/shard_map/ppermute | solution.py:159
  3.3 15.3 %collective-permute-start.1 = (bf16[2,128,1024]{2,1,0:T(8,128)(2,1)S(1)}, bf16[2,128,1024]{2,1,0:T(8,128)(2,1)S(1)}, u32[]{:S(2)}, u32[]{:S(2)}) collective-permute-start(bf16[2,128,1024]{2,1,0:T(8,128)(2,1)S(1)} %pad_maximum_fusion.refs_0_), channel_id=1, source_target_pairs={{4,8},{6,10},{8,4},{10,6},{5,9},{7,11},{9,5},{11,7},{20,24},{22,26... | collective-permute-start | bytes 1572872 | tf_op jit(solution)/shard_map/ppermute | solution.py:155
  6.8 13.2 %collective-permute-start = (bf16[2,128,1024]{2,1,0:T(8,128)(2,1)S(1)}, bf16[2,128,1024]{2,1,0:T(8,128)(2,1)S(1)}, u32[]{:S(2)}, u32[]{:S(2)}) collective-permute-start(bf16[2,128,1024]{2,1,0:T(8,128)(2,1)S(1)} %pad_maximum_fusion.refs_0_), channel_id=1, source_target_pairs={{0,4},{2,6},{4,0},{6,2},{8,12},{10,14},{12,8},{14,10},{1,5},{3,7},... | collective-permute-start | bytes 1572872 | tf_op jit(solution)/shard_map/ppermute | solution.py:155
  10.5 5.6 %collective-permute-start.4 = (bf16[8,16,128]{2,1,0:T(8,128)(2,1)S(1)}, bf16[8,16,128]{2,1,0:T(8,128)(2,1)S(1)}, u32[]{:S(2)}, u32[]{:S(2)}) collective-permute-start(bf16[8,16,128]{2,1,0:T(8,128)(2,1)S(1)} %add.82), channel_id=1, source_target_pairs={{0,2},{2,0},{4,6},{6,4},{8,10},{10,8},{12,14},{14,12},{1,3},{3,1},... | collective-permute-start | bytes 98312 | tf_op jit(solution)/shard_map/ppermute | solution.py:174
  20.4 4.9 %collective-permute-start.6 = (bf16[8,16,128]{2,1,0:T(8,128)(2,1)S(1)}, bf16[8,16,128]{2,1,0:T(8,128)(2,1)S(1)}, u32[]{:S(2)}, u32[]{:S(2)}) collective-permute-start(bf16[8,16,128]{2,1,0:T(8,128)(2,1)S(1)} %add.83), channel_id=1, source_target_pairs={{0,8},{2,10},{4,12},{6,14},{8,0},{10,2},{12,4},{14,6},{1,9},{3,11}... | collective-permute-start | bytes 98312 | tf_op jit(solution)/shard_map/ppermute | solution.py:174
  26.5 15.5 %collective-permute-start.8 = (bf16[2,128,1024]{2,1,0:T(8,128)(2,1)S(1)}, bf16[2,128,1024]{2,1,0:T(8,128)(2,1)S(1)}, u32[]{:S(2)}, u32[]{:S(2)}) collective-permute-start(bf16[2,128,1024]{2,1,0:T(8,128)(2,1)S(1)} %collective-permute-done.1), channel_id=1, source_target_pairs={{4,0},{6,2},{8,12},{10,14},{5,1},{7,3},{9,13},{11,15},{20,16},{22,... | collective-permute-start | bytes 1572872 | tf_op jit(solution)/shard_map/ppermute | solution.py:155
  29.3 12.7 %collective-permute-start.10 = (bf16[2,128,1024]{2,1,0:T(8,128)(2,1)S(1)}, bf16[2,128,1024]{2,1,0:T(8,128)(2,1)S(1)}, u32[]{:S(2)}, u32[]{:S(2)}) collective-permute-start(bf16[2,128,1024]{2,1,0:T(8,128)(2,1)S(1)} %collective-permute-done.refs_2_), channel_id=1, source_target_pairs={{0,2},{2,0},{4,6},{6,4},{8,10},{10,8},{12,14},{14,12},{1,3},{3,1},... | collective-permute-start | bytes 1572872 | tf_op jit(solution)/shard_map/ppermute | solution.py:159
  29.9 12.9 %collective-permute-start.9 = (bf16[2,128,1024]{2,1,0:T(8,128)(2,1)S(1)}, bf16[2,128,1024]{2,1,0:T(8,128)(2,1)}, u32[]{:S(2)}, u32[]{:S(2)}) collective-permute-start(bf16[2,128,1024]{2,1,0:T(8,128)(2,1)S(1)} %collective-permute-done.refs_2_), channel_id=1, source_target_pairs={{4,8},{6,10},{8,4},{10,6},{5,9},{7,11},{9,5},{11,7},{20,24},{22,26... | collective-permute-start | bytes 1572872 | tf_op jit(solution)/shard_map/ppermute | solution.py:155
  42.9 10.7 %collective-permute-start.12 = (bf16[2,128,1024]{2,1,0:T(8,128)(2,1)S(1)}, bf16[2,128,1024]{2,1,0:T(8,128)(2,1)S(1)}, u32[]{:S(2)}, u32[]{:S(2)}) collective-permute-start(bf16[2,128,1024]{2,1,0:T(8,128)(2,1)S(1)} %broadcast_select_fusion.refs_0_), channel_id=1, source_target_pairs={{0,2},{2,0},{4,6},{6,4},{8,10},{10,8},{12,14},{14,12},{1,3},{3,1},... | collective-permute-start | bytes 1572872 | tf_op jit(solution)/shard_map/ppermute | solution.py:159
  44.4 9.7 %collective-permute-start.11 = (bf16[2,128,1024]{2,1,0:T(8,128)(2,1)}, bf16[2,128,1024]{2,1,0:T(8,128)(2,1)}, u32[]{:S(2)}, u32[]{:S(2)}) collective-permute-start(bf16[2,128,1024]{2,1,0:T(8,128)(2,1)} %collective-permute-done.9), channel_id=1, source_target_pairs={{4,0},{6,2},{8,12},{10,14},{5,1},{7,3},{9,13},{11,15},{20,16},{22,... | collective-permute-start | bytes 1572872 | tf_op jit(solution)/shard_map/ppermute | solution.py:155
  55.2 7.9 %collective-permute-start.13 = (bf16[128,1024]{1,0:T(8,128)(2,1)S(1)}, bf16[128,1024]{1,0:T(8,128)(2,1)S(1)}, u32[]{:S(2)}, u32[]{:S(2)}) collective-permute-start(bf16[128,1024]{1,0:T(8,128)(2,1)S(1)} %select_bitcast_fusion.1.refs_2_), channel_id=1, source_target_pairs={{0,2},{2,0},{4,6},{6,4},{8,10},{10,8},{12,14},{14,12},{1,3},{3,1},... | collective-permute-start | bytes 786440 | tf_op jit(solution)/shard_map/ppermute | solution.py:159
  57.6 13.1 %collective-permute-start.16 = (bf16[128,1024]{1,0:T(8,128)(2,1)S(1)}, bf16[128,1024]{1,0:T(8,128)(2,1)S(1)}, u32[]{:S(2)}, u32[]{:S(2)}) collective-permute-start(bf16[128,1024]{1,0:T(8,128)(2,1)S(1)} %select_bitcast_fusion.refs_2_), channel_id=1, source_target_pairs={{0,2},{2,0},{4,6},{6,4},{8,10},{10,8},{12,14},{14,12},{1,3},{3,1},... | collective-permute-start | bytes 786440 | tf_op jit(solution)/shard_map/ppermute | solution.py:159
  70.7 8.2 %collective-permute-start.14 = (f32[16,96,384]{2,1,0:T(8,128)}, f32[16,96,384]{2,1,0:T(8,128)S(1)}, u32[]{:S(2)}, u32[]{:S(2)}) collective-permute-start(f32[16,96,384]{2,1,0:T(8,128)} %get-tuple-element.94.refs_1_), channel_id=1, source_target_pairs={{0,1},{1,0},{2,3},{3,2},{4,5},{5,4},{6,7},{7,6},{8,9},{9,8},{10,11... | collective-permute-start | bytes 7077896 | tf_op jit(solution)/shard_map/ppermute | solution.py:163
  70.8 8.1 %collective-permute-start.15 = (f32[16,96,384]{2,1,0:T(8,128)}, f32[16,96,384]{2,1,0:T(8,128)S(1)}, u32[]{:S(2)}, u32[]{:S(2)}) collective-permute-start(f32[16,96,384]{2,1,0:T(8,128)} %get-tuple-element.95.refs_3_), channel_id=1, source_target_pairs={{0,1},{1,0},{2,3},{3,2},{4,5},{5,4},{6,7},{7,6},{8,9},{9,8},{10,11... | collective-permute-start | bytes 7077896 | tf_op jit(solution)/shard_map/ppermute | solution.py:163
  78.7 6.6 %collective-permute-start.17 = (f32[16,96,384]{2,1,0:T(8,128)}, f32[16,96,384]{2,1,0:T(8,128)S(1)}, u32[]{:S(2)}, u32[]{:S(2)}) collective-permute-start(f32[16,96,384]{2,1,0:T(8,128)} %down.1.refs_5_), channel_id=1, source_target_pairs={{0,1},{1,0},{2,3},{3,2},{4,5},{5,4},{6,7},{7,6},{8,9},{9,8},{10,11... | collective-permute-start | bytes 7077896 | tf_op jit(solution)/shard_map/ppermute | solution.py:163
  100.7 9.4 %collective-permute-start.18 = (bf16[128,1024]{1,0:T(8,128)(2,1)}, bf16[128,1024]{1,0:T(8,128)(2,1)S(1)}, u32[]{:S(2)}, u32[]{:S(2)}) collective-permute-start(bf16[128,1024]{1,0:T(8,128)(2,1)} %get-tuple-element.108), channel_id=1, source_target_pairs={{0,2},{2,0},{4,6},{6,4},{8,10},{10,8},{12,14},{14,12},{1,3},{3,1},... | collective-permute-start | bytes 786440 | tf_op jit(solution)/shard_map/ppermute | solution.py:159
  102.0 14.8 %collective-permute-start.20 = (bf16[128,1024]{1,0:T(8,128)(2,1)S(1)}, bf16[128,1024]{1,0:T(8,128)(2,1)S(1)}, u32[]{:S(2)}, u32[]{:S(2)}) collective-permute-start(bf16[128,1024]{1,0:T(8,128)(2,1)S(1)} %get-tuple-element.113), channel_id=1, source_target_pairs={{0,2},{2,0},{4,6},{6,4},{8,10},{10,8},{12,14},{14,12},{1,3},{3,1},... | collective-permute-start | bytes 786440 | tf_op jit(solution)/shard_map/ppermute | solution.py:159
  110.2 9.4 %collective-permute-start.19 = (bf16[128,1024]{1,0:T(8,128)(2,1)S(1)}, bf16[128,1024]{1,0:T(8,128)(2,1)S(1)}, u32[]{:S(2)}, u32[]{:S(2)}) collective-permute-start(bf16[128,1024]{1,0:T(8,128)(2,1)S(1)} %fusion), channel_id=1, source_target_pairs={{0,4},{2,6},{12,8},{14,10},{1,5},{3,7},{13,9},{15,11},{16,20},{18,... | collective-permute-start | bytes 786440 | tf_op jit(solution)/shard_map/ppermute | solution.py:155
  111.5 17.8 %collective-permute-start.23 = (bf16[128,1024]{1,0:T(8,128)(2,1)S(1)}, bf16[128,1024]{1,0:T(8,128)(2,1)S(1)}, u32[]{:S(2)}, u32[]{:S(2)}) collective-permute-start(bf16[128,1024]{1,0:T(8,128)(2,1)S(1)} %get-tuple-element.112), channel_id=1, source_target_pairs={{0,2},{2,0},{4,6},{6,4},{8,10},{10,8},{12,14},{14,12},{1,3},{3,1},... | collective-permute-start | bytes 786440 | tf_op jit(solution)/shard_map/ppermute | solution.py:159
  119.8 9.5 %collective-permute-start.22 = (bf16[128,1024]{1,0:T(8,128)(2,1)S(1)}, bf16[128,1024]{1,0:T(8,128)(2,1)S(1)}, u32[]{:S(2)}, u32[]{:S(2)}) collective-permute-start(bf16[128,1024]{1,0:T(8,128)(2,1)S(1)} %fusion.1), channel_id=1, source_target_pairs={{0,4},{2,6},{12,8},{14,10},{1,5},{3,7},{13,9},{15,11},{16,20},{18,... | collective-permute-start | bytes 786440 | tf_op jit(solution)/shard_map/ppermute | solution.py:155
  121.1 8.5 %collective-permute-start.21 = (bf16[128,1024]{1,0:T(8,128)(2,1)S(1)}, bf16[128,1024]{1,0:T(8,128)(2,1)S(1)}, u32[]{:S(2)}, u32[]{:S(2)}) collective-permute-start(bf16[128,1024]{1,0:T(8,128)(2,1)S(1)} %add_convert_fusion.3), channel_id=1, source_target_pairs={{4,8},{6,10},{8,4},{10,6},{5,9},{7,11},{9,5},{11,7},{20,24},{22,26... | collective-permute-start | bytes 786440 | tf_op jit(solution)/shard_map/ppermute | solution.py:155
  123.8 13.3 %collective-permute-start.26 = (bf16[128,1024]{1,0:T(8,128)(2,1)S(1)}, bf16[128,1024]{1,0:T(8,128)(2,1)S(1)}, u32[]{:S(2)}, u32[]{:S(2)}) collective-permute-start(bf16[128,1024]{1,0:T(8,128)(2,1)S(1)} %get-tuple-element.110), channel_id=1, source_target_pairs={{0,2},{2,0},{4,6},{6,4},{8,10},{10,8},{12,14},{14,12},{1,3},{3,1},... | collective-permute-start | bytes 786440 | tf_op jit(solution)/shard_map/ppermute | solution.py:159
  129.8 7.3 %collective-permute-start.25 = (bf16[128,1024]{1,0:T(8,128)(2,1)S(1)}, bf16[128,1024]{1,0:T(8,128)(2,1)S(1)}, u32[]{:S(2)}, u32[]{:S(2)}) collective-permute-start(bf16[128,1024]{1,0:T(8,128)(2,1)S(1)} %add_convert_fusion.1), channel_id=1, source_target_pairs={{0,4},{2,6},{4,0},{6,2},{8,12},{10,14},{12,8},{14,10},{1,5},{3,7},... | collective-permute-start | bytes 786440 | tf_op jit(solution)/shard_map/ppermute | solution.py:155
  130.0 8.3 %collective-permute-start.24 = (bf16[128,1024]{1,0:T(8,128)(2,1)S(1)}, bf16[128,1024]{1,0:T(8,128)(2,1)S(1)}, u32[]{:S(2)}, u32[]{:S(2)}) collective-permute-start(bf16[128,1024]{1,0:T(8,128)(2,1)S(1)} %add_convert_fusion.2), channel_id=1, source_target_pairs={{4,8},{6,10},{8,4},{10,6},{5,9},{7,11},{9,5},{11,7},{20,24},{22,26... | collective-permute-start | bytes 786440 | tf_op jit(solution)/shard_map/ppermute | solution.py:155
  (9 other events, 32.8 us)

commit v3 on v2

--- a/solution.py
+++ b/solution.py
@@ -144,6 +144,7 @@
 ORDERS = ((0, 1, 2, 3), (1, 0, 2, 3), (2, 3, 1, 0), (3, 2, 1, 0))
 LINES = len(ORDERS)
 PARTS = 2
+HALVES = 2
 OUTER = ((0, 1), (1, 0), (2, 3), (3, 2))
 INNER = ((1, 2), (2, 1))
 TO_END = ((1, 0), (2, 3))
@@ -177,24 +178,22 @@
 
     outer, inner, other = along_line(rows, OUTER), along_line(rows, INNER), across_pair(rows)
     info = widen(info + across_cores(info), [1])
+    info = widen(info, [2, 4, 6])
     outer, inner, other, info = tie((outer, inner, other, info))
     pieces = [rows, other]
 
-    info = widen(info, [2, 4, 6])
-    outer, inner, info = tie((outer, inner, info))
     second, third = along_line(inner, TO_END), along_line(outer, INNER)
     other = across_pair(outer)
-    done = meanwhile(0, info, pieces)
-    second, third, other = tie((second, third, other), *done)
+    second, third, other = tie((second, third, other))
     pieces += [outer, other]
 
     middle = jnp.where(at_end, second, inner)
     last, other = along_line(third, TO_END), across_pair(middle)
-    done = meanwhile(1, info, pieces)
+    done = meanwhile(0, info, pieces)
     last, other = tie((last, other), *done)
     pieces += [middle, other]
 
-    meanwhile(2, info, [last, other])
+    meanwhile(1, info, [last, other])
     for part in range(2):
         far = jnp.where(at_end, last[part], third[part])
         pieces += [far, across_pair(far)]
@@ -289,36 +288,20 @@
     return [row == slot_ref[e : e + 1, columns] for e in experts]
 
 
-def dispatch(part, slot_ref, rows_ref, x_ref):
-    local_count = slot_ref.shape[0]
+def dispatch(part, slot_ref, rows_ref, x_ref, start=0):
+    local_count = x_ref.shape[0]
     count = 2 * LINES * 2 * CAP // PARTS
     first_slot = part * count if x_ref.shape[1] > count else 0
     group = min(8, local_count)
     for first in range(0, local_count, group):
-        experts = range(first, first + group)
+        experts = range(start + first, start + first + group)
         hot = jnp.concatenate(
             [h.astype(jnp.bfloat16) for h in hot_part(slot_ref, experts, part, count * PARTS)]
         )
         found = jnp.dot(hot, rows_ref[...], preferred_element_type=jnp.float32)
         found = found.astype(jnp.bfloat16)
         for i, e in enumerate(experts):
-            x_ref[e, first_slot : first_slot + count] = found[i * count : (i + 1) * count]
-
-
-def turn_kernel(w_ref, out_ref, w_here, out_here, w_sems, out_sems):
-    weights = group_copies(w_ref, w_here, w_sems)
-    group = w_here.shape[0] // len(weights)
-    copies = []
-    for i, weight in enumerate(weights):
-        weight.wait()
-        for e in range(i * group, (i + 1) * group):
-            out_here[e] = w_here[e].T
-        span = pl.ds(i * group, group)
-        copies += start_all(
-            [pltpu.make_async_copy(out_here.at[span], out_ref.at[span], out_sems.at[i])]
-        )
-    for copy in copies:
-        copy.wait()
+            x_ref[e - start, first_slot : first_slot + count] = found[i * count : (i + 1) * count]
 
 
 def first_kernel(slot_ref, gates_ref, *refs):
@@ -344,23 +327,27 @@
             )
 
 
-def finish_slots(index, slot_ref, pieces, first_ref, rows_ref, x_here, piece_sems, first_sem):
+def finish_slots(
+    index, slot_ref, pieces, first_ref, rows_ref, x_here, piece_sems, first_sem, start=0
+):
     sources = [piece.at[index] if len(piece.shape) == 3 else piece for piece in pieces]
     arrivals = piece_copies(sources, rows_ref, piece_sems)
-    count = first_ref.shape[1]
-    first = pltpu.make_async_copy(first_ref, x_here.at[:, pl.ds(0, count)], first_sem)
+    experts = pl.ds(start, x_here.shape[0])
+    first = pltpu.make_async_copy(
+        first_ref.at[experts], x_here.at[:, pl.ds(0, first_ref.shape[1])], first_sem
+    )
     first.start()
 
     def finish():
         for copy in arrivals:
             copy.wait()
-        dispatch(1, slot_ref, rows_ref, x_here)
+        dispatch(1, slot_ref, rows_ref, x_here, start)
         first.wait()
 
     return finish
 
 
-def multiply(x_ref, w_ref, here, out_ref, out_sems, weights=None, side=0):
+def multiply(x_ref, w_ref, here, out_refs, out_sems, weights=None, side=0):
     groups = out_sems.shape[0]
     group = x_ref.shape[0] // groups
     copies = []
@@ -374,10 +361,9 @@
                 (((1,), (side,)), ((), ())),
                 preferred_element_type=jnp.float32,
             )
-        span = pl.ds(i * group, group)
-        copies += start_all(
-            [pltpu.make_async_copy(here.at[span], out_ref.at[span], out_sems.at[i])]
-        )
+        span, each = pl.ds(i * group, group), groups // len(out_refs)
+        target = out_refs[i // each].at[pl.ds(i % each * group, group)]
+        copies += start_all([pltpu.make_async_copy(here.at[span], target, out_sems.at[i])])
     return copies
 
 
@@ -388,31 +374,33 @@
 
 def pre_kernel(slot_ref, *refs):
     pieces, refs = refs[:4], refs[4:]
-    first_ref, gate_w, up_w, x_ref, gate_ref, up_ref = refs[:6]
-    rows_here, x_here, up_w_here, gate_here, up_here = refs[6:11]
-    piece_sems, first_sem, up_w_sems, x_sem, gate_sems, up_sems = refs[11:]
+    first_ref, gate_w, up_w, x_ref = refs[:4]
+    gate_refs, up_refs = refs[4 : 4 + HALVES], refs[4 + HALVES : 4 + 2 * HALVES]
+    refs = refs[4 + 2 * HALVES :]
+    rows_here, x_here, up_w_here, gate_here, up_here = refs[:5]
+    piece_sems, first_sem, up_w_sems, x_sem, gate_sems, up_sems = refs[5:]
     finish = finish_slots(
         0, slot_ref, pieces, first_ref, rows_here, x_here, piece_sems, first_sem
     )
     up_ws = group_copies(up_w, up_w_here, up_w_sems)
     finish()
     copies = start_all([pltpu.make_async_copy(x_here, x_ref, x_sem)])
-    copies += multiply(x_here, gate_w, gate_here, gate_ref, gate_sems)
-    copies += multiply(x_here, up_w_here, up_here, up_ref, up_sems, up_ws)
+    copies += multiply(x_here, gate_w, gate_here, gate_refs, gate_sems)
+    copies += multiply(x_here, up_w_here, up_here, up_refs, up_sems, up_ws)
     for copy in copies:
         copy.wait()
 
 
-def down_kernel(slot_ref, *refs):
+def down_kernel(start, slot_ref, *refs):
     pieces, refs = refs[:4], refs[4:]
     first_ref, down_w, raw_ref = refs[:3]
     rows_here, x_here, w_here, here, piece_sems, first_sem, w_sems, out_sems = refs[3:]
     finish = finish_slots(
-        1, slot_ref, pieces, first_ref, rows_here, x_here, piece_sems, first_sem
-    )
-    weights = group_copies(down_w, w_here, w_sems)
+        1, slot_ref, pieces, first_ref, rows_here, x_here, piece_sems, first_sem, start
+    )
+    weights = group_copies(down_w.at[pl.ds(start, x_here.shape[0])], w_here, w_sems)
     finish()
-    for copy in multiply(x_here, w_here, here, raw_ref, out_sems, weights, 1):
+    for copy in multiply(x_here, w_here, here, [raw_ref], out_sems, weights, 1):
         copy.wait()
 
 
@@ -422,70 +410,56 @@
         rows_ref[part, e * count : (e + 1) * count] = row[part * count : (part + 1) * count]
 
 
-def combine(slot_ref, experts, rows_ref, sum_ref, outs, slots):
-    local_count = slot_ref.shape[0]
-    tokens, count = slot_ref.shape[1] // PARTS, slots // PARTS
-    copies = []
-    for part in reversed(range(PARTS)):
-        hot = jnp.concatenate(
-            [h.astype(jnp.bfloat16) for h in hot_part(slot_ref, experts, part, slots)]
-        )
-        total = lax.dot_general(
-            hot,
-            rows_ref[part, experts[0] * count : (experts[-1] + 1) * count],
-            (((0,), (0,)), ((), ())),
-            preferred_element_type=jnp.float32,
-        )
-        place = slice(part * tokens, (part + 1) * tokens)
-        if experts[0] > 0:
-            total += sum_ref[place]
-        if experts[-1] < local_count - 1:
-            sum_ref[place] = total
-        else:
-            each = len(outs) // PARTS
-            for i, (here, out, sem) in enumerate(outs[part * each : (part + 1) * each]):
-                rows = tokens // each
-                here[...] = total[i * rows : (i + 1) * rows].astype(jnp.bfloat16)
-                copies += start_all([pltpu.make_async_copy(here, out, sem)])
-    return copies
-
-
-def load_half_kernel(gate_w, up_w, gate_out, up_out, gate_sems, up_sems):
-    half = pl.ds(0, gate_out.shape[0])
-    copies = group_copies(gate_w.at[half], gate_out, gate_sems)
-    copies += group_copies(up_w.at[half], up_out, up_sems)
-    for copy in copies:
-        copy.wait()
-
-
-def rows_kernel(slot_ref, *refs):
-    slot_gates_ref, sources, refs = refs[0], refs[1:7], refs[7:]
-    gate_first, up_first, gate_w, up_w, grads_ref = refs[:5]
-    out_refs, refs = refs[5 : 5 + 2 * LINES], refs[5 + 2 * LINES :]
-    inputs_here, gate_here, up_here, grads_here, rows_ref, sum_ref, outs_here = refs[:7]
-    input_sems, gate_sems, up_sems, grad_sems, out_sems = refs[7:]
+def sum_rows(part, start, local_count, slot_ref, rows, slots):
+    experts = range(start, start + local_count)
+    hot = jnp.concatenate(
+        [h.astype(jnp.bfloat16) for h in hot_part(slot_ref, experts, part, slots)]
+    )
+    return lax.dot_general(
+        hot, rows, (((0,), (0,)), ((), ())), preferred_element_type=jnp.float32
+    )
+
+
+def give_out(total, outs_here, out_refs, out_sems):
+    rows = total.shape[0] // len(out_refs)
+    for i in range(len(out_refs)):
+        outs_here[i] = total[i * rows : (i + 1) * rows].astype(jnp.bfloat16)
+    return start_all(
+        [
+            pltpu.make_async_copy(outs_here.at[i], out_ref, out_sems.at[i])
+            for i, out_ref in enumerate(out_refs)
+        ]
+    )
+
+
+def rows_kernel(start, slot_ref, slot_gates_ref, *refs):
+    sources, gate_w, up_w, refs = refs[:6], refs[6], refs[7], refs[8:]
+    last = start > 0
+    if last:
+        before_ref, refs = refs[0], refs[1:]
+    grads_ref, near_ref, refs = refs[0], refs[1], refs[2:]
+    if last:
+        out_refs, refs = refs[:LINES], refs[LINES:]
+        outs_here, out_sems = refs[-2:]
+    else:
+        sum_ref, refs = refs[0], refs[1:]
+    inputs_here, gate_here, up_here, grads_here, rows_ref = refs[:5]
+    input_sems, gate_sems, up_sems, grads_sem, near_sem = refs[5:10]
     local_count, slots, hidden = inputs_here.shape[1:]
-    outs = [(outs_here.at[m], out, out_sems.at[m]) for m, out in enumerate(out_refs)]
-    copies = []
     groups = input_sems.shape[1]
     group = local_count // groups
-    half = gate_first.shape[0]
-    rest = pl.ds(half, local_count - half)
     arrivals = []
     for i in range(groups):
-        here = pl.ds(i * group, group)
-        arrivals.append(
-            start_all(
-                [
-                    pltpu.make_async_copy(
-                        source.at[here], inputs_here.at[j, here], input_sems.at[j, i]
-                    )
-                    for j, source in enumerate(sources)
-                ]
-            )
-        )
-    gate_ws = group_copies(gate_w.at[rest], gate_here, gate_sems)
-    up_ws = group_copies(up_w.at[rest], up_here, up_sems)
+        here, there = pl.ds(i * group, group), pl.ds(start + i * group, group)
+        moves = [
+            pltpu.make_async_copy(source.at[here], inputs_here.at[j, here], input_sems.at[j, i])
+            for j, source in enumerate(sources)
+        ]
+        moves += [
+            pltpu.make_async_copy(gate_w.at[there], gate_here.at[here], gate_sems.at[i]),
+            pltpu.make_async_copy(up_w.at[there], up_here.at[here], up_sems.at[i]),
+        ]
+        arrivals.append(start_all(moves))
     for i in range(groups):
         for copy in arrivals[i]:
             copy.wait()
@@ -494,37 +468,48 @@
             pre_up = inputs_here[2, e] + inputs_here[3, e]
             raw = inputs_here[4, e] + inputs_here[5, e]
             sigmoid = jax.nn.sigmoid(pre_gate)
-            scaled = slot_gates_ref[e, :, :1] * raw * sigmoid
+            scaled = slot_gates_ref[start + e, :, :1] * raw * sigmoid
             grad_gate = (scaled * pre_up * (1.0 + pre_gate * (1.0 - sigmoid))).astype(jnp.bfloat16)
             grad_up = (scaled * pre_gate).astype(jnp.bfloat16)
             grads_here[e, :, :hidden] = grad_gate
             grads_here[e, :, hidden:] = grad_up
-            if e < half:
-                gate_e, up_e = gate_first[e], up_first[e]
-            else:
-                span = half // len(gate_ws)
-                if (e - half) % span == 0:
-                    gate_ws[(e - half) // span].wait()
-                    up_ws[(e - half) // span].wait()
-                gate_e, up_e = gate_here[e - half], up_here[e - half]
-            row = jnp.dot(grad_gate, gate_e, preferred_element_type=jnp.float32)
-            row += lax.dot_general(
-                grad_up, up_e, (((1,), (1,)), ((), ())), preferred_element_type=jnp.float32
+            turned = (((1,), (1,)), ((), ()))
+            row = lax.dot_general(
+                grad_gate, gate_here[e], turned, preferred_element_type=jnp.float32
             )
+            row += lax.dot_general(grad_up, up_here[e], turned, preferred_element_type=jnp.float32)
             keep_row(row.astype(jnp.bfloat16), e, rows_ref)
-        if (i + 1) % (groups // 2) == 0:
-            last = (i + 1) * group
-            experts = range(last - local_count // 2, last)
-            here = pl.ds(experts[0], len(experts))
-            copies += start_all(
-                [
-                    pltpu.make_async_copy(
-                        grads_here.at[here], grads_ref.at[here], grad_sems.at[i // (groups // 2)]
-                    )
-                ]
-            )
-            copies += combine(slot_ref, experts, rows_ref, sum_ref, outs, slots)
+    copies = start_all(
+        [
+            pltpu.make_async_copy(grads_here, grads_ref, grads_sem),
+            pltpu.make_async_copy(rows_ref.at[0], near_ref, near_sem),
+        ]
+    )
+    total = sum_rows(1, start, local_count, slot_ref, rows_ref[1], slots)
+    if last:
+        copies += give_out(total + before_ref[...], outs_here, out_refs, out_sems)
+    else:
+        sum_ref[...] = total
     for copy in copies:
+        copy.wait()
+
+
+def near_kernel(slot_ref, *refs):
+    rows_refs, out_refs = refs[:HALVES], refs[HALVES : HALVES + LINES]
+    rows_here, outs_here, row_sems, out_sems = refs[HALVES + LINES :]
+    count = rows_here.shape[0] // HALVES
+    copies = start_all(
+        [
+            pltpu.make_async_copy(ref, rows_here.at[pl.ds(i * count, count)], row_sems.at[i])
+            for i, ref in enumerate(rows_refs)
+        ]
+    )
+    for copy in copies:
+        copy.wait()
+    local_count = slot_ref.shape[0]
+    slots = PARTS * rows_here.shape[0] // local_count
+    total = sum_rows(0, 0, local_count, slot_ref, rows_here[...], slots)
+    for copy in give_out(total, outs_here, out_refs, out_sems):
         copy.wait()
 
 
@@ -590,35 +575,18 @@
     x_here = pltpu.VMEM(x_shape.shape, bf16)
     w_here, down_here = pltpu.VMEM(w_gate.shape, bf16), pltpu.VMEM(w_down.shape, bf16)
     pre_shape = jax.ShapeDtypeStruct((local_count, slots, hidden), f32)
-    in_hbm_shape = pltpu.HBM(pre_shape.shape, f32)
+    half = local_count // HALVES
+    part_of_pre = pltpu.HBM((half, slots, hidden), f32)
     pre_here = pltpu.VMEM(pre_shape.shape, f32)
     batch = 2 if local_count % 2 == 0 else 1
 
     def batched(*shape):
         return pl.BlockSpec((batch,) + shape, lambda e: (e, 0, 0))
 
-    def turned(weights):
-        _, rows, columns = weights.shape
-        shape = (local_count, columns, rows)
-        return pl.pallas_call(
-            turn_kernel,
-            out_shape=pltpu.HBM(shape, bf16),
-            in_specs=[memory],
-            out_specs=memory,
-            scratch_shapes=[w_here, pltpu.VMEM(shape, bf16), w_sems, w_sems],
-            compiler_params=params(26),
-            cost_estimate=cost(0, 2 * weight_bytes),
-            name="turn",
-        )(in_hbm(weights))
-
     made = {}
 
     def beside_gather(turn, info, pieces):
-        if turn == 0:
-            (gate_w,) = tie([w_gate], info)
-            made["gate"] = turned(gate_w)
-            return [made["gate"]]
-        if turn == 2:
+        if turn == 1:
             (gate_w,) = tie([w_gate], *pieces)
             made["loaded"] = pl.pallas_call(
                 load_kernel,
@@ -663,11 +631,11 @@
     pieces = gather_rows(jnp.stack([tokens, out_grad]), info, at_end, beside_gather)
     slot_of = made["slots"]
 
-    x, gate_part, up_part = pl.pallas_call(
+    x, *pre_parts = pl.pallas_call(
         pre_kernel,
-        out_shape=(x_shape, in_hbm_shape, in_hbm_shape),
+        out_shape=(x_shape,) + (part_of_pre,) * (2 * HALVES),
         in_specs=[vmem] + [memory] * 5 + [vmem, memory],
-        out_specs=(memory,) * 3,
+        out_specs=(memory,) * (1 + 2 * HALVES),
         scratch_shapes=[rows_here, x_here, w_here, pre_here, pre_here]
         + [piece_sems, copies, w_sems, copies, w_sems, w_sems],
         compiler_params=params(24),
@@ -680,68 +648,100 @@
         in_vmem(made["loaded"]),
         in_hbm(w_up),
     )
+    gate_parts, up_parts = pre_parts[:HALVES], pre_parts[HALVES:]
     grad_pieces = tie(pieces[8:], x)
-    raw_part = pl.pallas_call(
-        down_kernel,
-        out_shape=in_hbm_shape,
-        in_specs=[vmem] + [memory] * 6,
-        out_specs=memory,
-        scratch_shapes=[rows_here, x_here, down_here, pre_here]
-        + [piece_sems, copies, w_sems, w_sems],
-        compiler_params=params(19),
-        cost_estimate=cost(hot_flops / 2 + matmul_flops, 1.4 * weight_bytes),
-        name="down",
-    )(slot_of, *pieces[4:6], *grad_pieces, made["grad_x"], in_hbm(w_down))
-    gate_other, up_other = across_cores(gate_part), across_cores(up_part)
-    raw_other = across_cores(raw_part)
-    half = local_count // 2
-    gate_half, up_half = (half, hidden, half_width), (half, half_width, hidden)
-    gate_w, up_w = tie((made["gate"], w_up), raw_part, gate_other, up_other)
-    gate_first, up_first = pl.pallas_call(
-        load_half_kernel,
-        out_shape=(pltpu.VMEM(gate_half, bf16), pltpu.VMEM(up_half, bf16)),
-        in_specs=[memory] * 2,
-        out_specs=(memory,) * 2,
-        scratch_shapes=[w_sems, w_sems],
-        compiler_params=params(40),
-        cost_estimate=cost(0, weight_bytes),
-        name="load_half",
-    )(in_hbm(gate_w), in_hbm(up_w))
-    grads, *partial = pl.pallas_call(
-        rows_kernel,
-        out_shape=(jax.ShapeDtypeStruct((local_count, slots, 2 * hidden), bf16),)
-        + (jax.ShapeDtypeStruct((chunk, half_width), bf16),) * ep_count,
-        in_specs=[vmem] * 2 + [memory] * 6 + [vmem] * 2 + [memory] * 2,
-        out_specs=(memory,) * (1 + ep_count),
-        scratch_shapes=[
-            pltpu.VMEM((6,) + pre_shape.shape, f32),
-            pltpu.VMEM(gate_half, bf16),
-            pltpu.VMEM(up_half, bf16),
-            pltpu.VMEM((local_count, slots, 2 * hidden), bf16),
-            pltpu.VMEM((PARTS, local_count * part_slots, half_width), bf16),
-            pltpu.VMEM((token_count, half_width), f32),
-            pltpu.VMEM((ep_count, chunk, half_width), bf16),
-            copies((6, 2 * groups)),
+
+    def down(start, pieces):
+        return pl.pallas_call(
+            functools.partial(down_kernel, start),
+            out_shape=part_of_pre,
+            in_specs=[vmem] + [memory] * 6,
+            out_specs=memory,
+            scratch_shapes=[
+                rows_here,
+                pltpu.VMEM((half, slots, half_width), bf16),
+                pltpu.VMEM((half, hidden, half_width), bf16),
+                pltpu.VMEM((half, slots, hidden), f32),
+            ]
+            + [piece_sems, copies, w_sems, w_sems],
+            compiler_params=params(12),
+            cost_estimate=cost((hot_flops / 2 + matmul_flops) / HALVES, 1.4 * weight_bytes / HALVES),
+            name="down",
+        )(slot_of, *pieces, made["grad_x"], in_hbm(w_down))
+
+    piece_shape = jax.ShapeDtypeStruct((chunk, half_width), bf16)
+    pieces_here = [pltpu.VMEM((LINES, chunk, half_width), bf16), copies((LINES,))]
+
+    def rows(number, sources, before):
+        scratch = [
+            pltpu.VMEM((6, half, slots, hidden), f32),
+            pltpu.VMEM((half, half_width, hidden), bf16),
+            pltpu.VMEM((half, half_width, hidden), bf16),
+            pltpu.VMEM((half, slots, 2 * hidden), bf16),
+            pltpu.VMEM((PARTS, half * part_slots, half_width), bf16),
+            copies((6, groups)),
             w_sems,
             w_sems,
-            copies((2,)),
-            copies((ep_count,)),
+            copies,
+            copies,
+        ]
+        out_shape = [
+            jax.ShapeDtypeStruct((half, slots, 2 * hidden), bf16),
+            jax.ShapeDtypeStruct((half * part_slots, half_width), bf16),
+        ]
+        if before:
+            out_shape += [piece_shape] * LINES
+            out_specs = (memory,) * (2 + LINES)
+            scratch += pieces_here
+        else:
+            out_shape += [pltpu.VMEM((part_tokens, half_width), f32)]
+            out_specs = (memory, memory, vmem)
+        return pl.pallas_call(
+            functools.partial(rows_kernel, number * half),
+            out_shape=tuple(out_shape),
+            in_specs=[vmem] * 2 + [memory] * 8 + [vmem] * len(before),
+            out_specs=out_specs,
+            scratch_shapes=scratch,
+            compiler_params=params(30),
+            cost_estimate=cost(
+                (2 * matmul_flops + hot_flops) / HALVES, 3.1 * weight_bytes / HALVES
+            ),
+            name="rows",
+        )(slot_of, made["slot_gates"], *sources, in_hbm(w_gate), in_hbm(w_up), *before)
+
+    def both(value):
+        return [value, across_cores(value)]
+
+    pre_first = [*both(gate_parts[0]), *both(up_parts[0])]
+    raw_first = down(0, [*pieces[4:6], *grad_pieces])
+    sent = both(raw_first)
+    gate_last, up_last, *last_pieces = tie(
+        [gate_parts[1], up_parts[1], *pieces[4:6], *grad_pieces], raw_first
+    )
+    pre_last = [*both(gate_last), *both(up_last)]
+    raw_last = down(half, last_pieces)
+    sent[1], pre_first[1], pre_first[3] = tie((sent[1], pre_first[1], pre_first[3]), raw_last)
+    grads_first, near_first, sums = rows(0, [*pre_first, *sent], [])
+    last = [*pre_last, *both(raw_last)]
+    grads_last, near_last, *far_sums = rows(1, last, [in_vmem(sums)])
+    grads = [grads_first, grads_last]
+    near_first, near_last = tie((near_first, near_last), *far_sums)
+    near_sums = pl.pallas_call(
+        near_kernel,
+        out_shape=(piece_shape,) * LINES,
+        in_specs=[vmem] + [memory] * HALVES,
+        out_specs=(memory,) * LINES,
+        scratch_shapes=[
+            pltpu.VMEM((local_count * part_slots, half_width), bf16),
+            pieces_here[0],
+            copies((HALVES,)),
+            pieces_here[1],
         ],
-        compiler_params=params(40),
-        cost_estimate=cost(2 * matmul_flops + hot_flops, 2 * weight_bytes),
-        name="rows",
-    )(
-        slot_of,
-        made["slot_gates"],
-        *[
-            in_hbm(value)
-            for value in (gate_part, gate_other, up_part, up_other, raw_part, raw_other)
-        ],
-        in_vmem(gate_first),
-        in_vmem(up_first),
-        in_hbm(made["gate"]),
-        in_hbm(w_up),
-    )
+        compiler_params=params(12),
+        cost_estimate=cost(hot_flops / 2, weight_bytes / 3),
+        name="near",
+    )(slot_of, near_first, near_last)
+    partial = [*near_sums, *far_sums]
 
     turns = LINES
     group = local_count // turns
@@ -753,13 +753,13 @@
 
     def meanwhile(turn, values):
         first = turn * group
-        operands = [x, grads]
+        operands = [x, grads[first // half]]
         operands = tie(operands, *(held or partial))
         weight_grads[:] = pl.pallas_call(
             weight_kernel,
             grid=(group,),
             out_shape=(weight_shape, weight_shape),
-            in_specs=[block_of(first, slots, half_width), block_of(first, slots, 2 * hidden)]
+            in_specs=[block_of(first, slots, half_width), block_of(first % half, slots, 2 * hidden)]
             + [memory] * len(weight_grads),
             out_specs=(block_of(first, half_width, hidden), block_of(first, half_width, hidden)),
             input_output_aliases={2 + i: i for i in range(len(weight_grads))},

time: 140 us -> 136 us (0.971)
  Pallas kernels: 68.8 us -> 59.5 us
  starting transfers between devices: 35.1 us -> 40.6 us
  waiting for transfers between devices: 22.5 us -> 26.7 us
  local copies, waits for them, and re-layouts: 4.14 us -> 0.35 us
    pallas_call x5 -> x6, Pallas kernels: 44.7 us -> 35.4 us  [the longest x2 16.8 us: rows(): pl.pallas_call(functools.partial(rows_kernel, number * half), out_shape=t...]
    ppermute x10, starting transfers between devices: 19.5 us -> 24.1 us  [along_line(): return lax.ppermute(value, 'ep', pairs)]
    unnamed x12 -> x14, local copies, waits for them, and re-layouts: 3.82 us -> 0.03 us
    ppermute x9, waiting for transfers between devices: 4.6 us -> 7.61 us  [across_pair(): return lax.ppermute(value, 'ep', [(i, i ^ 1) for i in range(2 * LINES)])]
  transfers between devices with their start and end apart: 27 -> 30, of which waited for: 13 -> 12; matrix products, arithmetic and copies ran while one was open for 3% -> 4% of each run, Pallas kernels for 39% -> 34%
where the time goes in v3:
time: 136 us
  Pallas kernels  59.5 us (44%)
  starting transfers between devices  40.6 us (30%)
  waiting for transfers between devices  26.7 us (20%)
  other arithmetic  7.62 us (6%)
    ppermute x10, starting transfers between devices, along_line(): return lax.ppermute(value, 'ep', pairs)  24.1 us
    pallas_call x2, Pallas kernels, rows(): pl.pallas_call(functools.partial(rows_kernel, number * half), out_shape=t...  16.8 us
    pallas_call x4, Pallas kernels, meanwhile(): pl.pallas_call(weight_kernel, grid=(group,), out_shape=(weight_shape, wei...  16.4 us
    pallas_call x2, Pallas kernels, down(): pl.pallas_call(functools.partial(down_kernel, start), out_shape=part_of_p...  9.8 us
    ppermute x9, starting transfers between devices, across_pair(): return lax.ppermute(value, 'ep', [(i, i ^ 1) for i in range(2 * LINES)])  9.57 us
    ppermute x10, waiting for transfers between devices, along_line(): return lax.ppermute(value, 'ep', pairs)  8.96 us
    ppermute x4, waiting for transfers between devices, widen(): lax.ppermute(info, 'ep', [(i, i ^ bit) for i in range(2 * LINES)])  8.92 us
    ppermute x9, waiting for transfers between devices, across_pair(): return lax.ppermute(value, 'ep', [(i, i ^ 1) for i in range(2 * LINES)])  7.61 us
  transfers between devices with their start and end apart: 30, of which 12 were waited for; matrix products, arithmetic and copies ran while one was open for 4% of the time, Pallas kernels for 34%

profile of v3, /device:TPU:12, one launch (start us, length us, event | category | flops | bytes accessed | tf_op | source)
XLA Modules:
  0.0 135.8 jit_solution(5524756549638394217)
XLA Ops:
  3.3 3.5 %collective-permute-start.1 = (bf16[2,128,1024]{2,1,0:T(8,128)(2,1)S(1)}, bf16[2,128,1024]{2,1,0:T(8,128)(2,1)S(1)}, u32[]{:S(2)}, u32[]{:S(2)}) collective-permute-start(bf16[2,128,1024]{2,1,0:T(8,128)(2,1)S(1)} %pad_maximum_fusion.refs_0_), channel_id=1, source_target_pairs={{4,8},{6,10},{8,4},{10,6},{5,9},{7,11},{9,5},{11,7},{20,24},{22,26... | collective-permute-start | bytes 1572872 | tf_op jit(solution)/shard_map/ppermute | solution.py:156
  11.1 5.1 %collective-permute-done.4 = bf16[8,16,128]{2,1,0:T(8,128)(2,1)S(1)} collective-permute-done((bf16[8,16,128]{2,1,0:T(8,128)(2,1)S(1)}, bf16[8,16,128]{2,1,0:T(8,128)(2,1)S(1)}, u32[]{:S(2)}, u32[]{:S(2)}) %collective-permute-start.4) | collective-permute-done | bytes 32800 | tf_op jit(solution)/shard_map/ppermute | solution.py:175
  22.6 2.0 %collective-permute-done.5 = bf16[8,16,128]{2,1,0:T(8,128)(2,1)S(1)} collective-permute-done((bf16[8,16,128]{2,1,0:T(8,128)(2,1)S(1)}, bf16[8,16,128]{2,1,0:T(8,128)(2,1)S(1)}, u32[]{:S(2)}, u32[]{:S(2)}) %collective-permute-start.5) | collective-permute-done | bytes 32800 | tf_op jit(solution)/shard_map/ppermute | solution.py:175
  24.7 3.7 %collective-permute-start.8 = (bf16[2,128,1024]{2,1,0:T(8,128)(2,1)S(1)}, bf16[2,128,1024]{2,1,0:T(8,128)(2,1)S(1)}, u32[]{:S(2)}, u32[]{:S(2)}) collective-permute-start(bf16[2,128,1024]{2,1,0:T(8,128)(2,1)S(1)} %collective-permute-done.1), channel_id=1, source_target_pairs={{4,0},{6,2},{8,12},{10,14},{5,1},{7,3},{9,13},{11,15},{20,16},{22,... | collective-permute-start | bytes 1572872 | tf_op jit(solution)/shard_map/ppermute | solution.py:156
  29.8 4.6 %collective-permute-start.9 = (bf16[2,128,1024]{2,1,0:T(8,128)(2,1)S(1)}, bf16[2,128,1024]{2,1,0:T(8,128)(2,1)}, u32[]{:S(2)}, u32[]{:S(2)}) collective-permute-start(bf16[2,128,1024]{2,1,0:T(8,128)(2,1)S(1)} %collective-permute-done.refs_2_), channel_id=1, source_target_pairs={{4,8},{6,10},{8,4},{10,6},{5,9},{7,11},{9,5},{11,7},{20,24},{22,26... | collective-permute-start | bytes 1572872 | tf_op jit(solution)/shard_map/ppermute | solution.py:156
  34.5 2.9 %collective-permute-done.8 = bf16[2,128,1024]{2,1,0:T(8,128)(2,1)S(1)} collective-permute-done((bf16[2,128,1024]{2,1,0:T(8,128)(2,1)S(1)}, bf16[2,128,1024]{2,1,0:T(8,128)(2,1)S(1)}, u32[]{:S(2)}, u32[]{:S(2)}) %collective-permute-start.8) | collective-permute-done | bytes 524320 | tf_op jit(solution)/shard_map/ppermute | solution.py:156
  37.4 2.3 %collective-permute-done.10.refs_3_ = bf16[2,128,1024]{2,1,0:T(8,128)(2,1)S(1)} collective-permute-done((bf16[2,128,1024]{2,1,0:T(8,128)(2,1)S(1)}, bf16[2,128,1024]{2,1,0:T(8,128)(2,1)S(1)}, u32[]{:S(2)}, u32[]{:S(2)}) %collective-permute-start.10) | collective-permute-done | bytes 524320 | tf_op jit(solution)/shard_map/ppermute | solution.py:160
  39.7 3.1 %collective-permute-done.9 = bf16[2,128,1024]{2,1,0:T(8,128)(2,1)} collective-permute-done((bf16[2,128,1024]{2,1,0:T(8,128)(2,1)S(1)}, bf16[2,128,1024]{2,1,0:T(8,128)(2,1)}, u32[]{:S(2)}, u32[]{:S(2)}) %collective-permute-start.9) | collective-permute-done | bytes 524320 | tf_op jit(solution)/shard_map/ppermute | solution.py:156
  43.6 2.1 %collective-permute-start.11 = (bf16[2,128,1024]{2,1,0:T(8,128)(2,1)}, bf16[2,128,1024]{2,1,0:T(8,128)(2,1)}, u32[]{:S(2)}, u32[]{:S(2)}) collective-permute-start(bf16[2,128,1024]{2,1,0:T(8,128)(2,1)} %collective-permute-done.9), channel_id=1, source_target_pairs={{4,0},{6,2},{8,12},{10,14},{5,1},{7,3},{9,13},{11,15},{20,16},{22,... | collective-permute-start | bytes 1572872 | tf_op jit(solution)/shard_map/ppermute | solution.py:156
  47.4 2.3 %first_slots.1 = (bf16[16,48,1024]{2,1,0:T(8,128)(2,1)S(1)}, bf16[16,48,1024]{2,1,0:T(8,128)(2,1)S(1)}, f32[16,96,128]{2,1,0:T(8,128)S(1)}) custom-call(s32[16,1024]{1,0:T(8,128)S(1)} %get-tuple-element.85.slot_ref, f32[16,1024]{1,0:T(8,128)S(1)} %get-tuple-element.86.gates_ref, bf16[2,128,1024]{2,1,0:T(8,128)(2,1)S(1)} %pad_maximum_fusion.refs_0_, ...), custom_call_target="tpu_custom_call" | custom-call | flops 1610612736 | bytes 6291456 | tf_op jit(solution)/shard_map/first_slots/pallas_call | solution.py:615
  49.7 3.5 %collective-permute-done.12.refs_1_ = bf16[2,128,1024]{2,1,0:T(8,128)(2,1)S(1)} collective-permute-done((bf16[2,128,1024]{2,1,0:T(8,128)(2,1)S(1)}, bf16[2,128,1024]{2,1,0:T(8,128)(2,1)S(1)}, u32[]{:S(2)}, u32[]{:S(2)}) %collective-permute-start.12) | collective-permute-done | bytes 524320 | tf_op jit(solution)/shard_map/ppermute | solution.py:160
  57.5 4.7 %load.1.refs_5_ = bf16[16,1024,384]{2,1,0:T(8,128)(2,1)S(1)} custom-call(bf16[16,1024,384]{2,1,0:T(8,128)(2,1)} %refs_6_.5), custom_call_target="tpu_custom_call" | custom-call | bytes 12582912 | tf_op jit(solution)/shard_map/load/pallas_call | solution.py:591
  62.2 7.6 %pre.1 = (bf16[16,96,1024]{2,1,0:T(8,128)(2,1)S(1)}, f32[8,96,384]{2,1,0:T(8,128)}, f32[8,96,384]{2,1,0:T(8,128)}, f32[8,96,384]{2,1,0:T(8,128)}, f32[8,96,384]{2,1,0:T(8,128)}) custom-call(s32[16,1024]{1,0:T(8,128)S(1)} %get-tuple-element.85.slot_ref, bf16[2,128,1024]{2,1,0:T(8,128)(2,1)S(1)} %broadcast_select_fusion.refs_0_, ...), custom_call_target="tpu_custom_call" | custom-call | flops 3221225472 | bytes 35232152 | tf_op jit(solution)/shard_map/pre/pallas_call | solution.py:634
  69.8 4.9 %down.2.refs_4_ = f32[8,96,384]{2,1,0:T(8,128)} custom-call(s32[16,1024]{1,0:T(8,128)S(1)} %get-tuple-element.85.slot_ref, bf16[2,128,1024]{2,1,0:T(8,128)(2,1)S(1)} %broadcast_select_fusion.refs_0_, bf16[2,128,1024]{2,1,0:T(8,128)(2,1)S(1)} %collective-permute-done.12.refs_1_, bf16[128,1024]{1,0:T(8,128)(2,1)S(1)} %select_bitcast_fusion.refs_2_, ...), custom_call_target="tpu_custom_call" | custom-call | flops 1006632960 | bytes 8808038 | tf_op jit(solution)/shard_map/down/pallas_call | solution.py:655
  75.4 4.9 %down.3.refs_4_ = f32[8,96,384]{2,1,0:T(8,128)} custom-call(s32[16,1024]{1,0:T(8,128)S(1)} %get-tuple-element.85.slot_ref, bf16[2,128,1024]{2,1,0:T(8,128)(2,1)S(1)} %broadcast_select_fusion.refs_0_, bf16[2,128,1024]{2,1,0:T(8,128)(2,1)S(1)} %collective-permute-done.12.refs_1_, bf16[128,1024]{1,0:T(8,128)(2,1)S(1)} %select_bitcast_fusion.refs_2_, ...), custom_call_target="tpu_custom_call" | custom-call | flops 1006632960 | bytes 8808038 | tf_op jit(solution)/shard_map/down/pallas_call | solution.py:655
  81.4 8.3 %rows.2 = (bf16[8,96,768]{2,1,0:T(8,128)(2,1)S(1)}, bf16[384,1024]{1,0:T(8,128)(2,1)S(1)}, f32[512,1024]{1,0:T(8,128)S(1)}) custom-call(s32[16,1024]{1,0:T(8,128)S(1)} %get-tuple-element.85.slot_ref, f32[16,96,128]{2,1,0:T(8,128)S(1)} %get-tuple-element.91.slot_gates_ref, f32[8,96,384]{2,1,0:T(8,128)S(1)} %copy-done.4, ...), custom_call_target="tpu_custom_call" | custom-call | flops 2013265920 | bytes 19503512 | tf_op jit(solution)/shard_map/rows/pallas_call | solution.py:699
  89.7 8.4 %rows.3 = (bf16[8,96,768]{2,1,0:T(8,128)(2,1)S(1)}, bf16[384,1024]{1,0:T(8,128)(2,1)S(1)}, bf16[128,1024]{1,0:T(8,128)(2,1)S(1)}, bf16[128,1024]{1,0:T(8,128)(2,...) custom-call(s32[16,1024]{1,0:T(8,128)S(1)} %get-tuple-element.85.slot_ref, ...), custom_call_target="tpu_custom_call" | custom-call | flops 2013265920 | bytes 19503512 | tf_op jit(solution)/shard_map/rows/pallas_call | solution.py:699
  101.5 4.1 %weight_grads.4 = (bf16[16,1024,384]{2,1,0:T(8,128)(2,1)}, bf16[16,1024,384]{2,1,0:T(8,128)(2,1)}) custom-call(bf16[16,96,1024]{2,1,0:T(8,128)(2,1)S(1)} %get-tuple-element.154.x_ref, bf16[8,96,768]{2,1,0:T(8,128)(2,1)S(1)} %get-tuple-element.137.grads_ref), custom_call_target="tpu_custom_call" | custom-call | flops 603979776 | bytes 7864320 | tf_op jit(solution)/shard_map/weight_grads/pallas_call | solution.py:758
  109.5 4.1 %weight_grads.5 = (bf16[16,1024,384]{2,1,0:T(8,128)(2,1)}, bf16[16,1024,384]{2,1,0:T(8,128)(2,1)}) custom-call(bf16[16,96,1024]{2,1,0:T(8,128)(2,1)S(1)} %get-tuple-element.154.x_ref, bf16[8,96,768]{2,1,0:T(8,128)(2,1)S(1)} %get-tuple-element.137.grads_ref, ...), custom_call_target="tpu_custom_call", output_to_operand_aliasing={{0}: (2, {}), {1}: (3, {})} | custom-call | flops 603979776 | bytes 7864320 | tf_op jit(solution)/shard_map/weight_grads/pallas_call | solution.py:758
  113.6 2.3 %collective-permute-done.22 = bf16[128,1024]{1,0:T(8,128)(2,1)S(1)} collective-permute-done((bf16[128,1024]{1,0:T(8,128)(2,1)S(1)}, bf16[128,1024]{1,0:T(8,128)(2,1)S(1)}, u32[]{:S(2)}, u32[]{:S(2)}) %collective-permute-start.22) | collective-permute-done | bytes 262176 | tf_op jit(solution)/shard_map/ppermute | solution.py:156
  117.5 4.1 %collective-permute-start.24 = (bf16[128,1024]{1,0:T(8,128)(2,1)S(1)}, bf16[128,1024]{1,0:T(8,128)(2,1)S(1)}, u32[]{:S(2)}, u32[]{:S(2)}) collective-permute-start(bf16[128,1024]{1,0:T(8,128)(2,1)S(1)} %add_convert_fusion.3), channel_id=1, source_target_pairs={{4,8},{6,10},{8,4},{10,6},{5,9},{7,11},{9,5},{11,7},{20,24},{22,26... | collective-permute-start | bytes 786440 | tf_op jit(solution)/shard_map/ppermute | solution.py:156
  122.2 4.1 %weight_grads.6 = (bf16[16,1024,384]{2,1,0:T(8,128)(2,1)}, bf16[16,1024,384]{2,1,0:T(8,128)(2,1)}) custom-call(bf16[16,96,1024]{2,1,0:T(8,128)(2,1)S(1)} %get-tuple-element.154.x_ref, bf16[8,96,768]{2,1,0:T(8,128)(2,1)S(1)} %get-tuple-element.155.grads_ref, ...), custom_call_target="tpu_custom_call", output_to_operand_aliasing={{0}: (2, {}), {1}: (3, {})} | custom-call | flops 603979776 | bytes 7864320 | tf_op jit(solution)/shard_map/weight_grads/pallas_call | solution.py:758
  126.7 3.5 %collective-permute-start.27 = (bf16[128,1024]{1,0:T(8,128)(2,1)S(1)}, bf16[128,1024]{1,0:T(8,128)(2,1)S(1)}, u32[]{:S(2)}, u32[]{:S(2)}) collective-permute-start(bf16[128,1024]{1,0:T(8,128)(2,1)S(1)} %add_convert_fusion.2), channel_id=1, source_target_pairs={{4,8},{6,10},{8,4},{10,6},{5,9},{7,11},{9,5},{11,7},{20,24},{22,26... | collective-permute-start | bytes 786440 | tf_op jit(solution)/shard_map/ppermute | solution.py:156
  130.1 4.1 %weight_grads.7 = (bf16[16,1024,384]{2,1,0:T(8,128)(2,1)}, bf16[16,1024,384]{2,1,0:T(8,128)(2,1)}) custom-call(bf16[16,96,1024]{2,1,0:T(8,128)(2,1)S(1)} %get-tuple-element.154.x_ref, bf16[8,96,768]{2,1,0:T(8,128)(2,1)S(1)} %get-tuple-element.155.grads_ref, ...), custom_call_target="tpu_custom_call", output_to_operand_aliasing={{0}: (2, {}), {1}: (3, {})} | custom-call | flops 603979776 | bytes 7864320 | tf_op jit(solution)/shard_map/weight_grads/pallas_call | solution.py:758
  (85 shorter events, 34.7 us)
Async XLA Ops:
  1.7 22.9 %collective-permute-start.2 = (bf16[2,128,1024]{2,1,0:T(8,128)(2,1)S(1)}, bf16[2,128,1024]{2,1,0:T(8,128)(2,1)S(1)}, u32[]{:S(2)}, u32[]{:S(2)}) collective-permute-start(bf16[2,128,1024]{2,1,0:T(8,128)(2,1)S(1)} %pad_maximum_fusion.refs_0_), channel_id=1, source_target_pairs={{0,2},{2,0},{4,6},{6,4},{8,10},{10,8},{12,14},{14,12},{1,3},{3,1},... | collective-permute-start | bytes 1572872 | tf_op jit(solution)/shard_map/ppermute | solution.py:160
  3.3 21.4 %collective-permute-start.1 = (bf16[2,128,1024]{2,1,0:T(8,128)(2,1)S(1)}, bf16[2,128,1024]{2,1,0:T(8,128)(2,1)S(1)}, u32[]{:S(2)}, u32[]{:S(2)}) collective-permute-start(bf16[2,128,1024]{2,1,0:T(8,128)(2,1)S(1)} %pad_maximum_fusion.refs_0_), channel_id=1, source_target_pairs={{4,8},{6,10},{8,4},{10,6},{5,9},{7,11},{9,5},{11,7},{20,24},{22,26... | collective-permute-start | bytes 1572872 | tf_op jit(solution)/shard_map/ppermute | solution.py:156
  6.7 17.9 %collective-permute-start = (bf16[2,128,1024]{2,1,0:T(8,128)(2,1)S(1)}, bf16[2,128,1024]{2,1,0:T(8,128)(2,1)S(1)}, u32[]{:S(2)}, u32[]{:S(2)}) collective-permute-start(bf16[2,128,1024]{2,1,0:T(8,128)(2,1)S(1)} %pad_maximum_fusion.refs_0_), channel_id=1, source_target_pairs={{0,4},{2,6},{4,0},{6,2},{8,12},{10,14},{12,8},{14,10},{1,5},{3,7},... | collective-permute-start | bytes 1572872 | tf_op jit(solution)/shard_map/ppermute | solution.py:156
  24.7 12.7 %collective-permute-start.8 = (bf16[2,128,1024]{2,1,0:T(8,128)(2,1)S(1)}, bf16[2,128,1024]{2,1,0:T(8,128)(2,1)S(1)}, u32[]{:S(2)}, u32[]{:S(2)}) collective-permute-start(bf16[2,128,1024]{2,1,0:T(8,128)(2,1)S(1)} %collective-permute-done.1), channel_id=1, source_target_pairs={{4,0},{6,2},{8,12},{10,14},{5,1},{7,3},{9,13},{11,15},{20,16},{22,... | collective-permute-start | bytes 1572872 | tf_op jit(solution)/shard_map/ppermute | solution.py:156
  28.3 11.4 %collective-permute-start.10 = (bf16[2,128,1024]{2,1,0:T(8,128)(2,1)S(1)}, bf16[2,128,1024]{2,1,0:T(8,128)(2,1)S(1)}, u32[]{:S(2)}, u32[]{:S(2)}) collective-permute-start(bf16[2,128,1024]{2,1,0:T(8,128)(2,1)S(1)} %collective-permute-done.refs_2_), channel_id=1, source_target_pairs={{0,2},{2,0},{4,6},{6,4},{8,10},{10,8},{12,14},{14,12},{1,3},{3,1},... | collective-permute-start | bytes 1572872 | tf_op jit(solution)/shard_map/ppermute | solution.py:160
  29.8 12.9 %collective-permute-start.9 = (bf16[2,128,1024]{2,1,0:T(8,128)(2,1)S(1)}, bf16[2,128,1024]{2,1,0:T(8,128)(2,1)}, u32[]{:S(2)}, u32[]{:S(2)}) collective-permute-start(bf16[2,128,1024]{2,1,0:T(8,128)(2,1)S(1)} %collective-permute-done.refs_2_), channel_id=1, source_target_pairs={{4,8},{6,10},{8,4},{10,6},{5,9},{7,11},{9,5},{11,7},{20,24},{22,26... | collective-permute-start | bytes 1572872 | tf_op jit(solution)/shard_map/ppermute | solution.py:156
  42.8 10.4 %collective-permute-start.12 = (bf16[2,128,1024]{2,1,0:T(8,128)(2,1)S(1)}, bf16[2,128,1024]{2,1,0:T(8,128)(2,1)S(1)}, u32[]{:S(2)}, u32[]{:S(2)}) collective-permute-start(bf16[2,128,1024]{2,1,0:T(8,128)(2,1)S(1)} %broadcast_select_fusion.refs_0_), channel_id=1, source_target_pairs={{0,2},{2,0},{4,6},{6,4},{8,10},{10,8},{12,14},{14,12},{1,3},{3,1},... | collective-permute-start | bytes 1572872 | tf_op jit(solution)/shard_map/ppermute | solution.py:160
  43.6 9.6 %collective-permute-start.11 = (bf16[2,128,1024]{2,1,0:T(8,128)(2,1)}, bf16[2,128,1024]{2,1,0:T(8,128)(2,1)}, u32[]{:S(2)}, u32[]{:S(2)}) collective-permute-start(bf16[2,128,1024]{2,1,0:T(8,128)(2,1)} %collective-permute-done.9), channel_id=1, source_target_pairs={{4,0},{6,2},{8,12},{10,14},{5,1},{7,3},{9,13},{11,15},{20,16},{22,... | collective-permute-start | bytes 1572872 | tf_op jit(solution)/shard_map/ppermute | solution.py:156
  54.3 7.9 %collective-permute-start.13 = (bf16[128,1024]{1,0:T(8,128)(2,1)S(1)}, bf16[128,1024]{1,0:T(8,128)(2,1)S(1)}, u32[]{:S(2)}, u32[]{:S(2)}) collective-permute-start(bf16[128,1024]{1,0:T(8,128)(2,1)S(1)} %select_bitcast_fusion.1.refs_2_), channel_id=1, source_target_pairs={{0,2},{2,0},{4,6},{6,4},{8,10},{10,8},{12,14},{14,12},{1,3},{3,1},... | collective-permute-start | bytes 786440 | tf_op jit(solution)/shard_map/ppermute | solution.py:160
  56.1 13.7 %collective-permute-start.14 = (bf16[128,1024]{1,0:T(8,128)(2,1)S(1)}, bf16[128,1024]{1,0:T(8,128)(2,1)S(1)}, u32[]{:S(2)}, u32[]{:S(2)}) collective-permute-start(bf16[128,1024]{1,0:T(8,128)(2,1)S(1)} %select_bitcast_fusion.refs_2_), channel_id=1, source_target_pairs={{0,2},{2,0},{4,6},{6,4},{8,10},{10,8},{12,14},{14,12},{1,3},{3,1},... | collective-permute-start | bytes 786440 | tf_op jit(solution)/shard_map/ppermute | solution.py:160
  74.7 6.2 %collective-permute-start.15 = (f32[8,96,384]{2,1,0:T(8,128)}, f32[8,96,384]{2,1,0:T(8,128)S(1)}, u32[]{:S(2)}, u32[]{:S(2)}) collective-permute-start(f32[8,96,384]{2,1,0:T(8,128)} %down.2.refs_4_), channel_id=1, source_target_pairs={{0,1},{1,0},{2,3},{3,2},{4,5},{5,4},{6,7},{7,6},{8,9},{9,8},{10,11... | collective-permute-start | bytes 3538952 | tf_op jit(solution)/shard_map/ppermute | solution.py:164
  74.8 6.5 %collective-permute-start.16 = (f32[8,96,384]{2,1,0:T(8,128)S(1)}, f32[8,96,384]{2,1,0:T(8,128)S(1)}, u32[]{:S(2)}, u32[]{:S(2)}) collective-permute-start(f32[8,96,384]{2,1,0:T(8,128)S(1)} %copy-done.4), channel_id=1, source_target_pairs={{0,1},{1,0},{2,3},{3,2},{4,5},{5,4},{6,7},{7,6},{8,9},{9,8},{10,11... | collective-permute-start | bytes 3538952 | tf_op jit(solution)/shard_map/ppermute | solution.py:164
  80.3 9.4 %collective-permute-start.20 = (f32[8,96,384]{2,1,0:T(8,128)}, f32[8,96,384]{2,1,0:T(8,128)S(1)}, u32[]{:S(2)}, u32[]{:S(2)}) collective-permute-start(f32[8,96,384]{2,1,0:T(8,128)} %down.3.refs_4_), channel_id=1, source_target_pairs={{0,1},{1,0},{2,3},{3,2},{4,5},{5,4},{6,7},{7,6},{8,9},{9,8},{10,11... | collective-permute-start | bytes 3538952 | tf_op jit(solution)/shard_map/ppermute | solution.py:164
  80.8 8.9 %collective-permute-start.18 = (f32[8,96,384]{2,1,0:T(8,128)S(1)}, f32[8,96,384]{2,1,0:T(8,128)S(1)}, u32[]{:S(2)}, u32[]{:S(2)}) collective-permute-start(f32[8,96,384]{2,1,0:T(8,128)S(1)} %copy-done.2), channel_id=1, source_target_pairs={{0,1},{1,0},{2,3},{3,2},{4,5},{5,4},{6,7},{7,6},{8,9},{9,8},{10,11... | collective-permute-start | bytes 3538952 | tf_op jit(solution)/shard_map/ppermute | solution.py:164
  80.9 8.8 %collective-permute-start.19 = (f32[8,96,384]{2,1,0:T(8,128)S(1)}, f32[8,96,384]{2,1,0:T(8,128)S(1)}, u32[]{:S(2)}, u32[]{:S(2)}) collective-permute-start(f32[8,96,384]{2,1,0:T(8,128)S(1)} %copy-done.3), channel_id=1, source_target_pairs={{0,1},{1,0},{2,3},{3,2},{4,5},{5,4},{6,7},{7,6},{8,9},{9,8},{10,11... | collective-permute-start | bytes 3538952 | tf_op jit(solution)/shard_map/ppermute | solution.py:164
  98.2 9.2 %collective-permute-start.21 = (bf16[128,1024]{1,0:T(8,128)(2,1)S(1)}, bf16[128,1024]{1,0:T(8,128)(2,1)S(1)}, u32[]{:S(2)}, u32[]{:S(2)}) collective-permute-start(bf16[128,1024]{1,0:T(8,128)(2,1)S(1)} %get-tuple-element.123), channel_id=1, source_target_pairs={{0,2},{2,0},{4,6},{6,4},{8,10},{10,8},{12,14},{14,12},{1,3},{3,1},... | collective-permute-start | bytes 786440 | tf_op jit(solution)/shard_map/ppermute | solution.py:160
  98.9 14.7 %collective-permute-start.23 = (bf16[128,1024]{1,0:T(8,128)(2,1)S(1)}, bf16[128,1024]{1,0:T(8,128)(2,1)S(1)}, u32[]{:S(2)}, u32[]{:S(2)}) collective-permute-start(bf16[128,1024]{1,0:T(8,128)(2,1)S(1)} %get-tuple-element.121), channel_id=1, source_target_pairs={{0,2},{2,0},{4,6},{6,4},{8,10},{10,8},{12,14},{14,12},{1,3},{3,1},... | collective-permute-start | bytes 786440 | tf_op jit(solution)/shard_map/ppermute | solution.py:160
  107.5 8.5 %collective-permute-start.22 = (bf16[128,1024]{1,0:T(8,128)(2,1)S(1)}, bf16[128,1024]{1,0:T(8,128)(2,1)S(1)}, u32[]{:S(2)}, u32[]{:S(2)}) collective-permute-start(bf16[128,1024]{1,0:T(8,128)(2,1)S(1)} %fusion), channel_id=1, source_target_pairs={{0,4},{2,6},{12,8},{14,10},{1,5},{3,7},{13,9},{15,11},{16,20},{18,... | collective-permute-start | bytes 786440 | tf_op jit(solution)/shard_map/ppermute | solution.py:156
  108.8 17.5 %collective-permute-start.26 = (bf16[128,1024]{1,0:T(8,128)(2,1)S(1)}, bf16[128,1024]{1,0:T(8,128)(2,1)S(1)}, u32[]{:S(2)}, u32[]{:S(2)}) collective-permute-start(bf16[128,1024]{1,0:T(8,128)(2,1)S(1)} %get-tuple-element.130), channel_id=1, source_target_pairs={{0,2},{2,0},{4,6},{6,4},{8,10},{10,8},{12,14},{14,12},{1,3},{3,1},... | collective-permute-start | bytes 786440 | tf_op jit(solution)/shard_map/ppermute | solution.py:160
  116.2 10.1 %collective-permute-start.25 = (bf16[128,1024]{1,0:T(8,128)(2,1)S(1)}, bf16[128,1024]{1,0:T(8,128)(2,1)S(1)}, u32[]{:S(2)}, u32[]{:S(2)}) collective-permute-start(bf16[128,1024]{1,0:T(8,128)(2,1)S(1)} %fusion.1), channel_id=1, source_target_pairs={{0,4},{2,6},{12,8},{14,10},{1,5},{3,7},{13,9},{15,11},{16,20},{18,... | collective-permute-start | bytes 786440 | tf_op jit(solution)/shard_map/ppermute | solution.py:156
  117.5 8.9 %collective-permute-start.24 = (bf16[128,1024]{1,0:T(8,128)(2,1)S(1)}, bf16[128,1024]{1,0:T(8,128)(2,1)S(1)}, u32[]{:S(2)}, u32[]{:S(2)}) collective-permute-start(bf16[128,1024]{1,0:T(8,128)(2,1)S(1)} %add_convert_fusion.3), channel_id=1, source_target_pairs={{4,8},{6,10},{8,4},{10,6},{5,9},{7,11},{9,5},{11,7},{20,24},{22,26... | collective-permute-start | bytes 786440 | tf_op jit(solution)/shard_map/ppermute | solution.py:156
  121.5 12.7 %collective-permute-start.29 = (bf16[128,1024]{1,0:T(8,128)(2,1)S(1)}, bf16[128,1024]{1,0:T(8,128)(2,1)S(1)}, u32[]{:S(2)}, u32[]{:S(2)}) collective-permute-start(bf16[128,1024]{1,0:T(8,128)(2,1)S(1)} %get-tuple-element.128), channel_id=1, source_target_pairs={{0,2},{2,0},{4,6},{6,4},{8,10},{10,8},{12,14},{14,12},{1,3},{3,1},... | collective-permute-start | bytes 786440 | tf_op jit(solution)/shard_map/ppermute | solution.py:160
  126.6 7.7 %collective-permute-start.28 = (bf16[128,1024]{1,0:T(8,128)(2,1)S(1)}, bf16[128,1024]{1,0:T(8,128)(2,1)S(1)}, u32[]{:S(2)}, u32[]{:S(2)}) collective-permute-start(bf16[128,1024]{1,0:T(8,128)(2,1)S(1)} %add_convert_fusion.1), channel_id=1, source_target_pairs={{0,4},{2,6},{4,0},{6,2},{8,12},{10,14},{12,8},{14,10},{1,5},{3,7},... | collective-permute-start | bytes 786440 | tf_op jit(solution)/shard_map/ppermute | solution.py:156
  126.7 8.3 %collective-permute-start.27 = (bf16[128,1024]{1,0:T(8,128)(2,1)S(1)}, bf16[128,1024]{1,0:T(8,128)(2,1)S(1)}, u32[]{:S(2)}, u32[]{:S(2)}) collective-permute-start(bf16[128,1024]{1,0:T(8,128)(2,1)S(1)} %add_convert_fusion.2), channel_id=1, source_target_pairs={{4,8},{6,10},{8,4},{10,6},{5,9},{7,11},{9,5},{11,7},{20,24},{22,26... | collective-permute-start | bytes 786440 | tf_op jit(solution)/shard_map/ppermute | solution.py:156
  (13 other events, 64.3 us)

commit v4 on v3

--- a/solution.py
+++ b/solution.py
@@ -178,12 +178,13 @@
 
     outer, inner, other = along_line(rows, OUTER), along_line(rows, INNER), across_pair(rows)
     info = widen(info + across_cores(info), [1])
-    info = widen(info, [2, 4, 6])
+    info = widen(info, [2])
     outer, inner, other, info = tie((outer, inner, other, info))
     pieces = [rows, other]
 
     second, third = along_line(inner, TO_END), along_line(outer, INNER)
     other = across_pair(outer)
+    info = widen(info, [4])
     second, third, other = tie((second, third, other))
     pieces += [outer, other]
 

time: 136 us -> 134 us (0.985)
  starting transfers between devices: 40.6 us -> 35.9 us
  waiting for transfers between devices: 26.7 us -> 28.9 us
    ppermute x4 -> x3, waiting for transfers between devices: 8.92 us -> 13.6 us  [widen(): lax.ppermute(info, 'ep', [(i, i ^ bit) for i in range(2 * LINES)])]
    ppermute x4 -> x3, starting transfers between devices: 5.2 us -> 1.12 us  [widen(): lax.ppermute(info, 'ep', [(i, i ^ bit) for i in range(2 * LINES)])]
    ppermute x9, waiting for transfers between devices: 7.61 us -> 4.81 us  [across_pair(): return lax.ppermute(value, 'ep', [(i, i ^ 1) for i in range(2 * LINES)])]
    ppermute x10, starting transfers between devices: 24.1 us -> 22.4 us  [along_line(): return lax.ppermute(value, 'ep', pairs)]
  transfers between devices with their start and end apart: 30 -> 29, of which waited for: 12 -> 10; matrix products, arithmetic and copies ran while one was open for 4% -> 4% of each run, Pallas kernels for 34% -> 35%
where the time goes in v4:
time: 134 us; the launch traced here: 133 us
  Pallas kernels  59.5 us (44%)
  starting transfers between devices  35.9 us (27%)
  waiting for transfers between devices  28.9 us (22%)
  other arithmetic  7.64 us (6%)
    ppermute x10, starting transfers between devices, along_line(): return lax.ppermute(value, 'ep', pairs)  22.4 us
    pallas_call x2, Pallas kernels, rows(): pl.pallas_call(functools.partial(rows_kernel, number * half), out_shape=t...  16.8 us
    pallas_call x4, Pallas kernels, meanwhile(): pl.pallas_call(weight_kernel, grid=(group,), out_shape=(weight_shape, wei...  16.4 us
    ppermute x3, waiting for transfers between devices, widen(): lax.ppermute(info, 'ep', [(i, i ^ bit) for i in range(2 * LINES)])  13.6 us
    ppermute x9, starting transfers between devices, across_pair(): return lax.ppermute(value, 'ep', [(i, i ^ 1) for i in range(2 * LINES)])  10.7 us
    pallas_call x2, Pallas kernels, down(): pl.pallas_call(functools.partial(down_kernel, start), out_shape=part_of_p...  9.82 us
    ppermute x10, waiting for transfers between devices, along_line(): return lax.ppermute(value, 'ep', pairs)  9.24 us
    pallas_call x1, Pallas kernels, gather_body(): pl.pallas_call(pre_kernel, out_shape=(x_shape,) + (part_of_pre,) * (2 * H...  7.55 us
  transfers between devices with their start and end apart: 29, of which 10 were waited for; matrix products, arithmetic and copies ran while one was open for 4% of the time, Pallas kernels for 35%

profile of v4, /device:TPU:12, one launch (start us, length us, event | category | flops | bytes accessed | tf_op | source)
XLA Modules:
  0.0 133.3 jit_solution(14431912035620516345)
XLA Ops:
  3.3 3.5 %collective-permute-start.1 = (bf16[2,128,1024]{2,1,0:T(8,128)(2,1)S(1)}, bf16[2,128,1024]{2,1,0:T(8,128)(2,1)S(1)}, u32[]{:S(2)}, u32[]{:S(2)}) collective-permute-start(bf16[2,128,1024]{2,1,0:T(8,128)(2,1)S(1)} %pad_maximum_fusion.refs_0_), channel_id=1, source_target_pairs={{4,8},{6,10},{8,4},{10,6},{5,9},{7,11},{9,5},{11,7},{20,24},{22,26... | collective-permute-start | bytes 1572872 | tf_op jit(solution)/shard_map/ppermute | solution.py:156
  11.1 5.0 %collective-permute-done.4 = bf16[8,16,128]{2,1,0:T(8,128)(2,1)S(1)} collective-permute-done((bf16[8,16,128]{2,1,0:T(8,128)(2,1)S(1)}, bf16[8,16,128]{2,1,0:T(8,128)(2,1)S(1)}, u32[]{:S(2)}, u32[]{:S(2)}) %collective-permute-start.4) | collective-permute-done | bytes 32800 | tf_op jit(solution)/shard_map/ppermute | solution.py:175
  16.7 3.9 %collective-permute-done.5 = bf16[8,16,128]{2,1,0:T(8,128)(2,1)S(1)} collective-permute-done((bf16[8,16,128]{2,1,0:T(8,128)(2,1)S(1)}, bf16[8,16,128]{2,1,0:T(8,128)(2,1)S(1)}, u32[]{:S(2)}, u32[]{:S(2)}) %collective-permute-start.5) | collective-permute-done | bytes 32800 | tf_op jit(solution)/shard_map/ppermute | solution.py:175
  20.7 3.0 %collective-permute-start.7 = (bf16[2,128,1024]{2,1,0:T(8,128)(2,1)S(1)}, bf16[2,128,1024]{2,1,0:T(8,128)(2,1)}, u32[]{:S(2)}, u32[]{:S(2)}) collective-permute-start(bf16[2,128,1024]{2,1,0:T(8,128)(2,1)S(1)} %collective-permute-done.1), channel_id=1, source_target_pairs={{4,0},{6,2},{8,12},{10,14},{5,1},{7,3},{9,13},{11,15},{20,16},{22,... | collective-permute-start | bytes 1572872 | tf_op jit(solution)/shard_map/ppermute | solution.py:156
  24.9 4.6 %collective-permute-start.8 = (bf16[2,128,1024]{2,1,0:T(8,128)(2,1)S(1)}, bf16[2,128,1024]{2,1,0:T(8,128)(2,1)}, u32[]{:S(2)}, u32[]{:S(2)}) collective-permute-start(bf16[2,128,1024]{2,1,0:T(8,128)(2,1)S(1)} %collective-permute-done.refs_2_), channel_id=1, source_target_pairs={{4,8},{6,10},{8,4},{10,6},{5,9},{7,11},{9,5},{11,7},{20,24},{22,26... | collective-permute-start | bytes 1572872 | tf_op jit(solution)/shard_map/ppermute | solution.py:156
  29.5 3.6 %collective-permute-done.7 = bf16[2,128,1024]{2,1,0:T(8,128)(2,1)} collective-permute-done((bf16[2,128,1024]{2,1,0:T(8,128)(2,1)S(1)}, bf16[2,128,1024]{2,1,0:T(8,128)(2,1)}, u32[]{:S(2)}, u32[]{:S(2)}) %collective-permute-start.7) | collective-permute-done | bytes 524320 | tf_op jit(solution)/shard_map/ppermute | solution.py:156
  33.1 3.0 %collective-permute-done.9.refs_3_ = bf16[2,128,1024]{2,1,0:T(8,128)(2,1)S(1)} collective-permute-done((bf16[2,128,1024]{2,1,0:T(8,128)(2,1)S(1)}, bf16[2,128,1024]{2,1,0:T(8,128)(2,1)S(1)}, u32[]{:S(2)}, u32[]{:S(2)}) %collective-permute-start.9) | collective-permute-done | bytes 524320 | tf_op jit(solution)/shard_map/ppermute | solution.py:160
  36.2 2.7 %collective-permute-done.8 = bf16[2,128,1024]{2,1,0:T(8,128)(2,1)} collective-permute-done((bf16[2,128,1024]{2,1,0:T(8,128)(2,1)S(1)}, bf16[2,128,1024]{2,1,0:T(8,128)(2,1)}, u32[]{:S(2)}, u32[]{:S(2)}) %collective-permute-start.8) | collective-permute-done | bytes 524320 | tf_op jit(solution)/shard_map/ppermute | solution.py:156
  40.0 2.1 %collective-permute-start.10 = (bf16[2,128,1024]{2,1,0:T(8,128)(2,1)}, bf16[2,128,1024]{2,1,0:T(8,128)(2,1)}, u32[]{:S(2)}, u32[]{:S(2)}) collective-permute-start(bf16[2,128,1024]{2,1,0:T(8,128)(2,1)} %collective-permute-done.8), channel_id=1, source_target_pairs={{4,0},{6,2},{8,12},{10,14},{5,1},{7,3},{9,13},{11,15},{20,16},{22,... | collective-permute-start | bytes 1572872 | tf_op jit(solution)/shard_map/ppermute | solution.py:156
  43.0 4.7 %collective-permute-done.6 = bf16[8,16,128]{2,1,0:T(8,128)(2,1)S(1)} collective-permute-done((bf16[8,16,128]{2,1,0:T(8,128)(2,1)S(1)}, bf16[8,16,128]{2,1,0:T(8,128)(2,1)S(1)}, u32[]{:S(2)}, u32[]{:S(2)}) %collective-permute-start.6) | collective-permute-done | bytes 32800 | tf_op jit(solution)/shard_map/ppermute | solution.py:175
  48.5 2.3 %first_slots.1 = (bf16[16,48,1024]{2,1,0:T(8,128)(2,1)S(1)}, bf16[16,48,1024]{2,1,0:T(8,128)(2,1)S(1)}, f32[16,96,128]{2,1,0:T(8,128)S(1)}) custom-call(s32[16,1024]{1,0:T(8,128)S(1)} %get-tuple-element.85.slot_ref, f32[16,1024]{1,0:T(8,128)S(1)} %get-tuple-element.86.gates_ref, bf16[2,128,1024]{2,1,0:T(8,128)(2,1)S(1)} %pad_maximum_fusion.refs_0_, ...), custom_call_target="tpu_custom_call" | custom-call | flops 1610612736 | bytes 6291456 | tf_op jit(solution)/shard_map/first_slots/pallas_call | solution.py:616
  55.1 4.7 %load.1.refs_5_ = bf16[16,1024,384]{2,1,0:T(8,128)(2,1)S(1)} custom-call(bf16[16,1024,384]{2,1,0:T(8,128)(2,1)} %refs_6_.5), custom_call_target="tpu_custom_call" | custom-call | bytes 12582912 | tf_op jit(solution)/shard_map/load/pallas_call | solution.py:592
  59.8 7.6 %pre.1 = (bf16[16,96,1024]{2,1,0:T(8,128)(2,1)S(1)}, f32[8,96,384]{2,1,0:T(8,128)}, f32[8,96,384]{2,1,0:T(8,128)}, f32[8,96,384]{2,1,0:T(8,128)}, f32[8,96,384]{2,1,0:T(8,128)}) custom-call(s32[16,1024]{1,0:T(8,128)S(1)} %get-tuple-element.85.slot_ref, bf16[2,128,1024]{2,1,0:T(8,128)(2,1)S(1)} %broadcast_select_fusion.refs_0_, ...), custom_call_target="tpu_custom_call" | custom-call | flops 3221225472 | bytes 35232152 | tf_op jit(solution)/shard_map/pre/pallas_call | solution.py:635
  67.4 4.9 %down.2.refs_4_ = f32[8,96,384]{2,1,0:T(8,128)} custom-call(s32[16,1024]{1,0:T(8,128)S(1)} %get-tuple-element.85.slot_ref, bf16[2,128,1024]{2,1,0:T(8,128)(2,1)S(1)} %broadcast_select_fusion.refs_0_, bf16[2,128,1024]{2,1,0:T(8,128)(2,1)S(1)} %collective-permute-done.11.refs_1_, bf16[128,1024]{1,0:T(8,128)(2,1)S(1)} %select_bitcast_fusion.refs_2_, ...), custom_call_target="tpu_custom_call" | custom-call | flops 1006632960 | bytes 8808038 | tf_op jit(solution)/shard_map/down/pallas_call | solution.py:656
  73.0 4.9 %down.3.refs_4_ = f32[8,96,384]{2,1,0:T(8,128)} custom-call(s32[16,1024]{1,0:T(8,128)S(1)} %get-tuple-element.85.slot_ref, bf16[2,128,1024]{2,1,0:T(8,128)(2,1)S(1)} %broadcast_select_fusion.refs_0_, bf16[2,128,1024]{2,1,0:T(8,128)(2,1)S(1)} %collective-permute-done.11.refs_1_, bf16[128,1024]{1,0:T(8,128)(2,1)S(1)} %select_bitcast_fusion.refs_2_, ...), custom_call_target="tpu_custom_call" | custom-call | flops 1006632960 | bytes 8808038 | tf_op jit(solution)/shard_map/down/pallas_call | solution.py:656
  78.9 8.3 %rows.2 = (bf16[8,96,768]{2,1,0:T(8,128)(2,1)S(1)}, bf16[384,1024]{1,0:T(8,128)(2,1)S(1)}, f32[512,1024]{1,0:T(8,128)S(1)}) custom-call(s32[16,1024]{1,0:T(8,128)S(1)} %get-tuple-element.85.slot_ref, f32[16,96,128]{2,1,0:T(8,128)S(1)} %get-tuple-element.91.slot_gates_ref, f32[8,96,384]{2,1,0:T(8,128)S(1)} %copy-done.4, ...), custom_call_target="tpu_custom_call" | custom-call | flops 2013265920 | bytes 19503512 | tf_op jit(solution)/shard_map/rows/pallas_call | solution.py:700
  87.3 8.4 %rows.3 = (bf16[8,96,768]{2,1,0:T(8,128)(2,1)S(1)}, bf16[384,1024]{1,0:T(8,128)(2,1)S(1)}, bf16[128,1024]{1,0:T(8,128)(2,1)S(1)}, bf16[128,1024]{1,0:T(8,128)(2,...) custom-call(s32[16,1024]{1,0:T(8,128)S(1)} %get-tuple-element.85.slot_ref, ...), custom_call_target="tpu_custom_call" | custom-call | flops 2013265920 | bytes 19503512 | tf_op jit(solution)/shard_map/rows/pallas_call | solution.py:700
  99.1 4.1 %weight_grads.4 = (bf16[16,1024,384]{2,1,0:T(8,128)(2,1)}, bf16[16,1024,384]{2,1,0:T(8,128)(2,1)}) custom-call(bf16[16,96,1024]{2,1,0:T(8,128)(2,1)S(1)} %get-tuple-element.154.x_ref, bf16[8,96,768]{2,1,0:T(8,128)(2,1)S(1)} %get-tuple-element.137.grads_ref), custom_call_target="tpu_custom_call" | custom-call | flops 603979776 | bytes 7864320 | tf_op jit(solution)/shard_map/weight_grads/pallas_call | solution.py:759
  107.4 4.1 %weight_grads.5 = (bf16[16,1024,384]{2,1,0:T(8,128)(2,1)}, bf16[16,1024,384]{2,1,0:T(8,128)(2,1)}) custom-call(bf16[16,96,1024]{2,1,0:T(8,128)(2,1)S(1)} %get-tuple-element.154.x_ref, bf16[8,96,768]{2,1,0:T(8,128)(2,1)S(1)} %get-tuple-element.137.grads_ref, ...), custom_call_target="tpu_custom_call", output_to_operand_aliasing={{0}: (2, {}), {1}: (3, {})} | custom-call | flops 603979776 | bytes 7864320 | tf_op jit(solution)/shard_map/weight_grads/pallas_call | solution.py:759
  111.5 2.0 %collective-permute-done.21 = bf16[128,1024]{1,0:T(8,128)(2,1)S(1)} collective-permute-done((bf16[128,1024]{1,0:T(8,128)(2,1)S(1)}, bf16[128,1024]{1,0:T(8,128)(2,1)S(1)}, u32[]{:S(2)}, u32[]{:S(2)}) %collective-permute-start.21) | collective-permute-done | bytes 262176 | tf_op jit(solution)/shard_map/ppermute | solution.py:156
  115.0 3.2 %collective-permute-start.23 = (bf16[128,1024]{1,0:T(8,128)(2,1)S(1)}, bf16[128,1024]{1,0:T(8,128)(2,1)S(1)}, u32[]{:S(2)}, u32[]{:S(2)}) collective-permute-start(bf16[128,1024]{1,0:T(8,128)(2,1)S(1)} %add_convert_fusion.3), channel_id=1, source_target_pairs={{4,8},{6,10},{8,4},{10,6},{5,9},{7,11},{9,5},{11,7},{20,24},{22,26... | collective-permute-start | bytes 786440 | tf_op jit(solution)/shard_map/ppermute | solution.py:156
  119.8 4.1 %weight_grads.6 = (bf16[16,1024,384]{2,1,0:T(8,128)(2,1)}, bf16[16,1024,384]{2,1,0:T(8,128)(2,1)}) custom-call(bf16[16,96,1024]{2,1,0:T(8,128)(2,1)S(1)} %get-tuple-element.154.x_ref, bf16[8,96,768]{2,1,0:T(8,128)(2,1)S(1)} %get-tuple-element.155.grads_ref, ...), custom_call_target="tpu_custom_call", output_to_operand_aliasing={{0}: (2, {}), {1}: (3, {})} | custom-call | flops 603979776 | bytes 7864320 | tf_op jit(solution)/shard_map/weight_grads/pallas_call | solution.py:759
  124.2 3.3 %collective-permute-start.26 = (bf16[128,1024]{1,0:T(8,128)(2,1)S(1)}, bf16[128,1024]{1,0:T(8,128)(2,1)S(1)}, u32[]{:S(2)}, u32[]{:S(2)}) collective-permute-start(bf16[128,1024]{1,0:T(8,128)(2,1)S(1)} %add_convert_fusion.2), channel_id=1, source_target_pairs={{4,8},{6,10},{8,4},{10,6},{5,9},{7,11},{9,5},{11,7},{20,24},{22,26... | collective-permute-start | bytes 786440 | tf_op jit(solution)/shard_map/ppermute | solution.py:156
  127.5 4.1 %weight_grads.7 = (bf16[16,1024,384]{2,1,0:T(8,128)(2,1)}, bf16[16,1024,384]{2,1,0:T(8,128)(2,1)}) custom-call(bf16[16,96,1024]{2,1,0:T(8,128)(2,1)S(1)} %get-tuple-element.154.x_ref, bf16[8,96,768]{2,1,0:T(8,128)(2,1)S(1)} %get-tuple-element.155.grads_ref, ...), custom_call_target="tpu_custom_call", output_to_operand_aliasing={{0}: (2, {}), {1}: (3, {})} | custom-call | flops 603979776 | bytes 7864320 | tf_op jit(solution)/shard_map/weight_grads/pallas_call | solution.py:759
  (82 shorter events, 30.1 us)
Async XLA Ops:
  1.7 18.9 %collective-permute-start.2 = (bf16[2,128,1024]{2,1,0:T(8,128)(2,1)S(1)}, bf16[2,128,1024]{2,1,0:T(8,128)(2,1)S(1)}, u32[]{:S(2)}, u32[]{:S(2)}) collective-permute-start(bf16[2,128,1024]{2,1,0:T(8,128)(2,1)S(1)} %pad_maximum_fusion.refs_0_), channel_id=1, source_target_pairs={{0,2},{2,0},{4,6},{6,4},{8,10},{10,8},{12,14},{14,12},{1,3},{3,1},... | collective-permute-start | bytes 1572872 | tf_op jit(solution)/shard_map/ppermute | solution.py:160
  3.3 17.4 %collective-permute-start.1 = (bf16[2,128,1024]{2,1,0:T(8,128)(2,1)S(1)}, bf16[2,128,1024]{2,1,0:T(8,128)(2,1)S(1)}, u32[]{:S(2)}, u32[]{:S(2)}) collective-permute-start(bf16[2,128,1024]{2,1,0:T(8,128)(2,1)S(1)} %pad_maximum_fusion.refs_0_), channel_id=1, source_target_pairs={{4,8},{6,10},{8,4},{10,6},{5,9},{7,11},{9,5},{11,7},{20,24},{22,26... | collective-permute-start | bytes 1572872 | tf_op jit(solution)/shard_map/ppermute | solution.py:156
  6.7 13.9 %collective-permute-start = (bf16[2,128,1024]{2,1,0:T(8,128)(2,1)S(1)}, bf16[2,128,1024]{2,1,0:T(8,128)(2,1)S(1)}, u32[]{:S(2)}, u32[]{:S(2)}) collective-permute-start(bf16[2,128,1024]{2,1,0:T(8,128)(2,1)S(1)} %pad_maximum_fusion.refs_0_), channel_id=1, source_target_pairs={{0,4},{2,6},{4,0},{6,2},{8,12},{10,14},{12,8},{14,10},{1,5},{3,7},... | collective-permute-start | bytes 1572872 | tf_op jit(solution)/shard_map/ppermute | solution.py:156
  20.7 12.5 %collective-permute-start.7 = (bf16[2,128,1024]{2,1,0:T(8,128)(2,1)S(1)}, bf16[2,128,1024]{2,1,0:T(8,128)(2,1)}, u32[]{:S(2)}, u32[]{:S(2)}) collective-permute-start(bf16[2,128,1024]{2,1,0:T(8,128)(2,1)S(1)} %collective-permute-done.1), channel_id=1, source_target_pairs={{4,0},{6,2},{8,12},{10,14},{5,1},{7,3},{9,13},{11,15},{20,16},{22,... | collective-permute-start | bytes 1572872 | tf_op jit(solution)/shard_map/ppermute | solution.py:156
  23.7 12.5 %collective-permute-start.9 = (bf16[2,128,1024]{2,1,0:T(8,128)(2,1)S(1)}, bf16[2,128,1024]{2,1,0:T(8,128)(2,1)S(1)}, u32[]{:S(2)}, u32[]{:S(2)}) collective-permute-start(bf16[2,128,1024]{2,1,0:T(8,128)(2,1)S(1)} %collective-permute-done.refs_2_), channel_id=1, source_target_pairs={{0,2},{2,0},{4,6},{6,4},{8,10},{10,8},{12,14},{14,12},{1,3},{3,1},... | collective-permute-start | bytes 1572872 | tf_op jit(solution)/shard_map/ppermute | solution.py:160
  24.9 14.0 %collective-permute-start.8 = (bf16[2,128,1024]{2,1,0:T(8,128)(2,1)S(1)}, bf16[2,128,1024]{2,1,0:T(8,128)(2,1)}, u32[]{:S(2)}, u32[]{:S(2)}) collective-permute-start(bf16[2,128,1024]{2,1,0:T(8,128)(2,1)S(1)} %collective-permute-done.refs_2_), channel_id=1, source_target_pairs={{4,8},{6,10},{8,4},{10,6},{5,9},{7,11},{9,5},{11,7},{20,24},{22,26... | collective-permute-start | bytes 1572872 | tf_op jit(solution)/shard_map/ppermute | solution.py:156
  39.0 11.8 %collective-permute-start.11 = (bf16[2,128,1024]{2,1,0:T(8,128)(2,1)S(1)}, bf16[2,128,1024]{2,1,0:T(8,128)(2,1)S(1)}, u32[]{:S(2)}, u32[]{:S(2)}) collective-permute-start(bf16[2,128,1024]{2,1,0:T(8,128)(2,1)S(1)} %broadcast_select_fusion.refs_0_), channel_id=1, source_target_pairs={{0,2},{2,0},{4,6},{6,4},{8,10},{10,8},{12,14},{14,12},{1,3},{3,1},... | collective-permute-start | bytes 1572872 | tf_op jit(solution)/shard_map/ppermute | solution.py:160
  40.0 10.8 %collective-permute-start.10 = (bf16[2,128,1024]{2,1,0:T(8,128)(2,1)}, bf16[2,128,1024]{2,1,0:T(8,128)(2,1)}, u32[]{:S(2)}, u32[]{:S(2)}) collective-permute-start(bf16[2,128,1024]{2,1,0:T(8,128)(2,1)} %collective-permute-done.8), channel_id=1, source_target_pairs={{4,0},{6,2},{8,12},{10,14},{5,1},{7,3},{9,13},{11,15},{20,16},{22,... | collective-permute-start | bytes 1572872 | tf_op jit(solution)/shard_map/ppermute | solution.py:156
  51.9 7.9 %collective-permute-start.12 = (bf16[128,1024]{1,0:T(8,128)(2,1)S(1)}, bf16[128,1024]{1,0:T(8,128)(2,1)S(1)}, u32[]{:S(2)}, u32[]{:S(2)}) collective-permute-start(bf16[128,1024]{1,0:T(8,128)(2,1)S(1)} %select_bitcast_fusion.1.refs_2_), channel_id=1, source_target_pairs={{0,2},{2,0},{4,6},{6,4},{8,10},{10,8},{12,14},{14,12},{1,3},{3,1},... | collective-permute-start | bytes 786440 | tf_op jit(solution)/shard_map/ppermute | solution.py:160
  54.0 13.3 %collective-permute-start.13 = (bf16[128,1024]{1,0:T(8,128)(2,1)S(1)}, bf16[128,1024]{1,0:T(8,128)(2,1)S(1)}, u32[]{:S(2)}, u32[]{:S(2)}) collective-permute-start(bf16[128,1024]{1,0:T(8,128)(2,1)S(1)} %select_bitcast_fusion.refs_2_), channel_id=1, source_target_pairs={{0,2},{2,0},{4,6},{6,4},{8,10},{10,8},{12,14},{14,12},{1,3},{3,1},... | collective-permute-start | bytes 786440 | tf_op jit(solution)/shard_map/ppermute | solution.py:160
  72.3 6.2 %collective-permute-start.14 = (f32[8,96,384]{2,1,0:T(8,128)}, f32[8,96,384]{2,1,0:T(8,128)S(1)}, u32[]{:S(2)}, u32[]{:S(2)}) collective-permute-start(f32[8,96,384]{2,1,0:T(8,128)} %down.2.refs_4_), channel_id=1, source_target_pairs={{0,1},{1,0},{2,3},{3,2},{4,5},{5,4},{6,7},{7,6},{8,9},{9,8},{10,11... | collective-permute-start | bytes 3538952 | tf_op jit(solution)/shard_map/ppermute | solution.py:164
  72.4 6.5 %collective-permute-start.15 = (f32[8,96,384]{2,1,0:T(8,128)S(1)}, f32[8,96,384]{2,1,0:T(8,128)S(1)}, u32[]{:S(2)}, u32[]{:S(2)}) collective-permute-start(f32[8,96,384]{2,1,0:T(8,128)S(1)} %copy-done.4), channel_id=1, source_target_pairs={{0,1},{1,0},{2,3},{3,2},{4,5},{5,4},{6,7},{7,6},{8,9},{9,8},{10,11... | collective-permute-start | bytes 3538952 | tf_op jit(solution)/shard_map/ppermute | solution.py:164
  77.9 9.4 %collective-permute-start.19 = (f32[8,96,384]{2,1,0:T(8,128)}, f32[8,96,384]{2,1,0:T(8,128)S(1)}, u32[]{:S(2)}, u32[]{:S(2)}) collective-permute-start(f32[8,96,384]{2,1,0:T(8,128)} %down.3.refs_4_), channel_id=1, source_target_pairs={{0,1},{1,0},{2,3},{3,2},{4,5},{5,4},{6,7},{7,6},{8,9},{9,8},{10,11... | collective-permute-start | bytes 3538952 | tf_op jit(solution)/shard_map/ppermute | solution.py:164
  78.4 8.9 %collective-permute-start.17 = (f32[8,96,384]{2,1,0:T(8,128)S(1)}, f32[8,96,384]{2,1,0:T(8,128)S(1)}, u32[]{:S(2)}, u32[]{:S(2)}) collective-permute-start(f32[8,96,384]{2,1,0:T(8,128)S(1)} %copy-done.2), channel_id=1, source_target_pairs={{0,1},{1,0},{2,3},{3,2},{4,5},{5,4},{6,7},{7,6},{8,9},{9,8},{10,11... | collective-permute-start | bytes 3538952 | tf_op jit(solution)/shard_map/ppermute | solution.py:164
  78.5 8.8 %collective-permute-start.18 = (f32[8,96,384]{2,1,0:T(8,128)S(1)}, f32[8,96,384]{2,1,0:T(8,128)S(1)}, u32[]{:S(2)}, u32[]{:S(2)}) collective-permute-start(f32[8,96,384]{2,1,0:T(8,128)S(1)} %copy-done.3), channel_id=1, source_target_pairs={{0,1},{1,0},{2,3},{3,2},{4,5},{5,4},{6,7},{7,6},{8,9},{9,8},{10,11... | collective-permute-start | bytes 3538952 | tf_op jit(solution)/shard_map/ppermute | solution.py:164
  95.7 9.2 %collective-permute-start.20 = (bf16[128,1024]{1,0:T(8,128)(2,1)S(1)}, bf16[128,1024]{1,0:T(8,128)(2,1)S(1)}, u32[]{:S(2)}, u32[]{:S(2)}) collective-permute-start(bf16[128,1024]{1,0:T(8,128)(2,1)S(1)} %get-tuple-element.123), channel_id=1, source_target_pairs={{0,2},{2,0},{4,6},{6,4},{8,10},{10,8},{12,14},{14,12},{1,3},{3,1},... | collective-permute-start | bytes 786440 | tf_op jit(solution)/shard_map/ppermute | solution.py:160
  96.8 14.7 %collective-permute-start.22 = (bf16[128,1024]{1,0:T(8,128)(2,1)S(1)}, bf16[128,1024]{1,0:T(8,128)(2,1)S(1)}, u32[]{:S(2)}, u32[]{:S(2)}) collective-permute-start(bf16[128,1024]{1,0:T(8,128)(2,1)S(1)} %get-tuple-element.121), channel_id=1, source_target_pairs={{0,2},{2,0},{4,6},{6,4},{8,10},{10,8},{12,14},{14,12},{1,3},{3,1},... | collective-permute-start | bytes 786440 | tf_op jit(solution)/shard_map/ppermute | solution.py:160
  105.0 8.5 %collective-permute-start.21 = (bf16[128,1024]{1,0:T(8,128)(2,1)S(1)}, bf16[128,1024]{1,0:T(8,128)(2,1)S(1)}, u32[]{:S(2)}, u32[]{:S(2)}) collective-permute-start(bf16[128,1024]{1,0:T(8,128)(2,1)S(1)} %fusion), channel_id=1, source_target_pairs={{0,4},{2,6},{12,8},{14,10},{1,5},{3,7},{13,9},{15,11},{16,20},{18,... | collective-permute-start | bytes 786440 | tf_op jit(solution)/shard_map/ppermute | solution.py:156
  106.3 17.5 %collective-permute-start.25 = (bf16[128,1024]{1,0:T(8,128)(2,1)S(1)}, bf16[128,1024]{1,0:T(8,128)(2,1)S(1)}, u32[]{:S(2)}, u32[]{:S(2)}) collective-permute-start(bf16[128,1024]{1,0:T(8,128)(2,1)S(1)} %get-tuple-element.130), channel_id=1, source_target_pairs={{0,2},{2,0},{4,6},{6,4},{8,10},{10,8},{12,14},{14,12},{1,3},{3,1},... | collective-permute-start | bytes 786440 | tf_op jit(solution)/shard_map/ppermute | solution.py:160
  113.7 10.1 %collective-permute-start.24 = (bf16[128,1024]{1,0:T(8,128)(2,1)S(1)}, bf16[128,1024]{1,0:T(8,128)(2,1)S(1)}, u32[]{:S(2)}, u32[]{:S(2)}) collective-permute-start(bf16[128,1024]{1,0:T(8,128)(2,1)S(1)} %fusion.1), channel_id=1, source_target_pairs={{0,4},{2,6},{12,8},{14,10},{1,5},{3,7},{13,9},{15,11},{16,20},{18,... | collective-permute-start | bytes 786440 | tf_op jit(solution)/shard_map/ppermute | solution.py:156
  115.0 8.8 %collective-permute-start.23 = (bf16[128,1024]{1,0:T(8,128)(2,1)S(1)}, bf16[128,1024]{1,0:T(8,128)(2,1)S(1)}, u32[]{:S(2)}, u32[]{:S(2)}) collective-permute-start(bf16[128,1024]{1,0:T(8,128)(2,1)S(1)} %add_convert_fusion.3), channel_id=1, source_target_pairs={{4,8},{6,10},{8,4},{10,6},{5,9},{7,11},{9,5},{11,7},{20,24},{22,26... | collective-permute-start | bytes 786440 | tf_op jit(solution)/shard_map/ppermute | solution.py:156
  118.2 13.4 %collective-permute-start.28 = (bf16[128,1024]{1,0:T(8,128)(2,1)S(1)}, bf16[128,1024]{1,0:T(8,128)(2,1)S(1)}, u32[]{:S(2)}, u32[]{:S(2)}) collective-permute-start(bf16[128,1024]{1,0:T(8,128)(2,1)S(1)} %get-tuple-element.128), channel_id=1, source_target_pairs={{0,2},{2,0},{4,6},{6,4},{8,10},{10,8},{12,14},{14,12},{1,3},{3,1},... | collective-permute-start | bytes 786440 | tf_op jit(solution)/shard_map/ppermute | solution.py:160
  124.1 7.5 %collective-permute-start.27 = (bf16[128,1024]{1,0:T(8,128)(2,1)S(1)}, bf16[128,1024]{1,0:T(8,128)(2,1)S(1)}, u32[]{:S(2)}, u32[]{:S(2)}) collective-permute-start(bf16[128,1024]{1,0:T(8,128)(2,1)S(1)} %add_convert_fusion.1), channel_id=1, source_target_pairs={{0,4},{2,6},{4,0},{6,2},{8,12},{10,14},{12,8},{14,10},{1,5},{3,7},... | collective-permute-start | bytes 786440 | tf_op jit(solution)/shard_map/ppermute | solution.py:156
  124.2 8.3 %collective-permute-start.26 = (bf16[128,1024]{1,0:T(8,128)(2,1)S(1)}, bf16[128,1024]{1,0:T(8,128)(2,1)S(1)}, u32[]{:S(2)}, u32[]{:S(2)}) collective-permute-start(bf16[128,1024]{1,0:T(8,128)(2,1)S(1)} %add_convert_fusion.2), channel_id=1, source_target_pairs={{4,8},{6,10},{8,4},{10,6},{5,9},{7,11},{9,5},{11,7},{20,24},{22,26... | collective-permute-start | bytes 786440 | tf_op jit(solution)/shard_map/ppermute | solution.py:156
  (11 other events, 58.0 us)

commit v5 on v4

--- a/solution.py
+++ b/solution.py
@@ -744,8 +744,13 @@
     )(slot_of, near_first, near_last)
     partial = [*near_sums, *far_sums]
 
-    turns = LINES
-    group = local_count // turns
+    early, late = half * 5 // 8, half * 5 // 8
+    spans = (
+        ((0, early),),
+        ((early, half), (half, local_count - 2 * (half - late))),
+        ((local_count - 2 * (half - late), local_count - half + late),),
+        ((local_count - half + late, local_count),),
+    )
     weight_shape = jax.ShapeDtypeStruct(w_gate.shape, bf16)
     weight_grads = []
 
@@ -753,21 +758,24 @@
         return pl.BlockSpec((1,) + shape, lambda e: (first + e, 0, 0))
 
     def meanwhile(turn, values):
-        first = turn * group
-        operands = [x, grads[first // half]]
-        operands = tie(operands, *(held or partial))
-        weight_grads[:] = pl.pallas_call(
-            weight_kernel,
-            grid=(group,),
-            out_shape=(weight_shape, weight_shape),
-            in_specs=[block_of(first, slots, half_width), block_of(first % half, slots, 2 * hidden)]
-            + [memory] * len(weight_grads),
-            out_specs=(block_of(first, half_width, hidden), block_of(first, half_width, hidden)),
-            input_output_aliases={2 + i: i for i in range(len(weight_grads))},
-            compiler_params=params(32),
-            cost_estimate=cost(2 * matmul_flops / turns, 2.5 * weight_bytes / turns),
-            name="weight_grads",
-        )(*operands, *weight_grads)
+        tied = held or partial
+        for first, end in spans[turn]:
+            operands = tie([x, grads[first // half]], *tied)
+            weight_grads[:] = pl.pallas_call(
+                weight_kernel,
+                grid=(end - first,),
+                out_shape=(weight_shape, weight_shape),
+                in_specs=[block_of(first, slots, half_width), block_of(first % half, slots, 2 * hidden)]
+                + [memory] * len(weight_grads),
+                out_specs=(block_of(first, half_width, hidden), block_of(first, half_width, hidden)),
+                input_output_aliases={2 + i: i for i in range(len(weight_grads))},
+                compiler_params=params(32),
+                cost_estimate=cost(
+                    2 * matmul_flops * (end - first) / local_count,
+                    2.5 * weight_bytes * (end - first) / local_count,
+                ),
+                name="weight_grads",
+            )(*operands, *weight_grads)
         *values, weight_grads[0], weight_grads[1] = tie([*values, *weight_grads])
         held[:] = values
         return values

time: 134 us -> 134 us (level)
  waiting for transfers between devices: 28.9 us -> 27.1 us
  Pallas kernels: 59.5 us -> 61.2 us
    pallas_call x4 -> x5, Pallas kernels: 16.4 us -> 18.1 us  [meanwhile(): pl.pallas_call(weight_kernel, grid=(end - first,), out_shape=(weight_shap...]
  transfers between devices with their start and end apart: 29 -> 29, of which waited for: 10 -> 10; matrix products, arithmetic and copies ran while one was open for 4% -> 4% of each run, Pallas kernels for 35% -> 36%
where the time goes in v5:
time: 134 us; the launch traced here: 133 us
  Pallas kernels  61.2 us (46%)
  starting transfers between devices  36 us (27%)
  waiting for transfers between devices  27.1 us (20%)
  other arithmetic  7.64 us (6%)
    ppermute x10, starting transfers between devices, along_line(): return lax.ppermute(value, 'ep', pairs)  22.4 us
    pallas_call x5, Pallas kernels, meanwhile(): pl.pallas_call(weight_kernel, grid=(end - first,), out_shape=(weight_shap...  18.1 us
    pallas_call x2, Pallas kernels, rows(): pl.pallas_call(functools.partial(rows_kernel, number * half), out_shape=t...  16.8 us
    ppermute x3, waiting for transfers between devices, widen(): lax.ppermute(info, 'ep', [(i, i ^ bit) for i in range(2 * LINES)])  13.6 us
    ppermute x9, starting transfers between devices, across_pair(): return lax.ppermute(value, 'ep', [(i, i ^ 1) for i in range(2 * LINES)])  10.7 us
    pallas_call x2, Pallas kernels, down(): pl.pallas_call(functools.partial(down_kernel, start), out_shape=part_of_p...  9.81 us
    ppermute x10, waiting for transfers between devices, along_line(): return lax.ppermute(value, 'ep', pairs)  8.6 us
    pallas_call x1, Pallas kernels, gather_body(): pl.pallas_call(pre_kernel, out_shape=(x_shape,) + (part_of_pre,) * (2 * H...  7.56 us
  transfers between devices with their start and end apart: 29, of which 10 were waited for; matrix products, arithmetic and copies ran while one was open for 4% of the time, Pallas kernels for 36%

profile of v5, /device:TPU:12, one launch (start us, length us, event | category | flops | bytes accessed | tf_op | source)
XLA Modules:
  0.0 133.3 jit_solution(9503474320163773265)
XLA Ops:
  3.3 3.5 %collective-permute-start.1 = (bf16[2,128,1024]{2,1,0:T(8,128)(2,1)S(1)}, bf16[2,128,1024]{2,1,0:T(8,128)(2,1)S(1)}, u32[]{:S(2)}, u32[]{:S(2)}) collective-permute-start(bf16[2,128,1024]{2,1,0:T(8,128)(2,1)S(1)} %pad_maximum_fusion.refs_0_), channel_id=1, source_target_pairs={{4,8},{6,10},{8,4},{10,6},{5,9},{7,11},{9,5},{11,7},{20,24},{22,26... | collective-permute-start | bytes 1572872 | tf_op jit(solution)/shard_map/ppermute | solution.py:156
  11.1 5.0 %collective-permute-done.4 = bf16[8,16,128]{2,1,0:T(8,128)(2,1)S(1)} collective-permute-done((bf16[8,16,128]{2,1,0:T(8,128)(2,1)S(1)}, bf16[8,16,128]{2,1,0:T(8,128)(2,1)S(1)}, u32[]{:S(2)}, u32[]{:S(2)}) %collective-permute-start.4) | collective-permute-done | bytes 32800 | tf_op jit(solution)/shard_map/ppermute | solution.py:175
  16.7 3.9 %collective-permute-done.5 = bf16[8,16,128]{2,1,0:T(8,128)(2,1)S(1)} collective-permute-done((bf16[8,16,128]{2,1,0:T(8,128)(2,1)S(1)}, bf16[8,16,128]{2,1,0:T(8,128)(2,1)S(1)}, u32[]{:S(2)}, u32[]{:S(2)}) %collective-permute-start.5) | collective-permute-done | bytes 32800 | tf_op jit(solution)/shard_map/ppermute | solution.py:175
  20.7 3.0 %collective-permute-start.7 = (bf16[2,128,1024]{2,1,0:T(8,128)(2,1)S(1)}, bf16[2,128,1024]{2,1,0:T(8,128)(2,1)}, u32[]{:S(2)}, u32[]{:S(2)}) collective-permute-start(bf16[2,128,1024]{2,1,0:T(8,128)(2,1)S(1)} %collective-permute-done.1), channel_id=1, source_target_pairs={{4,0},{6,2},{8,12},{10,14},{5,1},{7,3},{9,13},{11,15},{20,16},{22,... | collective-permute-start | bytes 1572872 | tf_op jit(solution)/shard_map/ppermute | solution.py:156
  24.9 4.6 %collective-permute-start.8 = (bf16[2,128,1024]{2,1,0:T(8,128)(2,1)S(1)}, bf16[2,128,1024]{2,1,0:T(8,128)(2,1)}, u32[]{:S(2)}, u32[]{:S(2)}) collective-permute-start(bf16[2,128,1024]{2,1,0:T(8,128)(2,1)S(1)} %collective-permute-done.refs_2_), channel_id=1, source_target_pairs={{4,8},{6,10},{8,4},{10,6},{5,9},{7,11},{9,5},{11,7},{20,24},{22,26... | collective-permute-start | bytes 1572872 | tf_op jit(solution)/shard_map/ppermute | solution.py:156
  29.5 3.6 %collective-permute-done.7 = bf16[2,128,1024]{2,1,0:T(8,128)(2,1)} collective-permute-done((bf16[2,128,1024]{2,1,0:T(8,128)(2,1)S(1)}, bf16[2,128,1024]{2,1,0:T(8,128)(2,1)}, u32[]{:S(2)}, u32[]{:S(2)}) %collective-permute-start.7) | collective-permute-done | bytes 524320 | tf_op jit(solution)/shard_map/ppermute | solution.py:156
  33.1 3.0 %collective-permute-done.9.refs_3_ = bf16[2,128,1024]{2,1,0:T(8,128)(2,1)S(1)} collective-permute-done((bf16[2,128,1024]{2,1,0:T(8,128)(2,1)S(1)}, bf16[2,128,1024]{2,1,0:T(8,128)(2,1)S(1)}, u32[]{:S(2)}, u32[]{:S(2)}) %collective-permute-start.9) | collective-permute-done | bytes 524320 | tf_op jit(solution)/shard_map/ppermute | solution.py:160
  36.2 2.7 %collective-permute-done.8 = bf16[2,128,1024]{2,1,0:T(8,128)(2,1)} collective-permute-done((bf16[2,128,1024]{2,1,0:T(8,128)(2,1)S(1)}, bf16[2,128,1024]{2,1,0:T(8,128)(2,1)}, u32[]{:S(2)}, u32[]{:S(2)}) %collective-permute-start.8) | collective-permute-done | bytes 524320 | tf_op jit(solution)/shard_map/ppermute | solution.py:156
  40.0 2.1 %collective-permute-start.10 = (bf16[2,128,1024]{2,1,0:T(8,128)(2,1)}, bf16[2,128,1024]{2,1,0:T(8,128)(2,1)}, u32[]{:S(2)}, u32[]{:S(2)}) collective-permute-start(bf16[2,128,1024]{2,1,0:T(8,128)(2,1)} %collective-permute-done.8), channel_id=1, source_target_pairs={{4,0},{6,2},{8,12},{10,14},{5,1},{7,3},{9,13},{11,15},{20,16},{22,... | collective-permute-start | bytes 1572872 | tf_op jit(solution)/shard_map/ppermute | solution.py:156
  43.1 4.7 %collective-permute-done.6 = bf16[8,16,128]{2,1,0:T(8,128)(2,1)S(1)} collective-permute-done((bf16[8,16,128]{2,1,0:T(8,128)(2,1)S(1)}, bf16[8,16,128]{2,1,0:T(8,128)(2,1)S(1)}, u32[]{:S(2)}, u32[]{:S(2)}) %collective-permute-start.6) | collective-permute-done | bytes 32800 | tf_op jit(solution)/shard_map/ppermute | solution.py:175
  48.5 2.3 %first_slots.1 = (bf16[16,48,1024]{2,1,0:T(8,128)(2,1)S(1)}, bf16[16,48,1024]{2,1,0:T(8,128)(2,1)S(1)}, f32[16,96,128]{2,1,0:T(8,128)S(1)}) custom-call(s32[16,1024]{1,0:T(8,128)S(1)} %get-tuple-element.89.slot_ref, f32[16,1024]{1,0:T(8,128)S(1)} %get-tuple-element.90.gates_ref, bf16[2,128,1024]{2,1,0:T(8,128)(2,1)S(1)} %pad_maximum_fusion.refs_0_, ...), custom_call_target="tpu_custom_call" | custom-call | flops 1610612736 | bytes 6291456 | tf_op jit(solution)/shard_map/first_slots/pallas_call | solution.py:616
  55.1 4.7 %load.1.refs_5_ = bf16[16,1024,384]{2,1,0:T(8,128)(2,1)S(1)} custom-call(bf16[16,1024,384]{2,1,0:T(8,128)(2,1)} %refs_6_.5), custom_call_target="tpu_custom_call" | custom-call | bytes 12582912 | tf_op jit(solution)/shard_map/load/pallas_call | solution.py:592
  59.8 7.6 %pre.1 = (bf16[16,96,1024]{2,1,0:T(8,128)(2,1)S(1)}, f32[8,96,384]{2,1,0:T(8,128)}, f32[8,96,384]{2,1,0:T(8,128)}, f32[8,96,384]{2,1,0:T(8,128)}, f32[8,96,384]{2,1,0:T(8,128)}) custom-call(s32[16,1024]{1,0:T(8,128)S(1)} %get-tuple-element.89.slot_ref, bf16[2,128,1024]{2,1,0:T(8,128)(2,1)S(1)} %broadcast_select_fusion.refs_0_, ...), custom_call_target="tpu_custom_call" | custom-call | flops 3221225472 | bytes 35232152 | tf_op jit(solution)/shard_map/pre/pallas_call | solution.py:635
  67.4 4.9 %down.2.refs_4_ = f32[8,96,384]{2,1,0:T(8,128)} custom-call(s32[16,1024]{1,0:T(8,128)S(1)} %get-tuple-element.89.slot_ref, bf16[2,128,1024]{2,1,0:T(8,128)(2,1)S(1)} %broadcast_select_fusion.refs_0_, bf16[2,128,1024]{2,1,0:T(8,128)(2,1)S(1)} %collective-permute-done.11.refs_1_, bf16[128,1024]{1,0:T(8,128)(2,1)S(1)} %select_bitcast_fusion.refs_2_, ...), custom_call_target="tpu_custom_call" | custom-call | flops 1006632960 | bytes 8808038 | tf_op jit(solution)/shard_map/down/pallas_call | solution.py:656
  73.0 4.9 %down.3.refs_4_ = f32[8,96,384]{2,1,0:T(8,128)} custom-call(s32[16,1024]{1,0:T(8,128)S(1)} %get-tuple-element.89.slot_ref, bf16[2,128,1024]{2,1,0:T(8,128)(2,1)S(1)} %broadcast_select_fusion.refs_0_, bf16[2,128,1024]{2,1,0:T(8,128)(2,1)S(1)} %collective-permute-done.11.refs_1_, bf16[128,1024]{1,0:T(8,128)(2,1)S(1)} %select_bitcast_fusion.refs_2_, ...), custom_call_target="tpu_custom_call" | custom-call | flops 1006632960 | bytes 8808038 | tf_op jit(solution)/shard_map/down/pallas_call | solution.py:656
  78.9 8.3 %rows.2 = (bf16[8,96,768]{2,1,0:T(8,128)(2,1)S(1)}, bf16[384,1024]{1,0:T(8,128)(2,1)S(1)}, f32[512,1024]{1,0:T(8,128)S(1)}) custom-call(s32[16,1024]{1,0:T(8,128)S(1)} %get-tuple-element.89.slot_ref, f32[16,96,128]{2,1,0:T(8,128)S(1)} %get-tuple-element.95.slot_gates_ref, f32[8,96,384]{2,1,0:T(8,128)S(1)} %copy-done.4, ...), custom_call_target="tpu_custom_call" | custom-call | flops 2013265920 | bytes 19503512 | tf_op jit(solution)/shard_map/rows/pallas_call | solution.py:700
  87.3 8.4 %rows.3 = (bf16[8,96,768]{2,1,0:T(8,128)(2,1)S(1)}, bf16[384,1024]{1,0:T(8,128)(2,1)S(1)}, bf16[128,1024]{1,0:T(8,128)(2,1)S(1)}, bf16[128,1024]{1,0:T(8,128)(2,...) custom-call(s32[16,1024]{1,0:T(8,128)S(1)} %get-tuple-element.89.slot_ref, ...), custom_call_target="tpu_custom_call" | custom-call | flops 2013265920 | bytes 19503512 | tf_op jit(solution)/shard_map/rows/pallas_call | solution.py:700
  99.1 5.3 %weight_grads.5 = (bf16[16,1024,384]{2,1,0:T(8,128)(2,1)}, bf16[16,1024,384]{2,1,0:T(8,128)(2,1)}) custom-call(bf16[16,96,1024]{2,1,0:T(8,128)(2,1)S(1)} %get-tuple-element.162.x_ref, bf16[8,96,768]{2,1,0:T(8,128)(2,1)S(1)} %get-tuple-element.144.grads_ref), custom_call_target="tpu_custom_call" | custom-call | flops 754974720 | bytes 9830400 | tf_op jit(solution)/shard_map/weight_grads/pallas_call | solution.py:764
  107.5 3.5 %weight_grads.6 = (bf16[16,1024,384]{2,1,0:T(8,128)(2,1)}, bf16[16,1024,384]{2,1,0:T(8,128)(2,1)}) custom-call(bf16[16,96,1024]{2,1,0:T(8,128)(2,1)S(1)} %get-tuple-element.162.x_ref, bf16[8,96,768]{2,1,0:T(8,128)(2,1)S(1)} %get-tuple-element.144.grads_ref, ...), custom_call_target="tpu_custom_call", output_to_operand_aliasing={{0}: (2, {}), {1}: (3, {})} | custom-call | flops 452984832 | bytes 5898240 | tf_op jit(solution)/shard_map/weight_grads/pallas_call | solution.py:764
  110.9 2.4 %weight_grads.7 = (bf16[16,1024,384]{2,1,0:T(8,128)(2,1)}, bf16[16,1024,384]{2,1,0:T(8,128)(2,1)}) custom-call(bf16[16,96,1024]{2,1,0:T(8,128)(2,1)S(1)} %get-tuple-element.162.x_ref, bf16[8,96,768]{2,1,0:T(8,128)(2,1)S(1)} %get-tuple-element.163.grads_ref, ...), custom_call_target="tpu_custom_call", output_to_operand_aliasing={{0}: (2, {}), {1}: (3, {})} | custom-call | flops 301989888 | bytes 3932160 | tf_op jit(solution)/shard_map/weight_grads/pallas_call | solution.py:764
  115.6 3.2 %collective-permute-start.23 = (bf16[128,1024]{1,0:T(8,128)(2,1)S(1)}, bf16[128,1024]{1,0:T(8,128)(2,1)S(1)}, u32[]{:S(2)}, u32[]{:S(2)}) collective-permute-start(bf16[128,1024]{1,0:T(8,128)(2,1)S(1)} %add_convert_fusion.3), channel_id=1, source_target_pairs={{4,8},{6,10},{8,4},{10,6},{5,9},{7,11},{9,5},{11,7},{20,24},{22,26... | collective-permute-start | bytes 786440 | tf_op jit(solution)/shard_map/ppermute | solution.py:156
  120.3 3.5 %weight_grads.8 = (bf16[16,1024,384]{2,1,0:T(8,128)(2,1)}, bf16[16,1024,384]{2,1,0:T(8,128)(2,1)}) custom-call(bf16[16,96,1024]{2,1,0:T(8,128)(2,1)S(1)} %get-tuple-element.162.x_ref, bf16[8,96,768]{2,1,0:T(8,128)(2,1)S(1)} %get-tuple-element.163.grads_ref, ...), custom_call_target="tpu_custom_call", output_to_operand_aliasing={{0}: (2, {}), {1}: (3, {})} | custom-call | flops 452984832 | bytes 5898240 | tf_op jit(solution)/shard_map/weight_grads/pallas_call | solution.py:764
  124.2 3.3 %collective-permute-start.26 = (bf16[128,1024]{1,0:T(8,128)(2,1)S(1)}, bf16[128,1024]{1,0:T(8,128)(2,1)S(1)}, u32[]{:S(2)}, u32[]{:S(2)}) collective-permute-start(bf16[128,1024]{1,0:T(8,128)(2,1)S(1)} %add_convert_fusion.2), channel_id=1, source_target_pairs={{4,8},{6,10},{8,4},{10,6},{5,9},{7,11},{9,5},{11,7},{20,24},{22,26... | collective-permute-start | bytes 786440 | tf_op jit(solution)/shard_map/ppermute | solution.py:156
  127.5 3.5 %weight_grads.9 = (bf16[16,1024,384]{2,1,0:T(8,128)(2,1)}, bf16[16,1024,384]{2,1,0:T(8,128)(2,1)}) custom-call(bf16[16,96,1024]{2,1,0:T(8,128)(2,1)S(1)} %get-tuple-element.162.x_ref, bf16[8,96,768]{2,1,0:T(8,128)(2,1)S(1)} %get-tuple-element.163.grads_ref, ...), custom_call_target="tpu_custom_call", output_to_operand_aliasing={{0}: (2, {}), {1}: (3, {})} | custom-call | flops 452984832 | bytes 5898240 | tf_op jit(solution)/shard_map/weight_grads/pallas_call | solution.py:764
  (83 shorter events, 30.3 us)
Async XLA Ops:
  1.7 18.9 %collective-permute-start.2 = (bf16[2,128,1024]{2,1,0:T(8,128)(2,1)S(1)}, bf16[2,128,1024]{2,1,0:T(8,128)(2,1)S(1)}, u32[]{:S(2)}, u32[]{:S(2)}) collective-permute-start(bf16[2,128,1024]{2,1,0:T(8,128)(2,1)S(1)} %pad_maximum_fusion.refs_0_), channel_id=1, source_target_pairs={{0,2},{2,0},{4,6},{6,4},{8,10},{10,8},{12,14},{14,12},{1,3},{3,1},... | collective-permute-start | bytes 1572872 | tf_op jit(solution)/shard_map/ppermute | solution.py:160
  3.3 17.4 %collective-permute-start.1 = (bf16[2,128,1024]{2,1,0:T(8,128)(2,1)S(1)}, bf16[2,128,1024]{2,1,0:T(8,128)(2,1)S(1)}, u32[]{:S(2)}, u32[]{:S(2)}) collective-permute-start(bf16[2,128,1024]{2,1,0:T(8,128)(2,1)S(1)} %pad_maximum_fusion.refs_0_), channel_id=1, source_target_pairs={{4,8},{6,10},{8,4},{10,6},{5,9},{7,11},{9,5},{11,7},{20,24},{22,26... | collective-permute-start | bytes 1572872 | tf_op jit(solution)/shard_map/ppermute | solution.py:156
  6.7 13.9 %collective-permute-start = (bf16[2,128,1024]{2,1,0:T(8,128)(2,1)S(1)}, bf16[2,128,1024]{2,1,0:T(8,128)(2,1)S(1)}, u32[]{:S(2)}, u32[]{:S(2)}) collective-permute-start(bf16[2,128,1024]{2,1,0:T(8,128)(2,1)S(1)} %pad_maximum_fusion.refs_0_), channel_id=1, source_target_pairs={{0,4},{2,6},{4,0},{6,2},{8,12},{10,14},{12,8},{14,10},{1,5},{3,7},... | collective-permute-start | bytes 1572872 | tf_op jit(solution)/shard_map/ppermute | solution.py:156
  20.7 12.5 %collective-permute-start.7 = (bf16[2,128,1024]{2,1,0:T(8,128)(2,1)S(1)}, bf16[2,128,1024]{2,1,0:T(8,128)(2,1)}, u32[]{:S(2)}, u32[]{:S(2)}) collective-permute-start(bf16[2,128,1024]{2,1,0:T(8,128)(2,1)S(1)} %collective-permute-done.1), channel_id=1, source_target_pairs={{4,0},{6,2},{8,12},{10,14},{5,1},{7,3},{9,13},{11,15},{20,16},{22,... | collective-permute-start | bytes 1572872 | tf_op jit(solution)/shard_map/ppermute | solution.py:156
  23.7 12.5 %collective-permute-start.9 = (bf16[2,128,1024]{2,1,0:T(8,128)(2,1)S(1)}, bf16[2,128,1024]{2,1,0:T(8,128)(2,1)S(1)}, u32[]{:S(2)}, u32[]{:S(2)}) collective-permute-start(bf16[2,128,1024]{2,1,0:T(8,128)(2,1)S(1)} %collective-permute-done.refs_2_), channel_id=1, source_target_pairs={{0,2},{2,0},{4,6},{6,4},{8,10},{10,8},{12,14},{14,12},{1,3},{3,1},... | collective-permute-start | bytes 1572872 | tf_op jit(solution)/shard_map/ppermute | solution.py:160
  24.9 14.0 %collective-permute-start.8 = (bf16[2,128,1024]{2,1,0:T(8,128)(2,1)S(1)}, bf16[2,128,1024]{2,1,0:T(8,128)(2,1)}, u32[]{:S(2)}, u32[]{:S(2)}) collective-permute-start(bf16[2,128,1024]{2,1,0:T(8,128)(2,1)S(1)} %collective-permute-done.refs_2_), channel_id=1, source_target_pairs={{4,8},{6,10},{8,4},{10,6},{5,9},{7,11},{9,5},{11,7},{20,24},{22,26... | collective-permute-start | bytes 1572872 | tf_op jit(solution)/shard_map/ppermute | solution.py:156
  39.0 11.8 %collective-permute-start.11 = (bf16[2,128,1024]{2,1,0:T(8,128)(2,1)S(1)}, bf16[2,128,1024]{2,1,0:T(8,128)(2,1)S(1)}, u32[]{:S(2)}, u32[]{:S(2)}) collective-permute-start(bf16[2,128,1024]{2,1,0:T(8,128)(2,1)S(1)} %broadcast_select_fusion.refs_0_), channel_id=1, source_target_pairs={{0,2},{2,0},{4,6},{6,4},{8,10},{10,8},{12,14},{14,12},{1,3},{3,1},... | collective-permute-start | bytes 1572872 | tf_op jit(solution)/shard_map/ppermute | solution.py:160
  40.0 10.8 %collective-permute-start.10 = (bf16[2,128,1024]{2,1,0:T(8,128)(2,1)}, bf16[2,128,1024]{2,1,0:T(8,128)(2,1)}, u32[]{:S(2)}, u32[]{:S(2)}) collective-permute-start(bf16[2,128,1024]{2,1,0:T(8,128)(2,1)} %collective-permute-done.8), channel_id=1, source_target_pairs={{4,0},{6,2},{8,12},{10,14},{5,1},{7,3},{9,13},{11,15},{20,16},{22,... | collective-permute-start | bytes 1572872 | tf_op jit(solution)/shard_map/ppermute | solution.py:156
  51.9 7.9 %collective-permute-start.12 = (bf16[128,1024]{1,0:T(8,128)(2,1)S(1)}, bf16[128,1024]{1,0:T(8,128)(2,1)S(1)}, u32[]{:S(2)}, u32[]{:S(2)}) collective-permute-start(bf16[128,1024]{1,0:T(8,128)(2,1)S(1)} %select_bitcast_fusion.1.refs_2_), channel_id=1, source_target_pairs={{0,2},{2,0},{4,6},{6,4},{8,10},{10,8},{12,14},{14,12},{1,3},{3,1},... | collective-permute-start | bytes 786440 | tf_op jit(solution)/shard_map/ppermute | solution.py:160
  54.1 13.3 %collective-permute-start.13 = (bf16[128,1024]{1,0:T(8,128)(2,1)S(1)}, bf16[128,1024]{1,0:T(8,128)(2,1)S(1)}, u32[]{:S(2)}, u32[]{:S(2)}) collective-permute-start(bf16[128,1024]{1,0:T(8,128)(2,1)S(1)} %select_bitcast_fusion.refs_2_), channel_id=1, source_target_pairs={{0,2},{2,0},{4,6},{6,4},{8,10},{10,8},{12,14},{14,12},{1,3},{3,1},... | collective-permute-start | bytes 786440 | tf_op jit(solution)/shard_map/ppermute | solution.py:160
  72.3 6.2 %collective-permute-start.14 = (f32[8,96,384]{2,1,0:T(8,128)}, f32[8,96,384]{2,1,0:T(8,128)S(1)}, u32[]{:S(2)}, u32[]{:S(2)}) collective-permute-start(f32[8,96,384]{2,1,0:T(8,128)} %down.2.refs_4_), channel_id=1, source_target_pairs={{0,1},{1,0},{2,3},{3,2},{4,5},{5,4},{6,7},{7,6},{8,9},{9,8},{10,11... | collective-permute-start | bytes 3538952 | tf_op jit(solution)/shard_map/ppermute | solution.py:164
  72.4 6.5 %collective-permute-start.15 = (f32[8,96,384]{2,1,0:T(8,128)S(1)}, f32[8,96,384]{2,1,0:T(8,128)S(1)}, u32[]{:S(2)}, u32[]{:S(2)}) collective-permute-start(f32[8,96,384]{2,1,0:T(8,128)S(1)} %copy-done.4), channel_id=1, source_target_pairs={{0,1},{1,0},{2,3},{3,2},{4,5},{5,4},{6,7},{7,6},{8,9},{9,8},{10,11... | collective-permute-start | bytes 3538952 | tf_op jit(solution)/shard_map/ppermute | solution.py:164
  77.9 9.4 %collective-permute-start.19 = (f32[8,96,384]{2,1,0:T(8,128)}, f32[8,96,384]{2,1,0:T(8,128)S(1)}, u32[]{:S(2)}, u32[]{:S(2)}) collective-permute-start(f32[8,96,384]{2,1,0:T(8,128)} %down.3.refs_4_), channel_id=1, source_target_pairs={{0,1},{1,0},{2,3},{3,2},{4,5},{5,4},{6,7},{7,6},{8,9},{9,8},{10,11... | collective-permute-start | bytes 3538952 | tf_op jit(solution)/shard_map/ppermute | solution.py:164
  78.4 8.9 %collective-permute-start.17 = (f32[8,96,384]{2,1,0:T(8,128)S(1)}, f32[8,96,384]{2,1,0:T(8,128)S(1)}, u32[]{:S(2)}, u32[]{:S(2)}) collective-permute-start(f32[8,96,384]{2,1,0:T(8,128)S(1)} %copy-done.2), channel_id=1, source_target_pairs={{0,1},{1,0},{2,3},{3,2},{4,5},{5,4},{6,7},{7,6},{8,9},{9,8},{10,11... | collective-permute-start | bytes 3538952 | tf_op jit(solution)/shard_map/ppermute | solution.py:164
  78.5 8.8 %collective-permute-start.18 = (f32[8,96,384]{2,1,0:T(8,128)S(1)}, f32[8,96,384]{2,1,0:T(8,128)S(1)}, u32[]{:S(2)}, u32[]{:S(2)}) collective-permute-start(f32[8,96,384]{2,1,0:T(8,128)S(1)} %copy-done.3), channel_id=1, source_target_pairs={{0,1},{1,0},{2,3},{3,2},{4,5},{5,4},{6,7},{7,6},{8,9},{9,8},{10,11... | collective-permute-start | bytes 3538952 | tf_op jit(solution)/shard_map/ppermute | solution.py:164
  95.8 9.2 %collective-permute-start.20 = (bf16[128,1024]{1,0:T(8,128)(2,1)S(1)}, bf16[128,1024]{1,0:T(8,128)(2,1)S(1)}, u32[]{:S(2)}, u32[]{:S(2)}) collective-permute-start(bf16[128,1024]{1,0:T(8,128)(2,1)S(1)} %get-tuple-element.127), channel_id=1, source_target_pairs={{0,2},{2,0},{4,6},{6,4},{8,10},{10,8},{12,14},{14,12},{1,3},{3,1},... | collective-permute-start | bytes 786440 | tf_op jit(solution)/shard_map/ppermute | solution.py:160
  96.9 16.5 %collective-permute-start.22 = (bf16[128,1024]{1,0:T(8,128)(2,1)S(1)}, bf16[128,1024]{1,0:T(8,128)(2,1)S(1)}, u32[]{:S(2)}, u32[]{:S(2)}) collective-permute-start(bf16[128,1024]{1,0:T(8,128)(2,1)S(1)} %get-tuple-element.125), channel_id=1, source_target_pairs={{0,2},{2,0},{4,6},{6,4},{8,10},{10,8},{12,14},{14,12},{1,3},{3,1},... | collective-permute-start | bytes 786440 | tf_op jit(solution)/shard_map/ppermute | solution.py:160
  105.0 9.0 %collective-permute-start.21 = (bf16[128,1024]{1,0:T(8,128)(2,1)S(1)}, bf16[128,1024]{1,0:T(8,128)(2,1)S(1)}, u32[]{:S(2)}, u32[]{:S(2)}) collective-permute-start(bf16[128,1024]{1,0:T(8,128)(2,1)S(1)} %fusion), channel_id=1, source_target_pairs={{0,4},{2,6},{12,8},{14,10},{1,5},{3,7},{13,9},{15,11},{16,20},{18,... | collective-permute-start | bytes 786440 | tf_op jit(solution)/shard_map/ppermute | solution.py:156
  106.3 17.5 %collective-permute-start.25 = (bf16[128,1024]{1,0:T(8,128)(2,1)S(1)}, bf16[128,1024]{1,0:T(8,128)(2,1)S(1)}, u32[]{:S(2)}, u32[]{:S(2)}) collective-permute-start(bf16[128,1024]{1,0:T(8,128)(2,1)S(1)} %get-tuple-element.134), channel_id=1, source_target_pairs={{0,2},{2,0},{4,6},{6,4},{8,10},{10,8},{12,14},{14,12},{1,3},{3,1},... | collective-permute-start | bytes 786440 | tf_op jit(solution)/shard_map/ppermute | solution.py:160
  114.3 9.5 %collective-permute-start.24 = (bf16[128,1024]{1,0:T(8,128)(2,1)S(1)}, bf16[128,1024]{1,0:T(8,128)(2,1)S(1)}, u32[]{:S(2)}, u32[]{:S(2)}) collective-permute-start(bf16[128,1024]{1,0:T(8,128)(2,1)S(1)} %fusion.1), channel_id=1, source_target_pairs={{0,4},{2,6},{12,8},{14,10},{1,5},{3,7},{13,9},{15,11},{16,20},{18,... | collective-permute-start | bytes 786440 | tf_op jit(solution)/shard_map/ppermute | solution.py:156
  115.6 8.3 %collective-permute-start.23 = (bf16[128,1024]{1,0:T(8,128)(2,1)S(1)}, bf16[128,1024]{1,0:T(8,128)(2,1)S(1)}, u32[]{:S(2)}, u32[]{:S(2)}) collective-permute-start(bf16[128,1024]{1,0:T(8,128)(2,1)S(1)} %add_convert_fusion.3), channel_id=1, source_target_pairs={{4,8},{6,10},{8,4},{10,6},{5,9},{7,11},{9,5},{11,7},{20,24},{22,26... | collective-permute-start | bytes 786440 | tf_op jit(solution)/shard_map/ppermute | solution.py:156
  118.8 12.3 %collective-permute-start.28 = (bf16[128,1024]{1,0:T(8,128)(2,1)S(1)}, bf16[128,1024]{1,0:T(8,128)(2,1)S(1)}, u32[]{:S(2)}, u32[]{:S(2)}) collective-permute-start(bf16[128,1024]{1,0:T(8,128)(2,1)S(1)} %get-tuple-element.132), channel_id=1, source_target_pairs={{0,2},{2,0},{4,6},{6,4},{8,10},{10,8},{12,14},{14,12},{1,3},{3,1},... | collective-permute-start | bytes 786440 | tf_op jit(solution)/shard_map/ppermute | solution.py:160
  124.1 6.9 %collective-permute-start.27 = (bf16[128,1024]{1,0:T(8,128)(2,1)S(1)}, bf16[128,1024]{1,0:T(8,128)(2,1)S(1)}, u32[]{:S(2)}, u32[]{:S(2)}) collective-permute-start(bf16[128,1024]{1,0:T(8,128)(2,1)S(1)} %add_convert_fusion.1), channel_id=1, source_target_pairs={{0,4},{2,6},{4,0},{6,2},{8,12},{10,14},{12,8},{14,10},{1,5},{3,7},... | collective-permute-start | bytes 786440 | tf_op jit(solution)/shard_map/ppermute | solution.py:156
  124.2 8.3 %collective-permute-start.26 = (bf16[128,1024]{1,0:T(8,128)(2,1)S(1)}, bf16[128,1024]{1,0:T(8,128)(2,1)S(1)}, u32[]{:S(2)}, u32[]{:S(2)}) collective-permute-start(bf16[128,1024]{1,0:T(8,128)(2,1)S(1)} %add_convert_fusion.2), channel_id=1, source_target_pairs={{4,8},{6,10},{8,4},{10,6},{5,9},{7,11},{9,5},{11,7},{20,24},{22,26... | collective-permute-start | bytes 786440 | tf_op jit(solution)/shard_map/ppermute | solution.py:156
  (11 other events, 58.0 us)
